TPU v7x, 1024 devices: a whole 8x8x8 slice. The times are simulated.
1024 devices in a mesh: rows: 64 (over y, x), cols: 16 (over z, core).
Axes of the slice: x: 8, y: 8, z: 8, core: 2. Of those that a mesh axis runs over, the one named last changes fastest.
Arguments:
- head_start: float32 [8, 2048, 2048], P(None, 'rows', 'cols'), may hold values from -6 to 6
- class_map: int32 [8, 2048, 2048], P(None, 'rows', 'cols'), may hold values from 0 to 7
- class_cond: float32 [8], replicated, may hold values from 1 to 10
- partials: float32 [64, 16, 16, 32, 128], P('rows', 'cols'), may hold values from -6 to 6
- send_count: int32 [64, 16, 16], P('rows', 'cols'), may hold values from 1 to 32, as said below
- recv_block: int32 [64, 16, 16, 32], P('rows', 'cols'), may hold values from 0 to 255
Outputs:
- head: float32 [8, 2048, 2048], P(None, 'rows', 'cols')
- residual: float32 [8, 2048, 2048], P(None, 'rows', 'cols')
Inputs may be any that keep to these rules, and one draw needn't show every extreme that they name: `send_count`: live slots of one sender to one receiver; in each row group some sender fills all 32 slots to one receiver and sends a single one to another. `recv_block`: blocks are numbered z * 32 + local y.
All inputs are finite; a program needn't handle non-finite values.
Results may differ from a plain program's by a relative error of at most 0.00013.
Values sent between devices are 32-bit elements; how exact they have to be, the bound alone decides.
No kernel may reach another device: no remote copies, remote signals or barrier semaphores. Data moves between devices by JAX's collectives and lax.ppermute only.
A program may use at most 32 MiB of HBM per device.

v0:
```python
import jax
import jax.numpy as jnp
from jax import lax
from jax.sharding import PartitionSpec as P

NU1 = 2
NU2 = 2
NUC = 4


OMEGA = 0.8


def extended(cells, sides, width):
    for axis, dim in sides:
        count = lax.axis_size(axis)
        ends = count - 1
        head = lax.slice_in_dim(cells, 0, width, axis=dim)
        tail = lax.slice_in_dim(cells, cells.shape[dim] - width, cells.shape[dim], axis=dim)
        cells = jnp.concatenate(
            [
                lax.ppermute(tail, axis, [(i, (i + 1) % count) for i in range(ends)]),
                cells,
                lax.ppermute(head, axis, [((i + 1) % count, i) for i in range(ends)]),
            ],
            axis=dim,
        )
    return cells


def diagonal_of(cond_pad, zweight):
    center = cond_pad[:, 1:-1, 1:-1]
    total = jnp.zeros_like(center)
    for ylo, xlo in ((0, 1), (2, 1), (1, 0), (1, 2)):
        neighbour = cond_pad[:, ylo : ylo + center.shape[1], xlo : xlo + center.shape[2]]
        total = total + 0.5 * (center + neighbour)
    vertical = zweight * 0.5 * (center[1:] + center[:-1])
    total = (
        total
        + jnp.pad(vertical, ((0, 1), (0, 0), (0, 0)))
        + jnp.pad(vertical, ((1, 0), (0, 0), (0, 0)))
    )
    return total


def apply_op(field_pad, cond_pad, zweight):
    center = cond_pad[:, 1:-1, 1:-1]
    value = field_pad[:, 1:-1, 1:-1]
    total = jnp.zeros_like(value)
    for ylo, xlo in ((0, 1), (2, 1), (1, 0), (1, 2)):
        neighbour = cond_pad[:, ylo : ylo + center.shape[1], xlo : xlo + center.shape[2]]
        other = field_pad[:, ylo : ylo + center.shape[1], xlo : xlo + center.shape[2]]
        total = total + 0.5 * (center + neighbour) * (value - other)
    vertical = zweight * 0.5 * (center[1:] + center[:-1]) * (value[1:] - value[:-1])
    total = (
        total
        + jnp.pad(vertical, ((0, 1), (0, 0), (0, 0)))
        - jnp.pad(vertical, ((1, 0), (0, 0), (0, 0)))
    )
    return total


def restrict_sum(field):
    depth, height, width = field.shape
    return jnp.sum(field.reshape(depth, height // 2, 2, width // 2, 2), axis=(2, 4))


def fine_pad(field):
    return extended(field, (("rows", 1), ("cols", 2)), 1)


def split_pad(field):
    return extended(field, (("rows", 1), ("cols", 2)), 1)


def coarse_solve(source, cond_pad, padder):
    coarse_diag = diagonal_of(cond_pad, 4.0)
    correction = OMEGA * source / coarse_diag
    for sweep in range(NUC - 1):
        correction = (
            correction
            + OMEGA * (source - apply_op(padder(correction), cond_pad, 4.0)) / coarse_diag
        )
    return correction


def body(head_start, class_map, class_cond, partials, send_count, recv_block):
    depth, height, width = head_start.shape
    cond = jnp.zeros(head_start.shape, jnp.float32)
    for category in range(class_cond.shape[0]):
        cond = cond + jnp.where(class_map == category, class_cond[category], 0.0)
    slots = partials.shape[3]
    live = lax.broadcasted_iota(jnp.int32, send_count.shape + (slots,), 3) < send_count[..., None]
    outgoing = partials * live[..., None].astype(jnp.float32)
    incoming = lax.all_to_all(outgoing, "cols", split_axis=2, concat_axis=1, tiled=True)
    values = incoming.reshape(-1, width)
    block_ids = recv_block.reshape(-1)
    onehot = (block_ids[:, None] == lax.broadcasted_iota(jnp.int32, (1, depth * height), 1)).astype(
        jnp.float32
    )
    recharge = jnp.einsum(
        "sb,sc->bc",
        onehot,
        values,
        precision=lax.Precision.HIGHEST,
        preferred_element_type=jnp.float32,
    ).reshape(depth, height, width)
    cond_pad = fine_pad(cond)
    fine_diag = diagonal_of(cond_pad, 1.0)
    head = head_start
    for sweep in range(NU1):
        head = head + OMEGA * (recharge - apply_op(fine_pad(head), cond_pad, 1.0)) / fine_diag
    fine_res = recharge - apply_op(fine_pad(head), cond_pad, 1.0)
    coarse_src = restrict_sum(fine_res)
    coarse_cond = 0.25 * restrict_sum(cond)
    correction = coarse_solve(coarse_src, split_pad(coarse_cond), split_pad)
    head = head + jnp.repeat(jnp.repeat(correction, 2, axis=1), 2, axis=2)
    for sweep in range(NU2):
        head = head + OMEGA * (recharge - apply_op(fine_pad(head), cond_pad, 1.0)) / fine_diag
    residual = recharge - apply_op(fine_pad(head), cond_pad, 1.0)
    return (head, residual)


def solution(mesh):
    placed = (
        P(None, "rows", "cols"),
        P(None, "rows", "cols"),
        P(),
        P("rows", "cols", None, None, None),
        P("rows", "cols", None),
        P("rows", "cols", None, None),
    )
    return jax.shard_map(
        body,
        mesh=mesh,
        in_specs=placed,
        out_specs=(P(None, "rows", "cols"), P(None, "rows", "cols")),
        check_vma=False,
    )
```

profile of v0, /device:TPU:447, one launch (start us, length us, event | category | flops | bytes accessed | tf_op | source)
XLA Modules:
  0.0 242.8 jit_solution(6651072239193917360)
XLA Ops:
  1.4 4.3 %collective-permute-start.1 = (f32[8,1,128]{2,1,0:T(1,128)S(1)}, f32[8,1,128]{2,1,0:T(1,128)S(1)}, u32[]{:S(2)}, u32[]{:S(2)}) collective-permute-start(f32[8,1,128]{2,1,0:T(1,128)S(1)} %get-tuple-element.33), channel_id=1, source_target_pairs={{0,16},{16,32},{32,48},{48,64},{64,80},{80,96},{96,112},{112,128},... | collective-permute-start | bytes 12296 | tf_op jit(solution)/shard_map/ppermute | solution.py:22
  5.7 1.9 collective-permute-start.3
  9.3 6.1 %select_add_fusion = f32[8,32,128]{2,1,0:T(8,128)S(1)} fusion(s32[8,32,128]{2,1,0:T(8,128)} %param.7, f32[]{:T(128)} %bitcast.11, f32[]{:T(128)} %bitcast.10, f32[]{:T(128)} %bitcast.9, f32[]{:T(128)} %bitcast.8, f32[]{:T(128)} %bitcast.7, f32[]{:T(128)} %bitcast.6, f32[]{:T(128)} %bitcast.5, f32[]{:T(128)} %bitcast.4), kind=kLoop, calls=%fused_computation.173 | loop fusion | flops 753664 | bytes 262176 | tf_op jit(solution)/shard_map/add | solution.py:91
  15.4 2.1 collective-permute-start.2
  17.5 6.5 %collective-permute-start = (f32[8,1,128]{2,1,0:T(1,128)S(1)}, f32[8,1,128]{2,1,0:T(1,128)S(1)}, u32[]{:S(2)}, u32[]{:S(2)}) collective-permute-start(f32[8,1,128]{2,1,0:T(1,128)S(1)} %get-tuple-element.32), channel_id=1, source_target_pairs={{0,16},{16,32},{32,48},{48,64},{64,80},{80,96},{96,112},{112,128},... | collective-permute-start | bytes 12296 | tf_op jit(solution)/shard_map/ppermute | solution.py:22
  24.7 1.8 bitcast_multiply_fusion
  26.5 13.0 %all-to-all-start = ((f32[1,1,16,32,128]{4,3,1,0,2:T(8,128)}), f32[1,1,16,32,128]{4,3,1,0,2:T(8,128)S(1)}, u32[]{:S(2)}, u32[]{:S(2)}) async-start(f32[1,1,16,32,128]{4,3,1,0,2:T(8,128)} %bitcast_multiply_fusion), calls=%async_computation | async-start | bytes 524288 | tf_op jit(solution)/shard_map/all_to_all | solution.py:95
  42.1 1.9 collective-permute-start.17
  44.8 6.7 %collective-permute-start.16 = (f32[8,1,64]{2,1,0:T(1,128)S(1)}, f32[8,1,64]{2,1,0:T(1,128)S(1)}, u32[]{:S(2)}, u32[]{:S(2)}) collective-permute-start(f32[8,1,64]{2,1,0:T(1,128)S(1)} %get-tuple-element.58), channel_id=1, source_target_pairs={{0,16},{16,32},{32,48},{48,64},{64,80},{80,96},{96,112},{112,128},... | collective-permute-start | bytes 6152 | tf_op jit(solution)/shard_map/ppermute | solution.py:22
  51.8 2.8 %collective-permute-start.6 = (f32[8,34,1]{2,1,0:T(8,128)S(1)}, f32[8,34,1]{2,1,0:T(8,128)S(1)}, u32[]{:S(2)}, u32[]{:S(2)}) collective-permute-start(f32[8,34,1]{2,1,0:T(8,128)S(1)} %get-tuple-element.17), channel_id=1, source_target_pairs={{1,0},{2,1},{3,2},{4,3},{5,4},{6,5},{7,6},{8,7},{9,8},{10,9},{11,1... | collective-permute-start | bytes 3272 | tf_op jit(solution)/shard_map/ppermute | solution.py:24
  54.6 4.2 %collective-permute-start.4 = (f32[8,34,1]{2,1,0:T(8,128)S(1)}, f32[8,34,1]{2,1,0:T(8,128)S(1)}, u32[]{:S(2)}, u32[]{:S(2)}) collective-permute-start(f32[8,34,1]{2,1,0:T(8,128)S(1)} %get-tuple-element.18), channel_id=1, source_target_pairs={{0,1},{1,2},{2,3},{3,4},{4,5},{5,6},{6,7},{7,8},{8,9},{9,10},{10,1... | collective-permute-start | bytes 3272 | tf_op jit(solution)/shard_map/ppermute | solution.py:22
  58.8 2.4 collective-permute-start.5
  61.2 1.9 collective-permute-start.7
  63.5 5.6 %collective-permute-done.7 = f32[8,34,1]{2,1,0:T(8,128)S(1)} collective-permute-done((f32[8,34,1]{2,1,0:T(8,128)S(1)}, f32[8,34,1]{2,1,0:T(8,128)S(1)}, u32[]{:S(2)}, u32[]{:S(2)}) %collective-permute-start.7) | collective-permute-done | bytes 1120 | tf_op jit(solution)/shard_map/ppermute | solution.py:24
  69.6 1.9 collective-permute-start.8
  71.5 3.4 %collective-permute-start.9 = (f32[8,1,128]{2,1,0:T(1,128)S(1)}, f32[8,1,128]{2,1,0:T(1,128)S(1)}, u32[]{:S(2)}, u32[]{:S(2)}) collective-permute-start(f32[8,1,128]{2,1,0:T(1,128)S(1)} %get-tuple-element.30), channel_id=1, source_target_pairs={{16,0},{32,16},{48,32},{64,48},{80,64},{96,80},{112,96},{128,112},... | collective-permute-start | bytes 12296 | tf_op jit(solution)/shard_map/ppermute | solution.py:24
  75.0 1.9 collective-permute-start.19
  76.9 4.9 %collective-permute-start.18 = (f32[8,18,1]{2,0,1:T(8,128)S(1)}, f32[8,18,1]{2,0,1:T(8,128)S(1)}, u32[]{:S(2)}, u32[]{:S(2)}) collective-permute-start(f32[8,18,1]{2,0,1:T(8,128)S(1)} %get-tuple-element.50), channel_id=1, source_target_pairs={{0,1},{1,2},{2,3},{3,4},{4,5},{5,6},{6,7},{7,8},{8,9},{9,10},{10,1... | collective-permute-start | bytes 1736 | tf_op jit(solution)/shard_map/ppermute | solution.py:22
  81.9 1.9 collective-permute-start.10
  83.9 2.4 collective-permute-start.11
  86.3 5.4 %collective-permute-done.11 = f32[8,34,1]{2,1,0:T(8,128)S(1)} collective-permute-done((f32[8,34,1]{2,1,0:T(8,128)S(1)}, f32[8,34,1]{2,1,0:T(8,128)S(1)}, u32[]{:S(2)}, u32[]{:S(2)}) %collective-permute-start.11) | collective-permute-done | bytes 1120 | tf_op jit(solution)/shard_map/ppermute | solution.py:24
  92.0 5.2 %collective-permute-start.12 = (f32[8,1,128]{2,1,0:T(1,128)S(1)}, f32[8,1,128]{2,1,0:T(1,128)S(1)}, u32[]{:S(2)}, u32[]{:S(2)}) collective-permute-start(f32[8,1,128]{2,1,0:T(1,128)S(1)} %get-tuple-element.27), channel_id=1, source_target_pairs={{0,16},{16,32},{32,48},{48,64},{64,80},{80,96},{96,112},{112,128},... | collective-permute-start | bytes 12296 | tf_op jit(solution)/shard_map/ppermute | solution.py:22
  97.2 1.9 collective-permute-start.13
  99.9 5.0 %collective-permute-done.13 = f32[8,1,128]{2,1,0:T(1,128)S(1)} collective-permute-done((f32[8,1,128]{2,1,0:T(1,128)S(1)}, f32[8,1,128]{2,1,0:T(1,128)S(1)}, u32[]{:S(2)}, u32[]{:S(2)}) %collective-permute-start.13) | collective-permute-done | bytes 4128 | tf_op jit(solution)/shard_map/ppermute | solution.py:24
  105.0 3.2 %collective-permute-start.14 = (f32[8,34,1]{2,1,0:T(8,128)S(1)}, f32[8,34,1]{2,1,0:T(8,128)S(1)}, u32[]{:S(2)}, u32[]{:S(2)}) collective-permute-start(f32[8,34,1]{2,1,0:T(8,128)S(1)} %get-tuple-element.13), channel_id=1, source_target_pairs={{0,1},{1,2},{2,3},{3,4},{4,5},{5,6},{6,7},{7,8},{8,9},{9,10},{10,1... | collective-permute-start | bytes 3272 | tf_op jit(solution)/shard_map/ppermute | solution.py:22
  108.2 1.9 collective-permute-start.15
  110.5 5.6 %collective-permute-done.15 = f32[8,34,1]{2,1,0:T(8,128)S(1)} collective-permute-done((f32[8,34,1]{2,1,0:T(8,128)S(1)}, f32[8,34,1]{2,1,0:T(8,128)S(1)}, u32[]{:S(2)}, u32[]{:S(2)}) %collective-permute-start.15) | collective-permute-done | bytes 1120 | tf_op jit(solution)/shard_map/ppermute | solution.py:24
  116.9 1.7 reduce_sum.18
  119.8 1.9 collective-permute-start.20
  121.7 3.4 %collective-permute-start.21 = (f32[8,1,64]{2,1,0:T(1,128)S(1)}, f32[8,1,64]{2,1,0:T(1,128)S(1)}, u32[]{:S(2)}, u32[]{:S(2)}) collective-permute-start(f32[8,1,64]{2,1,0:T(1,128)S(1)} %get-tuple-element.56), channel_id=1, source_target_pairs={{16,0},{32,16},{48,32},{64,48},{80,64},{96,80},{112,96},{128,112},... | collective-permute-start | bytes 6152 | tf_op jit(solution)/shard_map/ppermute | solution.py:24
  125.2 4.3 %collective-permute-done.21 = f32[8,1,64]{2,1,0:T(1,128)S(1)} collective-permute-done((f32[8,1,64]{2,1,0:T(1,128)S(1)}, f32[8,1,64]{2,1,0:T(1,128)S(1)}, u32[]{:S(2)}, u32[]{:S(2)}) %collective-permute-start.21) | collective-permute-done | bytes 2080 | tf_op jit(solution)/shard_map/ppermute | solution.py:24
  129.5 2.9 %collective-permute-start.22 = (f32[8,18,1]{2,0,1:T(8,128)S(1)}, f32[8,18,1]{2,0,1:T(8,128)S(1)}, u32[]{:S(2)}, u32[]{:S(2)}) collective-permute-start(f32[8,18,1]{2,0,1:T(8,128)S(1)} %get-tuple-element.45), channel_id=1, source_target_pairs={{0,1},{1,2},{2,3},{3,4},{4,5},{5,6},{6,7},{7,8},{8,9},{9,10},{10,1... | collective-permute-start | bytes 1736 | tf_op jit(solution)/shard_map/ppermute | solution.py:22
  132.4 1.9 collective-permute-start.23
  134.4 4.9 %collective-permute-done.23 = f32[8,18,1]{2,0,1:T(8,128)S(1)} collective-permute-done((f32[8,18,1]{2,0,1:T(8,128)S(1)}, f32[8,18,1]{2,0,1:T(8,128)S(1)}, u32[]{:S(2)}, u32[]{:S(2)}) %collective-permute-start.23) | collective-permute-done | bytes 608 | tf_op jit(solution)/shard_map/ppermute | solution.py:24
  139.6 1.9 collective-permute-start.24
  141.5 3.4 %collective-permute-start.25 = (f32[8,1,64]{2,1,0:T(1,128)S(1)}, f32[8,1,64]{2,1,0:T(1,128)S(1)}, u32[]{:S(2)}, u32[]{:S(2)}) collective-permute-start(f32[8,1,64]{2,1,0:T(1,128)S(1)} %get-tuple-element.54), channel_id=1, source_target_pairs={{16,0},{32,16},{48,32},{64,48},{80,64},{96,80},{112,96},{128,112},... | collective-permute-start | bytes 6152 | tf_op jit(solution)/shard_map/ppermute | solution.py:24
  144.9 4.3 %collective-permute-done.25 = f32[8,1,64]{2,1,0:T(1,128)S(1)} collective-permute-done((f32[8,1,64]{2,1,0:T(1,128)S(1)}, f32[8,1,64]{2,1,0:T(1,128)S(1)}, u32[]{:S(2)}, u32[]{:S(2)}) %collective-permute-start.25) | collective-permute-done | bytes 2080 | tf_op jit(solution)/shard_map/ppermute | solution.py:24
  149.3 3.0 %collective-permute-start.26 = (f32[8,18,1]{2,0,1:T(8,128)S(1)}, f32[8,18,1]{2,0,1:T(8,128)S(1)}, u32[]{:S(2)}, u32[]{:S(2)}) collective-permute-start(f32[8,18,1]{2,0,1:T(8,128)S(1)} %get-tuple-element.41), channel_id=1, source_target_pairs={{0,1},{1,2},{2,3},{3,4},{4,5},{5,6},{6,7},{7,8},{8,9},{9,10},{10,1... | collective-permute-start | bytes 1736 | tf_op jit(solution)/shard_map/ppermute | solution.py:22
  152.3 1.9 collective-permute-start.27
  154.3 4.9 %collective-permute-done.27 = f32[8,18,1]{2,0,1:T(8,128)S(1)} collective-permute-done((f32[8,18,1]{2,0,1:T(8,128)S(1)}, f32[8,18,1]{2,0,1:T(8,128)S(1)}, u32[]{:S(2)}, u32[]{:S(2)}) %collective-permute-start.27) | collective-permute-done | bytes 608 | tf_op jit(solution)/shard_map/ppermute | solution.py:24
  159.5 1.9 collective-permute-start.28
  161.4 3.4 %collective-permute-start.29 = (f32[8,1,64]{2,1,0:T(1,128)S(1)}, f32[8,1,64]{2,1,0:T(1,128)S(1)}, u32[]{:S(2)}, u32[]{:S(2)}) collective-permute-start(f32[8,1,64]{2,1,0:T(1,128)S(1)} %get-tuple-element.52), channel_id=1, source_target_pairs={{16,0},{32,16},{48,32},{64,48},{80,64},{96,80},{112,96},{128,112},... | collective-permute-start | bytes 6152 | tf_op jit(solution)/shard_map/ppermute | solution.py:24
  164.8 4.3 %collective-permute-done.29 = f32[8,1,64]{2,1,0:T(1,128)S(1)} collective-permute-done((f32[8,1,64]{2,1,0:T(1,128)S(1)}, f32[8,1,64]{2,1,0:T(1,128)S(1)}, u32[]{:S(2)}, u32[]{:S(2)}) %collective-permute-start.29) | collective-permute-done | bytes 2080 | tf_op jit(solution)/shard_map/ppermute | solution.py:24
  169.2 3.0 %collective-permute-start.30 = (f32[8,18,1]{2,0,1:T(8,128)S(1)}, f32[8,18,1]{2,0,1:T(8,128)S(1)}, u32[]{:S(2)}, u32[]{:S(2)}) collective-permute-start(f32[8,18,1]{2,0,1:T(8,128)S(1)} %get-tuple-element.37), channel_id=1, source_target_pairs={{0,1},{1,2},{2,3},{3,4},{4,5},{5,6},{6,7},{7,8},{8,9},{9,10},{10,1... | collective-permute-start | bytes 1736 | tf_op jit(solution)/shard_map/ppermute | solution.py:22
  172.2 1.9 collective-permute-start.31
  174.1 4.9 %collective-permute-done.31 = f32[8,18,1]{2,0,1:T(8,128)S(1)} collective-permute-done((f32[8,18,1]{2,0,1:T(8,128)S(1)}, f32[8,18,1]{2,0,1:T(8,128)S(1)}, u32[]{:S(2)}, u32[]{:S(2)}) %collective-permute-start.31) | collective-permute-done | bytes 608 | tf_op jit(solution)/shard_map/ppermute | solution.py:24
  179.8 1.9 collective-permute-start.32
  181.8 3.4 %collective-permute-start.33 = (f32[8,1,128]{2,1,0:T(1,128)S(1)}, f32[8,1,128]{2,1,0:T(1,128)S(1)}, u32[]{:S(2)}, u32[]{:S(2)}) collective-permute-start(f32[8,1,128]{2,1,0:T(1,128)S(1)} %get-tuple-element.26), channel_id=1, source_target_pairs={{16,0},{32,16},{48,32},{64,48},{80,64},{96,80},{112,96},{128,112},... | collective-permute-start | bytes 12296 | tf_op jit(solution)/shard_map/ppermute | solution.py:24
  185.1 4.3 %collective-permute-done.33 = f32[8,1,128]{2,1,0:T(1,128)S(1)} collective-permute-done((f32[8,1,128]{2,1,0:T(1,128)S(1)}, f32[8,1,128]{2,1,0:T(1,128)S(1)}, u32[]{:S(2)}, u32[]{:S(2)}) %collective-permute-start.33) | collective-permute-done | bytes 4128 | tf_op jit(solution)/shard_map/ppermute | solution.py:24
  189.6 3.0 %collective-permute-start.34 = (f32[8,34,1]{2,1,0:T(8,128)S(1)}, f32[8,34,1]{2,1,0:T(8,128)S(1)}, u32[]{:S(2)}, u32[]{:S(2)}) collective-permute-start(f32[8,34,1]{2,1,0:T(8,128)S(1)} %get-tuple-element.11), channel_id=1, source_target_pairs={{0,1},{1,2},{2,3},{3,4},{4,5},{5,6},{6,7},{7,8},{8,9},{9,10},{10,1... | collective-permute-start | bytes 3272 | tf_op jit(solution)/shard_map/ppermute | solution.py:22
  192.6 1.9 collective-permute-start.35
  194.8 5.6 %collective-permute-done.35 = f32[8,34,1]{2,1,0:T(8,128)S(1)} collective-permute-done((f32[8,34,1]{2,1,0:T(8,128)S(1)}, f32[8,34,1]{2,1,0:T(8,128)S(1)}, u32[]{:S(2)}, u32[]{:S(2)}) %collective-permute-start.35) | collective-permute-done | bytes 1120 | tf_op jit(solution)/shard_map/ppermute | solution.py:24
  200.7 1.9 collective-permute-start.36
  202.6 3.4 %collective-permute-start.37 = (f32[8,1,128]{2,1,0:T(1,128)S(1)}, f32[8,1,128]{2,1,0:T(1,128)S(1)}, u32[]{:S(2)}, u32[]{:S(2)}) collective-permute-start(f32[8,1,128]{2,1,0:T(1,128)S(1)} %get-tuple-element.24), channel_id=1, source_target_pairs={{16,0},{32,16},{48,32},{64,48},{80,64},{96,80},{112,96},{128,112},... | collective-permute-start | bytes 12296 | tf_op jit(solution)/shard_map/ppermute | solution.py:24
  206.0 4.3 %collective-permute-done.37 = f32[8,1,128]{2,1,0:T(1,128)S(1)} collective-permute-done((f32[8,1,128]{2,1,0:T(1,128)S(1)}, f32[8,1,128]{2,1,0:T(1,128)S(1)}, u32[]{:S(2)}, u32[]{:S(2)}) %collective-permute-start.37) | collective-permute-done | bytes 4128 | tf_op jit(solution)/shard_map/ppermute | solution.py:24
  210.4 2.9 %collective-permute-start.38 = (f32[8,34,1]{2,1,0:T(8,128)S(1)}, f32[8,34,1]{2,1,0:T(8,128)S(1)}, u32[]{:S(2)}, u32[]{:S(2)}) collective-permute-start(f32[8,34,1]{2,1,0:T(8,128)S(1)} %get-tuple-element.9), channel_id=1, source_target_pairs={{0,1},{1,2},{2,3},{3,4},{4,5},{5,6},{6,7},{7,8},{8,9},{9,10},{10,1... | collective-permute-start | bytes 3272 | tf_op jit(solution)/shard_map/ppermute | solution.py:22
  213.3 1.9 collective-permute-start.39
  215.6 5.6 %collective-permute-done.39 = f32[8,34,1]{2,1,0:T(8,128)S(1)} collective-permute-done((f32[8,34,1]{2,1,0:T(8,128)S(1)}, f32[8,34,1]{2,1,0:T(8,128)S(1)}, u32[]{:S(2)}, u32[]{:S(2)}) %collective-permute-start.39) | collective-permute-done | bytes 1120 | tf_op jit(solution)/shard_map/ppermute | solution.py:24
  221.4 1.9 collective-permute-start.40
  223.4 3.4 %collective-permute-start.41 = (f32[8,1,128]{2,1,0:T(1,128)S(1)}, f32[8,1,128]{2,1,0:T(1,128)S(1)}, u32[]{:S(2)}, u32[]{:S(2)}) collective-permute-start(f32[8,1,128]{2,1,0:T(1,128)S(1)} %get-tuple-element.22), channel_id=1, source_target_pairs={{16,0},{32,16},{48,32},{64,48},{80,64},{96,80},{112,96},{128,112},... | collective-permute-start | bytes 12296 | tf_op jit(solution)/shard_map/ppermute | solution.py:24
  226.8 4.3 %collective-permute-done.41 = f32[8,1,128]{2,1,0:T(1,128)S(1)} collective-permute-done((f32[8,1,128]{2,1,0:T(1,128)S(1)}, f32[8,1,128]{2,1,0:T(1,128)S(1)}, u32[]{:S(2)}, u32[]{:S(2)}) %collective-permute-start.41) | collective-permute-done | bytes 4128 | tf_op jit(solution)/shard_map/ppermute | solution.py:24
  231.2 2.9 %collective-permute-start.42 = (f32[8,34,1]{2,1,0:T(8,128)S(1)}, f32[8,34,1]{2,1,0:T(8,128)S(1)}, u32[]{:S(2)}, u32[]{:S(2)}) collective-permute-start(f32[8,34,1]{2,1,0:T(8,128)S(1)} %get-tuple-element.7), channel_id=1, source_target_pairs={{0,1},{1,2},{2,3},{3,4},{4,5},{5,6},{6,7},{7,8},{8,9},{9,10},{10,1... | collective-permute-start | bytes 3272 | tf_op jit(solution)/shard_map/ppermute | solution.py:22
  234.1 1.9 collective-permute-start.43
  236.3 5.6 %collective-permute-done.43 = f32[8,34,1]{2,1,0:T(8,128)S(1)} collective-permute-done((f32[8,34,1]{2,1,0:T(8,128)S(1)}, f32[8,34,1]{2,1,0:T(8,128)S(1)}, u32[]{:S(2)}, u32[]{:S(2)}) %collective-permute-start.43) | collective-permute-done | bytes 1120 | tf_op jit(solution)/shard_map/ppermute | solution.py:24
  (116 shorter events, 15.5 us)
Async XLA Ops:
  1.4 43.4 %collective-permute-start.1 = (f32[8,1,128]{2,1,0:T(1,128)S(1)}, f32[8,1,128]{2,1,0:T(1,128)S(1)}, u32[]{:S(2)}, u32[]{:S(2)}) collective-permute-start(f32[8,1,128]{2,1,0:T(1,128)S(1)} %get-tuple-element.33), channel_id=1, source_target_pairs={{0,16},{16,32},{32,48},{48,64},{64,80},{80,96},{96,112},{112,128},... | collective-permute-start | bytes 12296 | tf_op jit(solution)/shard_map/ppermute | solution.py:22
  5.7 45.7 %collective-permute-start.3 = (f32[8,1,128]{2,1,0:T(1,128)S(1)}, f32[8,1,128]{2,1,0:T(1,128)S(1)}, u32[]{:S(2)}, u32[]{:S(2)}) collective-permute-start(f32[8,1,128]{2,1,0:T(1,128)S(1)} %get-tuple-element.34), channel_id=1, source_target_pairs={{16,0},{32,16},{48,32},{64,48},{80,64},{96,80},{112,96},{128,112},... | collective-permute-start | bytes 12296 | tf_op jit(solution)/shard_map/ppermute | solution.py:24
  15.4 36.2 %collective-permute-start.2 = (f32[8,1,128]{2,1,0:T(1,128)S(1)}, f32[8,1,128]{2,1,0:T(1,128)S(1)}, u32[]{:S(2)}, u32[]{:S(2)}) collective-permute-start(f32[8,1,128]{2,1,0:T(1,128)S(1)} %get-tuple-element.31), channel_id=1, source_target_pairs={{16,0},{32,16},{48,32},{64,48},{80,64},{96,80},{112,96},{128,112},... | collective-permute-start | bytes 12296 | tf_op jit(solution)/shard_map/ppermute | solution.py:24
  17.5 34.1 %collective-permute-start = (f32[8,1,128]{2,1,0:T(1,128)S(1)}, f32[8,1,128]{2,1,0:T(1,128)S(1)}, u32[]{:S(2)}, u32[]{:S(2)}) collective-permute-start(f32[8,1,128]{2,1,0:T(1,128)S(1)} %get-tuple-element.32), channel_id=1, source_target_pairs={{0,16},{16,32},{32,48},{48,64},{64,80},{80,96},{96,112},{112,128},... | collective-permute-start | bytes 12296 | tf_op jit(solution)/shard_map/ppermute | solution.py:22
  26.5 42.6 %all-to-all-start = ((f32[1,1,16,32,128]{4,3,1,0,2:T(8,128)}), f32[1,1,16,32,128]{4,3,1,0,2:T(8,128)S(1)}, u32[]{:S(2)}, u32[]{:S(2)}) async-start(f32[1,1,16,32,128]{4,3,1,0,2:T(8,128)} %bitcast_multiply_fusion), calls=%async_computation | async-start | bytes 524288 | tf_op jit(solution)/shard_map/all_to_all | solution.py:95
  40.1 3.9 %copy-start.3 = (f32[8,32,128]{2,1,0:T(8,128)S(1)}, f32[8,32,128]{2,1,0:T(8,128)}, u32[]{:S(2)}) copy-start(f32[8,32,128]{2,1,0:T(8,128)} %param.6) | copy-start | bytes 393220
  40.1 4.6 %copy-start.4 = (s32[1,1,16,32]{3,2,1,0:T(8,128)S(1)}, s32[1,1,16,32]{3,2,1,0:T(8,128)}, u32[]{:S(2)}) copy-start(s32[1,1,16,32]{3,2,1,0:T(8,128)} %param.11) | copy-start | bytes 6148
  42.1 19.2 %collective-permute-start.17 = (f32[8,1,64]{2,1,0:T(1,128)S(1)}, f32[8,1,64]{2,1,0:T(1,128)S(1)}, u32[]{:S(2)}, u32[]{:S(2)}) collective-permute-start(f32[8,1,64]{2,1,0:T(1,128)S(1)} %get-tuple-element.57), channel_id=1, source_target_pairs={{16,0},{32,16},{48,32},{64,48},{80,64},{96,80},{112,96},{128,112},... | collective-permute-start | bytes 6152 | tf_op jit(solution)/shard_map/ppermute | solution.py:24
  44.8 18.4 %collective-permute-start.16 = (f32[8,1,64]{2,1,0:T(1,128)S(1)}, f32[8,1,64]{2,1,0:T(1,128)S(1)}, u32[]{:S(2)}, u32[]{:S(2)}) collective-permute-start(f32[8,1,64]{2,1,0:T(1,128)S(1)} %get-tuple-element.58), channel_id=1, source_target_pairs={{0,16},{16,32},{32,48},{48,64},{64,80},{80,96},{96,112},{112,128},... | collective-permute-start | bytes 6152 | tf_op jit(solution)/shard_map/ppermute | solution.py:22
  51.8 11.4 %collective-permute-start.6 = (f32[8,34,1]{2,1,0:T(8,128)S(1)}, f32[8,34,1]{2,1,0:T(8,128)S(1)}, u32[]{:S(2)}, u32[]{:S(2)}) collective-permute-start(f32[8,34,1]{2,1,0:T(8,128)S(1)} %get-tuple-element.17), channel_id=1, source_target_pairs={{1,0},{2,1},{3,2},{4,3},{5,4},{6,5},{7,6},{8,7},{9,8},{10,9},{11,1... | collective-permute-start | bytes 3272 | tf_op jit(solution)/shard_map/ppermute | solution.py:24
  54.6 8.6 %collective-permute-start.4 = (f32[8,34,1]{2,1,0:T(8,128)S(1)}, f32[8,34,1]{2,1,0:T(8,128)S(1)}, u32[]{:S(2)}, u32[]{:S(2)}) collective-permute-start(f32[8,34,1]{2,1,0:T(8,128)S(1)} %get-tuple-element.18), channel_id=1, source_target_pairs={{0,1},{1,2},{2,3},{3,4},{4,5},{5,6},{6,7},{7,8},{8,9},{9,10},{10,1... | collective-permute-start | bytes 3272 | tf_op jit(solution)/shard_map/ppermute | solution.py:22
  58.8 4.7 %collective-permute-start.5 = (f32[8,34,1]{2,1,0:T(8,128)S(1)}, f32[8,34,1]{2,1,0:T(8,128)S(1)}, u32[]{:S(2)}, u32[]{:S(2)}) collective-permute-start(f32[8,34,1]{2,1,0:T(8,128)S(1)} %get-tuple-element.19), channel_id=1, source_target_pairs={{0,1},{1,2},{2,3},{3,4},{4,5},{5,6},{6,7},{7,8},{8,9},{9,10},{10,1... | collective-permute-start | bytes 3272 | tf_op jit(solution)/shard_map/ppermute | solution.py:22
  61.2 7.8 %collective-permute-start.7 = (f32[8,34,1]{2,1,0:T(8,128)S(1)}, f32[8,34,1]{2,1,0:T(8,128)S(1)}, u32[]{:S(2)}, u32[]{:S(2)}) collective-permute-start(f32[8,34,1]{2,1,0:T(8,128)S(1)} %get-tuple-element.20), channel_id=1, source_target_pairs={{1,0},{2,1},{3,2},{4,3},{5,4},{6,5},{7,6},{8,7},{9,8},{10,9},{11,1... | collective-permute-start | bytes 3272 | tf_op jit(solution)/shard_map/ppermute | solution.py:24
  69.6 12.2 %collective-permute-start.8 = (f32[8,1,128]{2,1,0:T(1,128)S(1)}, f32[8,1,128]{2,1,0:T(1,128)S(1)}, u32[]{:S(2)}, u32[]{:S(2)}) collective-permute-start(f32[8,1,128]{2,1,0:T(1,128)S(1)} %get-tuple-element.29), channel_id=1, source_target_pairs={{0,16},{16,32},{32,48},{48,64},{64,80},{80,96},{96,112},{112,128},... | collective-permute-start | bytes 12296 | tf_op jit(solution)/shard_map/ppermute | solution.py:22
  71.5 10.3 %collective-permute-start.9 = (f32[8,1,128]{2,1,0:T(1,128)S(1)}, f32[8,1,128]{2,1,0:T(1,128)S(1)}, u32[]{:S(2)}, u32[]{:S(2)}) collective-permute-start(f32[8,1,128]{2,1,0:T(1,128)S(1)} %get-tuple-element.30), channel_id=1, source_target_pairs={{16,0},{32,16},{48,32},{64,48},{80,64},{96,80},{112,96},{128,112},... | collective-permute-start | bytes 12296 | tf_op jit(solution)/shard_map/ppermute | solution.py:24
  75.0 24.2 %collective-permute-start.19 = (f32[8,18,1]{2,0,1:T(8,128)S(1)}, f32[8,18,1]{2,0,1:T(8,128)S(1)}, u32[]{:S(2)}, u32[]{:S(2)}) collective-permute-start(f32[8,18,1]{2,0,1:T(8,128)S(1)} %get-tuple-element.49), channel_id=1, source_target_pairs={{1,0},{2,1},{3,2},{4,3},{5,4},{6,5},{7,6},{8,7},{9,8},{10,9},{11,1... | collective-permute-start | bytes 1736 | tf_op jit(solution)/shard_map/ppermute | solution.py:24
  76.9 22.2 %collective-permute-start.18 = (f32[8,18,1]{2,0,1:T(8,128)S(1)}, f32[8,18,1]{2,0,1:T(8,128)S(1)}, u32[]{:S(2)}, u32[]{:S(2)}) collective-permute-start(f32[8,18,1]{2,0,1:T(8,128)S(1)} %get-tuple-element.50), channel_id=1, source_target_pairs={{0,1},{1,2},{2,3},{3,4},{4,5},{5,6},{6,7},{7,8},{8,9},{9,10},{10,1... | collective-permute-start | bytes 1736 | tf_op jit(solution)/shard_map/ppermute | solution.py:22
  81.9 4.4 %collective-permute-start.10 = (f32[8,34,1]{2,1,0:T(8,128)S(1)}, f32[8,34,1]{2,1,0:T(8,128)S(1)}, u32[]{:S(2)}, u32[]{:S(2)}) collective-permute-start(f32[8,34,1]{2,1,0:T(8,128)S(1)} %get-tuple-element.15), channel_id=1, source_target_pairs={{0,1},{1,2},{2,3},{3,4},{4,5},{5,6},{6,7},{7,8},{8,9},{9,10},{10,1... | collective-permute-start | bytes 3272 | tf_op jit(solution)/shard_map/ppermute | solution.py:22
  83.9 7.8 %collective-permute-start.11 = (f32[8,34,1]{2,1,0:T(8,128)S(1)}, f32[8,34,1]{2,1,0:T(8,128)S(1)}, u32[]{:S(2)}, u32[]{:S(2)}) collective-permute-start(f32[8,34,1]{2,1,0:T(8,128)S(1)} %get-tuple-element.16), channel_id=1, source_target_pairs={{1,0},{2,1},{3,2},{4,3},{5,4},{6,5},{7,6},{8,7},{9,8},{10,9},{11,1... | collective-permute-start | bytes 3272 | tf_op jit(solution)/shard_map/ppermute | solution.py:24
  92.0 7.9 %collective-permute-start.12 = (f32[8,1,128]{2,1,0:T(1,128)S(1)}, f32[8,1,128]{2,1,0:T(1,128)S(1)}, u32[]{:S(2)}, u32[]{:S(2)}) collective-permute-start(f32[8,1,128]{2,1,0:T(1,128)S(1)} %get-tuple-element.27), channel_id=1, source_target_pairs={{0,16},{16,32},{32,48},{48,64},{64,80},{80,96},{96,112},{112,128},... | collective-permute-start | bytes 12296 | tf_op jit(solution)/shard_map/ppermute | solution.py:22
  97.2 7.7 %collective-permute-start.13 = (f32[8,1,128]{2,1,0:T(1,128)S(1)}, f32[8,1,128]{2,1,0:T(1,128)S(1)}, u32[]{:S(2)}, u32[]{:S(2)}) collective-permute-start(f32[8,1,128]{2,1,0:T(1,128)S(1)} %get-tuple-element.28), channel_id=1, source_target_pairs={{16,0},{32,16},{48,32},{64,48},{80,64},{96,80},{112,96},{128,112},... | collective-permute-start | bytes 12296 | tf_op jit(solution)/shard_map/ppermute | solution.py:24
  105.0 5.4 %collective-permute-start.14 = (f32[8,34,1]{2,1,0:T(8,128)S(1)}, f32[8,34,1]{2,1,0:T(8,128)S(1)}, u32[]{:S(2)}, u32[]{:S(2)}) collective-permute-start(f32[8,34,1]{2,1,0:T(8,128)S(1)} %get-tuple-element.13), channel_id=1, source_target_pairs={{0,1},{1,2},{2,3},{3,4},{4,5},{5,6},{6,7},{7,8},{8,9},{9,10},{10,1... | collective-permute-start | bytes 3272 | tf_op jit(solution)/shard_map/ppermute | solution.py:22
  108.2 7.8 %collective-permute-start.15 = (f32[8,34,1]{2,1,0:T(8,128)S(1)}, f32[8,34,1]{2,1,0:T(8,128)S(1)}, u32[]{:S(2)}, u32[]{:S(2)}) collective-permute-start(f32[8,34,1]{2,1,0:T(8,128)S(1)} %get-tuple-element.14), channel_id=1, source_target_pairs={{1,0},{2,1},{3,2},{4,3},{5,4},{6,5},{7,6},{8,7},{9,8},{10,9},{11,1... | collective-permute-start | bytes 3272 | tf_op jit(solution)/shard_map/ppermute | solution.py:24
  118.6 20.8 %copy-start.1 = (f32[8,16,64]{2,0,1:T(8,128)S(1)}, f32[8,16,64]{2,0,1:T(8,128)}, u32[]{:S(2)}) copy-start(f32[8,16,64]{2,0,1:T(8,128)} %get-tuple-element.48) | copy-start | bytes 98308
  118.6 20.8 %copy-start.2 = (f32[7,16,64]{2,1,0:T(8,128)S(1)}, f32[7,16,64]{2,1,0:T(8,128)}, u32[]{:S(2)}) copy-start(f32[7,16,64]{2,1,0:T(8,128)} %fusion.169) | copy-start | bytes 86020
  119.8 5.3 %collective-permute-start.20 = (f32[8,1,64]{2,1,0:T(1,128)S(1)}, f32[8,1,64]{2,1,0:T(1,128)S(1)}, u32[]{:S(2)}, u32[]{:S(2)}) collective-permute-start(f32[8,1,64]{2,1,0:T(1,128)S(1)} %get-tuple-element.55), channel_id=1, source_target_pairs={{0,16},{16,32},{32,48},{48,64},{64,80},{80,96},{96,112},{112,128},... | collective-permute-start | bytes 6152 | tf_op jit(solution)/shard_map/ppermute | solution.py:22
  121.7 7.7 %collective-permute-start.21 = (f32[8,1,64]{2,1,0:T(1,128)S(1)}, f32[8,1,64]{2,1,0:T(1,128)S(1)}, u32[]{:S(2)}, u32[]{:S(2)}) collective-permute-start(f32[8,1,64]{2,1,0:T(1,128)S(1)} %get-tuple-element.56), channel_id=1, source_target_pairs={{16,0},{32,16},{48,32},{64,48},{80,64},{96,80},{112,96},{128,112},... | collective-permute-start | bytes 6152 | tf_op jit(solution)/shard_map/ppermute | solution.py:24
  129.5 4.9 %collective-permute-start.22 = (f32[8,18,1]{2,0,1:T(8,128)S(1)}, f32[8,18,1]{2,0,1:T(8,128)S(1)}, u32[]{:S(2)}, u32[]{:S(2)}) collective-permute-start(f32[8,18,1]{2,0,1:T(8,128)S(1)} %get-tuple-element.45), channel_id=1, source_target_pairs={{0,1},{1,2},{2,3},{3,4},{4,5},{5,6},{6,7},{7,8},{8,9},{9,10},{10,1... | collective-permute-start | bytes 1736 | tf_op jit(solution)/shard_map/ppermute | solution.py:22
  132.4 6.9 %collective-permute-start.23 = (f32[8,18,1]{2,0,1:T(8,128)S(1)}, f32[8,18,1]{2,0,1:T(8,128)S(1)}, u32[]{:S(2)}, u32[]{:S(2)}) collective-permute-start(f32[8,18,1]{2,0,1:T(8,128)S(1)} %get-tuple-element.46), channel_id=1, source_target_pairs={{1,0},{2,1},{3,2},{4,3},{5,4},{6,5},{7,6},{8,7},{9,8},{10,9},{11,1... | collective-permute-start | bytes 1736 | tf_op jit(solution)/shard_map/ppermute | solution.py:24
  139.6 5.3 %collective-permute-start.24 = (f32[8,1,64]{2,1,0:T(1,128)S(1)}, f32[8,1,64]{2,1,0:T(1,128)S(1)}, u32[]{:S(2)}, u32[]{:S(2)}) collective-permute-start(f32[8,1,64]{2,1,0:T(1,128)S(1)} %get-tuple-element.53), channel_id=1, source_target_pairs={{0,16},{16,32},{32,48},{48,64},{64,80},{80,96},{96,112},{112,128},... | collective-permute-start | bytes 6152 | tf_op jit(solution)/shard_map/ppermute | solution.py:22
  141.5 7.7 %collective-permute-start.25 = (f32[8,1,64]{2,1,0:T(1,128)S(1)}, f32[8,1,64]{2,1,0:T(1,128)S(1)}, u32[]{:S(2)}, u32[]{:S(2)}) collective-permute-start(f32[8,1,64]{2,1,0:T(1,128)S(1)} %get-tuple-element.54), channel_id=1, source_target_pairs={{16,0},{32,16},{48,32},{64,48},{80,64},{96,80},{112,96},{128,112},... | collective-permute-start | bytes 6152 | tf_op jit(solution)/shard_map/ppermute | solution.py:24
  149.3 5.0 %collective-permute-start.26 = (f32[8,18,1]{2,0,1:T(8,128)S(1)}, f32[8,18,1]{2,0,1:T(8,128)S(1)}, u32[]{:S(2)}, u32[]{:S(2)}) collective-permute-start(f32[8,18,1]{2,0,1:T(8,128)S(1)} %get-tuple-element.41), channel_id=1, source_target_pairs={{0,1},{1,2},{2,3},{3,4},{4,5},{5,6},{6,7},{7,8},{8,9},{9,10},{10,1... | collective-permute-start | bytes 1736 | tf_op jit(solution)/shard_map/ppermute | solution.py:22
  152.3 6.9 %collective-permute-start.27 = (f32[8,18,1]{2,0,1:T(8,128)S(1)}, f32[8,18,1]{2,0,1:T(8,128)S(1)}, u32[]{:S(2)}, u32[]{:S(2)}) collective-permute-start(f32[8,18,1]{2,0,1:T(8,128)S(1)} %get-tuple-element.42), channel_id=1, source_target_pairs={{1,0},{2,1},{3,2},{4,3},{5,4},{6,5},{7,6},{8,7},{9,8},{10,9},{11,1... | collective-permute-start | bytes 1736 | tf_op jit(solution)/shard_map/ppermute | solution.py:24
  159.5 5.3 %collective-permute-start.28 = (f32[8,1,64]{2,1,0:T(1,128)S(1)}, f32[8,1,64]{2,1,0:T(1,128)S(1)}, u32[]{:S(2)}, u32[]{:S(2)}) collective-permute-start(f32[8,1,64]{2,1,0:T(1,128)S(1)} %get-tuple-element.51), channel_id=1, source_target_pairs={{0,16},{16,32},{32,48},{48,64},{64,80},{80,96},{96,112},{112,128},... | collective-permute-start | bytes 6152 | tf_op jit(solution)/shard_map/ppermute | solution.py:22
  161.4 7.7 %collective-permute-start.29 = (f32[8,1,64]{2,1,0:T(1,128)S(1)}, f32[8,1,64]{2,1,0:T(1,128)S(1)}, u32[]{:S(2)}, u32[]{:S(2)}) collective-permute-start(f32[8,1,64]{2,1,0:T(1,128)S(1)} %get-tuple-element.52), channel_id=1, source_target_pairs={{16,0},{32,16},{48,32},{64,48},{80,64},{96,80},{112,96},{128,112},... | collective-permute-start | bytes 6152 | tf_op jit(solution)/shard_map/ppermute | solution.py:24
  169.2 5.0 %collective-permute-start.30 = (f32[8,18,1]{2,0,1:T(8,128)S(1)}, f32[8,18,1]{2,0,1:T(8,128)S(1)}, u32[]{:S(2)}, u32[]{:S(2)}) collective-permute-start(f32[8,18,1]{2,0,1:T(8,128)S(1)} %get-tuple-element.37), channel_id=1, source_target_pairs={{0,1},{1,2},{2,3},{3,4},{4,5},{5,6},{6,7},{7,8},{8,9},{9,10},{10,1... | collective-permute-start | bytes 1736 | tf_op jit(solution)/shard_map/ppermute | solution.py:22
  172.2 6.9 %collective-permute-start.31 = (f32[8,18,1]{2,0,1:T(8,128)S(1)}, f32[8,18,1]{2,0,1:T(8,128)S(1)}, u32[]{:S(2)}, u32[]{:S(2)}) collective-permute-start(f32[8,18,1]{2,0,1:T(8,128)S(1)} %get-tuple-element.38), channel_id=1, source_target_pairs={{1,0},{2,1},{3,2},{4,3},{5,4},{6,5},{7,6},{8,7},{9,8},{10,9},{11,1... | collective-permute-start | bytes 1736 | tf_op jit(solution)/shard_map/ppermute | solution.py:24
  179.8 5.3 %collective-permute-start.32 = (f32[8,1,128]{2,1,0:T(1,128)S(1)}, f32[8,1,128]{2,1,0:T(1,128)S(1)}, u32[]{:S(2)}, u32[]{:S(2)}) collective-permute-start(f32[8,1,128]{2,1,0:T(1,128)S(1)} %get-tuple-element.25), channel_id=1, source_target_pairs={{0,16},{16,32},{32,48},{48,64},{64,80},{80,96},{96,112},{112,128},... | collective-permute-start | bytes 12296 | tf_op jit(solution)/shard_map/ppermute | solution.py:22
  181.8 7.7 %collective-permute-start.33 = (f32[8,1,128]{2,1,0:T(1,128)S(1)}, f32[8,1,128]{2,1,0:T(1,128)S(1)}, u32[]{:S(2)}, u32[]{:S(2)}) collective-permute-start(f32[8,1,128]{2,1,0:T(1,128)S(1)} %get-tuple-element.26), channel_id=1, source_target_pairs={{16,0},{32,16},{48,32},{64,48},{80,64},{96,80},{112,96},{128,112},... | collective-permute-start | bytes 12296 | tf_op jit(solution)/shard_map/ppermute | solution.py:24
  189.6 5.3 %collective-permute-start.34 = (f32[8,34,1]{2,1,0:T(8,128)S(1)}, f32[8,34,1]{2,1,0:T(8,128)S(1)}, u32[]{:S(2)}, u32[]{:S(2)}) collective-permute-start(f32[8,34,1]{2,1,0:T(8,128)S(1)} %get-tuple-element.11), channel_id=1, source_target_pairs={{0,1},{1,2},{2,3},{3,4},{4,5},{5,6},{6,7},{7,8},{8,9},{9,10},{10,1... | collective-permute-start | bytes 3272 | tf_op jit(solution)/shard_map/ppermute | solution.py:22
  192.6 7.8 %collective-permute-start.35 = (f32[8,34,1]{2,1,0:T(8,128)S(1)}, f32[8,34,1]{2,1,0:T(8,128)S(1)}, u32[]{:S(2)}, u32[]{:S(2)}) collective-permute-start(f32[8,34,1]{2,1,0:T(8,128)S(1)} %get-tuple-element.12), channel_id=1, source_target_pairs={{1,0},{2,1},{3,2},{4,3},{5,4},{6,5},{7,6},{8,7},{9,8},{10,9},{11,1... | collective-permute-start | bytes 3272 | tf_op jit(solution)/shard_map/ppermute | solution.py:24
  200.7 5.3 %collective-permute-start.36 = (f32[8,1,128]{2,1,0:T(1,128)S(1)}, f32[8,1,128]{2,1,0:T(1,128)S(1)}, u32[]{:S(2)}, u32[]{:S(2)}) collective-permute-start(f32[8,1,128]{2,1,0:T(1,128)S(1)} %get-tuple-element.23), channel_id=1, source_target_pairs={{0,16},{16,32},{32,48},{48,64},{64,80},{80,96},{96,112},{112,128},... | collective-permute-start | bytes 12296 | tf_op jit(solution)/shard_map/ppermute | solution.py:22
  202.6 7.7 %collective-permute-start.37 = (f32[8,1,128]{2,1,0:T(1,128)S(1)}, f32[8,1,128]{2,1,0:T(1,128)S(1)}, u32[]{:S(2)}, u32[]{:S(2)}) collective-permute-start(f32[8,1,128]{2,1,0:T(1,128)S(1)} %get-tuple-element.24), channel_id=1, source_target_pairs={{16,0},{32,16},{48,32},{64,48},{80,64},{96,80},{112,96},{128,112},... | collective-permute-start | bytes 12296 | tf_op jit(solution)/shard_map/ppermute | solution.py:24
  210.4 5.1 %collective-permute-start.38 = (f32[8,34,1]{2,1,0:T(8,128)S(1)}, f32[8,34,1]{2,1,0:T(8,128)S(1)}, u32[]{:S(2)}, u32[]{:S(2)}) collective-permute-start(f32[8,34,1]{2,1,0:T(8,128)S(1)} %get-tuple-element.9), channel_id=1, source_target_pairs={{0,1},{1,2},{2,3},{3,4},{4,5},{5,6},{6,7},{7,8},{8,9},{9,10},{10,1... | collective-permute-start | bytes 3272 | tf_op jit(solution)/shard_map/ppermute | solution.py:22
  213.3 7.8 %collective-permute-start.39 = (f32[8,34,1]{2,1,0:T(8,128)S(1)}, f32[8,34,1]{2,1,0:T(8,128)S(1)}, u32[]{:S(2)}, u32[]{:S(2)}) collective-permute-start(f32[8,34,1]{2,1,0:T(8,128)S(1)} %get-tuple-element.10), channel_id=1, source_target_pairs={{1,0},{2,1},{3,2},{4,3},{5,4},{6,5},{7,6},{8,7},{9,8},{10,9},{11,1... | collective-permute-start | bytes 3272 | tf_op jit(solution)/shard_map/ppermute | solution.py:24
  221.4 21.4 %copy-start = (f32[8,32,128]{2,1,0:T(8,128)}, f32[8,32,128]{2,1,0:T(8,128)S(1)}, u32[]{:S(2)}) copy-start(f32[8,32,128]{2,1,0:T(8,128)S(1)} %fusion.26) | copy-start | bytes 393220
  221.4 5.3 %collective-permute-start.40 = (f32[8,1,128]{2,1,0:T(1,128)S(1)}, f32[8,1,128]{2,1,0:T(1,128)S(1)}, u32[]{:S(2)}, u32[]{:S(2)}) collective-permute-start(f32[8,1,128]{2,1,0:T(1,128)S(1)} %get-tuple-element.21), channel_id=1, source_target_pairs={{0,16},{16,32},{32,48},{48,64},{64,80},{80,96},{96,112},{112,128},... | collective-permute-start | bytes 12296 | tf_op jit(solution)/shard_map/ppermute | solution.py:22
  223.4 7.7 %collective-permute-start.41 = (f32[8,1,128]{2,1,0:T(1,128)S(1)}, f32[8,1,128]{2,1,0:T(1,128)S(1)}, u32[]{:S(2)}, u32[]{:S(2)}) collective-permute-start(f32[8,1,128]{2,1,0:T(1,128)S(1)} %get-tuple-element.22), channel_id=1, source_target_pairs={{16,0},{32,16},{48,32},{64,48},{80,64},{96,80},{112,96},{128,112},... | collective-permute-start | bytes 12296 | tf_op jit(solution)/shard_map/ppermute | solution.py:24
  231.2 5.1 %collective-permute-start.42 = (f32[8,34,1]{2,1,0:T(8,128)S(1)}, f32[8,34,1]{2,1,0:T(8,128)S(1)}, u32[]{:S(2)}, u32[]{:S(2)}) collective-permute-start(f32[8,34,1]{2,1,0:T(8,128)S(1)} %get-tuple-element.7), channel_id=1, source_target_pairs={{0,1},{1,2},{2,3},{3,4},{4,5},{5,6},{6,7},{7,8},{8,9},{9,10},{10,1... | collective-permute-start | bytes 3272 | tf_op jit(solution)/shard_map/ppermute | solution.py:22
  234.1 7.8 %collective-permute-start.43 = (f32[8,34,1]{2,1,0:T(8,128)S(1)}, f32[8,34,1]{2,1,0:T(8,128)S(1)}, u32[]{:S(2)}, u32[]{:S(2)}) collective-permute-start(f32[8,34,1]{2,1,0:T(8,128)S(1)} %get-tuple-element.8), channel_id=1, source_target_pairs={{1,0},{2,1},{3,2},{4,3},{5,4},{6,5},{7,6},{8,7},{9,8},{10,9},{11,1... | collective-permute-start | bytes 3272 | tf_op jit(solution)/shard_map/ppermute | solution.py:24
where the time goes:
time: 244 us; the launch traced here: 243 us
  starting transfers between devices  137 us (56%)
  waiting for transfers between devices  80.3 us (33%)
  other arithmetic  17.3 us (7%)
  local copies, waits for them, and re-layouts  5.75 us (2%)
    ppermute x22, waiting for transfers between devices, extended(): lax.ppermute(head, axis, [((i + 1) % count, i) for i in range(ends)])  78.9 us
    ppermute x22, starting transfers between devices, extended(): lax.ppermute(tail, axis, [(i, (i + 1) % count) for i in range(ends)])  70.4 us
    ppermute x22, starting transfers between devices, extended(): lax.ppermute(head, axis, [((i + 1) % count, i) for i in range(ends)])  53.9 us
    all_to_all x1, starting transfers between devices, body(): lax.all_to_all(outgoing, 'cols', split_axis=2, concat_axis=1, tiled=True)  13 us
    add x1, other arithmetic, body(): cond = cond + jnp.where(class_map == category, class_cond[category], 0.0)  6.07 us
  transfers between devices with their start and end apart: 45, of which 21 were waited for; matrix products, arithmetic and copies ran while one was open for 6% of the time, Pallas kernels for 0%

commit v1 on v0

v1 whole, which is shorter than its diff:
```python
import jax
import jax.numpy as jnp
from jax import lax
from jax.experimental import pallas as pl
from jax.experimental.pallas import tpu as pltpu
from jax.sharding import PartitionSpec as P

NZ, CY, CX, SLOTS = 8, 32, 128, 32
OMEGA = 0.8
NU1, NU2, NUC = 2, 2, 4
HY, HX = 14, 16
RY = 12
ROWS = CY + 2 * HY
LANES = 2 * CX
F32 = jnp.float32


def lane_of(shape):
    return lax.broadcasted_iota(jnp.int32, shape, len(shape) - 1)


def packed(rows, lane):
    out = None
    for q, row in enumerate(rows):
        turned = pltpu.roll(row, 32 * q + 16, 1)
        out = turned if q == 0 else jnp.where(lane // 32 == q, turned, out)
    return out


def unpacked(block, q, lane):
    turned = pltpu.roll(block, (CX - 32 * q - 16) % CX, 1)
    return jnp.where((lane < HX) | (lane >= CX - HX), turned, 0.0)


def outgoing_kernel(count_ref, partials_ref, out_ref):
    ncols = partials_ref.shape[0]
    lane = lane_of((8, CX))
    slot = lax.broadcasted_iota(jnp.int32, (8, CX), 0)
    strips = []
    for d in range(ncols):
        rows = []
        for q in range(SLOTS // 8):
            row = jnp.where(slot + 8 * q < count_ref[d], partials_ref[d, 8 * q : 8 * q + 8, :], 0.0)
            out_ref[d, 8 * q : 8 * q + 8, :] = row
            rows.append(row)
        strips.append(packed(rows, lane))
    zero = jnp.zeros((8, CX), F32)
    for d in range(ncols):
        left = strips[d - 1] if d > 0 else zero
        right = strips[d + 1] if d < ncols - 1 else zero
        out_ref[d, SLOTS : SLOTS + 8, :] = jnp.where(lane % 32 < HX, left, right)


def fields_kernel(class_cond_ref, head_ref, class_ref, ids_ref, head_out, cond_out, strip_out):
    lane = lane_of((8, CX))
    values = [class_cond_ref[c] for c in range(8)]
    for block in range(CY // 4):
        heads, conds = [], []
        for q in range(4):
            y = 4 * block + q
            head = head_ref[pl.ds(y, NZ, stride=CY), :]
            kind = class_ref[pl.ds(y, NZ, stride=CY), :]
            cond = jnp.full((8, CX), values[0], F32)
            for c in range(1, 8):
                cond = jnp.where(kind == c, values[c], cond)
            head_out[y] = head
            cond_out[y] = cond
            heads.append(head)
            conds.append(cond)
        strip_out[block] = packed(heads, lane)
        strip_out[CY // 4 + block] = packed(conds, lane)
    strip_out[CY // 2] = ids_ref[...]


def recharge_kernel(incoming_ref, ids_ref, left_ref, right_ref, head_ref, cond_ref, main_out, halo_out, up_out, down_out):
    ncols = incoming_ref.shape[0]
    total = ncols * SLOTS
    chunk = min(256, total)
    senders = chunk // SLOTS
    lane = lane_of((8, CX))
    row = lax.broadcasted_iota(jnp.int32, (NZ * CY, chunk), 0)
    block_of = ((row % NZ) * CY + row // NZ).astype(F32)

    def onehot(ids, m):
        flat = jnp.concatenate([ids[r : r + 1, :] for r in range(m * chunk // CX, (m + 1) * chunk // CX)], axis=1)
        return jnp.where(block_of == flat, 1.0, 0.0).astype(jnp.bfloat16)

    def halves(values):
        high = values.astype(jnp.bfloat16)
        low = (values - high.astype(F32)).astype(jnp.bfloat16)
        return jnp.concatenate([high, low], axis=1)

    own, left, right = ids_ref[...], left_ref[CY // 2], right_ref[CY // 2]
    main = jnp.zeros((NZ * CY, LANES), F32)
    from_left = jnp.zeros((NZ * CY, LANES), F32)
    from_right = jnp.zeros((NZ * CY, LANES), F32)
    for m in range(total // chunk):
        values = incoming_ref[m * senders : (m + 1) * senders, 0:SLOTS, :].reshape(chunk, CX)
        main = main + jnp.dot(onehot(own, m), halves(values), preferred_element_type=F32)
        strips = []
        for s in range(m * senders, (m + 1) * senders):
            strip = incoming_ref[s, SLOTS : SLOTS + 8, :]
            strips += [pltpu.roll(strip, (CX - 32 * q - 16) % CX, 1) for q in range(4)]
        edges = halves(jnp.concatenate(strips, axis=0))
        from_left = from_left + jnp.dot(onehot(left, m), edges, preferred_element_type=F32)
        from_right = from_right + jnp.dot(onehot(right, m), edges, preferred_element_type=F32)
    main = (main[:, :CX] + main[:, CX:]).reshape(CY, NZ, CX)
    from_left = (from_left[:, :CX] + from_left[:, CX:]).reshape(CY, NZ, CX)
    from_right = (from_right[:, :CX] + from_right[:, CX:]).reshape(CY, NZ, CX)
    wide = lane_of((CY, NZ, CX))
    halo = jnp.where(wide >= CX - HX, from_left, jnp.where(wide < HX, from_right, 0.0))
    main_out[...] = main
    halo_out[...] = halo
    for out, first, strip0 in ((up_out, 0, 0), (down_out, CY - HY, CY // 4 - 4)):
        skip = first and HY - RY
        out[0:HY] = head_ref[first : first + HY]
        out[HY : 2 * HY] = cond_ref[first : first + HY]
        out[2 * HY : 2 * HY + RY] = main[first + skip : first + skip + RY]
        base = 2 * HY + RY
        for i in range(4):
            for f in range(2):
                at = f * (CY // 4) + strip0 + i
                out[base + 4 * f + i] = jnp.where(lane % 32 < HX, left_ref[at], right_ref[at])
        for i in range(RY // 4):
            y = first + skip + 4 * i
            out[base + 8 + i] = packed([halo[y + q] for q in range(4)], lane)


SENT = 2 * HY + RY + 8 + RY // 4


def cycle_kernel(place_ref, head_ref, cond_ref, main_ref, halo_ref, left_ref, right_ref, top_ref, bottom_ref,
                 head_out, residual_out,
                 u0, u1, cond, source, face_x, face_y, face_z, weight,
                 c_cond, c_src, c_u0, c_u1, c_x, c_y, c_z, c_weight):
    lane = lane_of((8, CX))
    for y in range(CY):
        r = HY + y
        u0[r, :, 0:CX] = head_ref[y]
        cond[r, :, 0:CX] = cond_ref[y]
        source[r, :, 0:CX] = main_ref[y]
        source[r, :, CX:LANES] = halo_ref[y]
    for i in range(CY // 4):
        for f, field in ((0, u0), (1, cond)):
            at = f * (CY // 4) + i
            block = jnp.where(lane % 32 < HX, left_ref[at], right_ref[at])
            for q in range(4):
                field[HY + 4 * i + q, :, CX:LANES] = unpacked(block, q, lane)
    base = 2 * HY + RY
    for ref, row0, shift, rrow, in ((top_ref, 0, 2, HY - RY), (bottom_ref, HY + CY, 0, HY + CY)):
        for i in range(HY):
            for f, field in ((0, u0), (1, cond)):
                field[row0 + i, :, 0:CX] = ref[f * HY + i]
                field[row0 + i, :, CX:LANES] = unpacked(ref[base + 4 * f + (i + shift) // 4], (i + shift) % 4, lane)
        for i in range(RY):
            source[rrow + i, :, 0:CX] = ref[2 * HY + i]
            source[rrow + i, :, CX:LANES] = unpacked(ref[base + 8 + i // 4], i % 4, lane)

    g, d, ngroups, ncols = place_ref[0], place_ref[1], place_ref[2], place_ref[3]

    def over_rows(first, last, step, body):
        count = last - first + 1
        assert count % step == 0
        pl.loop(0, count // step)(lambda i: body(first + i * step))

    def turn(x, by):
        return pltpu.roll(x, by % LANES, x.ndim - 1)

    def turn_z(x, by):
        return pltpu.roll(x, by % NZ, x.ndim - 2)

    def inside(shape, r, factor):
        at = lane_of(shape)
        x = jnp.where(at < CX + HX, at, jnp.where(at >= LANES - HX, at - LANES, -(1 << 20))) + d * CX
        y = lax.broadcasted_iota(jnp.int32, shape, 0) + (r - HY // factor) + g * (CY // factor)
        return (x >= 0) & (x < ncols * CX) & (y >= 0) & (y < ngroups * (CY // factor))

    def faces(k, fx, fy, fz, shift, zweight, first, last, step):
        def body(r):
            c = k[pl.ds(r, step + 1)]
            low, high = c[:-1], c[1:]
            fx[pl.ds(r, step)] = 0.5 * (low + turn(low, -shift))
            fy[pl.ds(r, step)] = 0.5 * (low + high)
            z = lax.broadcasted_iota(jnp.int32, low.shape, 1)
            fz[pl.ds(r, step)] = jnp.where(z < NZ - 1, (0.5 * zweight) * (low + turn_z(low, -1)), 0.0)

        over_rows(first, last, step, body)

    def weights(fx, fy, fz, w, shift, factor, first, last, step):
        def body(r):
            x, z = fx[pl.ds(r, step)], fz[pl.ds(r, step)]
            y = fy[pl.ds(r - 1, step + 1)]
            total = x + turn(x, shift) + y[1:] + y[:-1] + z + turn_z(z, 1)
            ok = inside(total.shape, r, factor)
            w[pl.ds(r, step)] = jnp.where(ok, OMEGA / jnp.where(ok, total, 1.0), 0.0)

        over_rows(first, last, step, body)

    def operator(u, fx, fy, fz, shift, r, step):
        v = u[pl.ds(r - 1, step + 2)]
        own = v[1:-1]
        x = fx[pl.ds(r, step)] * (own - turn(own, -shift))
        y = fy[pl.ds(r - 1, step + 1)] * (v[:-1] - v[1:])
        z = fz[pl.ds(r, step)] * (turn_z(own, -1) - own)
        return own, (x - turn(x, shift)) + (y[1:] - y[:-1]) + (z - turn_z(z, 1))

    def sweep(old, new, src, fx, fy, fz, w, shift, first, last, step):
        def body(r):
            own, applied = operator(old, fx, fy, fz, shift, r, step)
            new[pl.ds(r, step)] = own + w[pl.ds(r, step)] * (src[pl.ds(r, step)] - applied)

        over_rows(first, last, step, body)

    def pairs(x):
        even = lane_of(x.shape) % 2 == 0
        return x + jnp.where(even, turn(x, -1), turn(x, 1))

    fine = (face_x, face_y, face_z)
    coarse = (c_x, c_y, c_z)
    faces(cond, *fine, 1, 1.0, 0, ROWS - 3, 2)
    faces(cond, *fine, 1, 1.0, ROWS - 2, ROWS - 2, 1)
    weights(*fine, weight, 1, 1, 2, ROWS - 3, 2)
    sweep(u0, u1, source, *fine, weight, 1, 2, ROWS - 3, 2)
    sweep(u1, u0, source, *fine, weight, 1, 3, ROWS - 4, 2)

    def restrict_cond(c):
        k = cond[pl.ds(2 * c, 2)]
        c_cond[pl.ds(c, 1)] = 0.25 * pairs(k[0:1] + k[1:2])

    over_rows(0, ROWS // 2 - 1, 1, restrict_cond)
    faces(c_cond, *coarse, 2, 4.0, 0, ROWS // 2 - 3, 2)
    weights(*coarse, c_weight, 2, 2, 2, ROWS // 2 - 3, 2)

    def restrict_residual(c):
        r = 2 * c
        _, applied = operator(u0, *fine, 1, r, 2)
        res = source[pl.ds(r, 2)] - applied
        summed = pairs(res[0:1] + res[1:2])
        c_src[pl.ds(c, 1)] = summed
        c_u0[pl.ds(c, 1)] = c_weight[pl.ds(c, 1)] * summed

    over_rows(2, ROWS // 2 - 3, 1, restrict_residual)
    old, new = c_u0, c_u1
    for i in range(1, NUC):
        sweep(old, new, c_src, *coarse, c_weight, 2, 2 + i, ROWS // 2 - 3 - i, 2)
        old, new = new, old

    def prolong(c):
        u0[pl.ds(2 * c, 2)] = u0[pl.ds(2 * c, 2)] + old[pl.ds(c, 1)]

    over_rows(5, ROWS // 2 - 6, 1, prolong)
    sweep(u0, u1, source, *fine, weight, 1, 12, ROWS - 13, 2)
    sweep(u1, u0, source, *fine, weight, 1, 13, ROWS - 14, 2)

    def finish(r):
        own, applied = operator(u0, *fine, 1, r, 2)
        res = source[pl.ds(r, 2)] - applied
        for i in range(2):
            head_out[pl.ds(r + i - HY, NZ, stride=CY), :] = own[i, :, 0:CX]
            residual_out[pl.ds(r + i - HY, NZ, stride=CY), :] = res[i, :, 0:CX]

    over_rows(HY, HY + CY - 1, 2, finish)


VMEM = pl.BlockSpec(memory_space=pltpu.VMEM)
SMEM = pl.BlockSpec(memory_space=pltpu.SMEM)


def call(kernel, ins, outs, scratch=(), flops=1 << 20, nbytes=1 << 20):
    return pl.pallas_call(
        kernel,
        out_shape=tuple(jax.ShapeDtypeStruct(s, F32) for s in outs),
        in_specs=[SMEM if i else VMEM for i in ins],
        out_specs=tuple(VMEM for _ in outs),
        scratch_shapes=[pltpu.VMEM(s, F32) for s in scratch],
        cost_estimate=pl.CostEstimate(flops=flops, bytes_accessed=nbytes, transcendentals=0),
        compiler_params=pltpu.CompilerParams(vmem_limit_bytes=32 << 20),
    )


def forward(count):
    return [(i, i + 1) for i in range(count - 1)]


def backward(count):
    return [(i + 1, i) for i in range(count - 1)]


def body(head_start, class_map, class_cond, partials, send_count, recv_block):
    ngroups, ncols = lax.axis_size("rows"), lax.axis_size("cols")
    row, lanes = (CY, NZ, CX), (ROWS, NZ, LANES)
    payload = call(outgoing_kernel, (1, 0), [(ncols, SLOTS + 8, CX)])(
        send_count.reshape(ncols), partials.reshape(ncols, SLOTS, CX)
    )[0]
    incoming = lax.all_to_all(payload, "cols", split_axis=0, concat_axis=0, tiled=True)
    ids = recv_block.astype(F32).reshape(ncols * SLOTS // CX, CX)
    ids = jnp.pad(ids, ((0, 8 - ids.shape[0]), (0, 0)))
    head_t, cond_t, strip = call(fields_kernel, (1, 0, 0, 0), [row, row, (CY // 2 + 1, 8, CX)])(
        class_cond, head_start.reshape(NZ * CY, CX), class_map.reshape(NZ * CY, CX), ids
    )
    left = lax.ppermute(strip, "cols", forward(ncols))
    right = lax.ppermute(strip, "cols", backward(ncols))
    sent = (SENT, 8, CX)
    main, halo, up, down = call(recharge_kernel, (0,) * 6, [row, row, sent, sent])(
        incoming, ids, left, right, head_t, cond_t
    )
    top = lax.ppermute(down, "rows", forward(ngroups))
    bottom = lax.ppermute(up, "rows", backward(ngroups))
    place = jnp.stack([lax.axis_index("rows"), lax.axis_index("cols"), ngroups, ncols]).astype(jnp.int32)
    half = (ROWS // 2, NZ, LANES)
    head, residual = call(
        cycle_kernel, (1,) + (0,) * 8, [(NZ * CY, CX)] * 2, scratch=[lanes] * 8 + [half] * 8
    )(place, head_t, cond_t, main, halo, left, right, top, bottom)
    return head.reshape(NZ, CY, CX), residual.reshape(NZ, CY, CX)


def solution(mesh):
    placed = (
        P(None, "rows", "cols"),
        P(None, "rows", "cols"),
        P(),
        P("rows", "cols", None, None, None),
        P("rows", "cols", None),
        P("rows", "cols", None, None),
    )
    return jax.shard_map(
        body,
        mesh=mesh,
        in_specs=placed,
        out_specs=(P(None, "rows", "cols"), P(None, "rows", "cols")),
        check_vma=False,
    )
```

time: 244 us -> 89 us (0.36)
  the two profiles are of different devices: /device:TPU:447 before, /device:TPU:63 now
where the time goes in v1:
time: 89 us; the launch traced here: 88.6 us
  Pallas kernels  40 us (45%)
  starting transfers between devices  29.2 us (33%)
  waiting for transfers between devices  16.3 us (18%)
  local copies, waits for them, and re-layouts  2.34 us (3%)
    pallas_call x1, Pallas kernels, body(): call(cycle_kernel, (1,) + (0,) * 8, [(NZ * CY, CX)] * 2, scratch=[lanes]...  37.4 us
    all_to_all x1, starting transfers between devices, body(): lax.all_to_all(payload, 'cols', split_axis=0, concat_axis=0, tiled=True)  17.5 us
    ppermute x1, waiting for transfers between devices, body(): bottom = lax.ppermute(up, 'rows', backward(ngroups))  7.33 us
    ppermute x1, starting transfers between devices, body(): top = lax.ppermute(down, 'rows', forward(ngroups))  4.33 us
    ppermute x1, waiting for transfers between devices, body(): right = lax.ppermute(strip, 'cols', backward(ncols))  3.71 us
    ppermute x1, starting transfers between devices, body(): left = lax.ppermute(strip, 'cols', forward(ncols))  3.54 us
    ppermute x1, waiting for transfers between devices, body(): top = lax.ppermute(down, 'rows', forward(ngroups))  2.89 us
    unnamed x12, local copies, waits for them, and re-layouts  2.25 us
  transfers between devices with their start and end apart: 5, of which 5 were waited for; matrix products, arithmetic and copies ran while one was open for 0% of the time, Pallas kernels for 1%

profile of v1, /device:TPU:63, one launch (start us, length us, event | category | flops | bytes accessed | tf_op | source)
XLA Modules:
  0.0 88.6 jit_solution(15410855528711346971)
XLA Ops:
  0.6 0.0 copy-start.4
  0.6 0.6 copy-done.4
  1.3 0.0 copy-start
  1.3 0.9 %copy-done = f32[1,1,16,32,128]{4,3,2,1,0:T(8,128)S(1)} copy-done((f32[1,1,16,32,128]{4,3,2,1,0:T(8,128)S(1)}, f32[1,1,16,32,128]{4,3,2,1,0:T(8,128)}, u32[]{:S(2)}) %copy-start) | copy-done | bytes 262168
  2.2 1.4 %shard_map.78 = f32[16,40,128]{2,1,0:T(8,128)} custom-call(s32[16]{0:T(128)S(1)} %bitcast.13, f32[16,32,128]{2,1,0:T(8,128)S(1)} %bitcast.10), custom_call_target="tpu_custom_call" | custom-call | flops 1048576 | bytes 1048576 | tf_op jit(solution)/shard_map/pallas_call | solution.py:292
  3.6 0.0 copy-start.5
  3.6 0.0 copy-start.1
  3.6 0.0 copy-start.2
  3.6 17.5 %all-to-all-start = ((f32[16,40,128]{2,1,0:T(8,128)}), f32[16,40,128]{2,1,0:T(8,128)S(1)}, u32[]{:S(2)}, u32[]{:S(2)}) async-start(f32[16,40,128]{2,1,0:T(8,128)} %shard_map.78), calls=%async_computation | async-start | bytes 655360 | tf_op jit(solution)/shard_map/all_to_all | solution.py:295
  21.1 0.0 copy-done.5
  21.2 0.1 reshape.27
  21.2 0.0 copy-start.3
  21.3 0.0 copy-done.1
  21.3 0.0 copy-done.2
  21.3 0.6 copy-done.3
  21.9 0.8 shard_map.77
  22.7 3.5 %collective-permute-start = (f32[17,8,128]{2,1,0:T(8,128)S(1)}, f32[17,8,128]{2,1,0:T(8,128)S(1)}, u32[]{:S(2)}, u32[]{:S(2)}) collective-permute-start(f32[17,8,128]{2,1,0:T(8,128)S(1)} %get-tuple-element.13), channel_id=1, source_target_pairs={{0,1},{1,2},{2,3},{3,4},{4,5},{5,6},{6,7},{7,8},{8,9},{9,10},{10,1... | collective-permute-start | bytes 208904 | tf_op jit(solution)/shard_map/ppermute | solution.py:301
  26.2 1.9 %collective-permute-start.1 = (f32[17,8,128]{2,1,0:T(8,128)S(1)}, f32[17,8,128]{2,1,0:T(8,128)S(1)}, u32[]{:S(2)}, u32[]{:S(2)}) collective-permute-start(f32[17,8,128]{2,1,0:T(8,128)S(1)} %get-tuple-element.13), channel_id=1, source_target_pairs={{1,0},{2,1},{3,2},{4,3},{5,4},{6,5},{7,6},{8,7},{9,8},{10,9},{11,1... | collective-permute-start | bytes 208904 | tf_op jit(solution)/shard_map/ppermute | solution.py:302
  28.2 0.3 collective-permute-done.left_ref
  28.4 3.7 %collective-permute-done.1.right_ref = f32[17,8,128]{2,1,0:T(8,128)S(1)} collective-permute-done((f32[17,8,128]{2,1,0:T(8,128)S(1)}, f32[17,8,128]{2,1,0:T(8,128)S(1)}, u32[]{:S(2)}, u32[]{:S(2)}) %collective-permute-start.1) | collective-permute-done | bytes 69664 | tf_op jit(solution)/shard_map/ppermute | solution.py:302
  32.2 2.1 %all-to-all-done.incoming_ref = f32[16,40,128]{2,1,0:T(8,128)S(1)} async-done(((f32[16,40,128]{2,1,0:T(8,128)}), f32[16,40,128]{2,1,0:T(8,128)S(1)}, u32[]{:S(2)}, u32[]{:S(2)}) %all-to-all-start) | async-done | bytes 327712 | tf_op jit(solution)/shard_map/all_to_all | solution.py:295
  34.2 0.4 shard_map.79
  34.7 4.3 %collective-permute-start.2 = (f32[51,8,128]{2,1,0:T(8,128)S(1)}, f32[51,8,128]{2,1,0:T(8,128)S(1)}, u32[]{:S(2)}, u32[]{:S(2)}) collective-permute-start(f32[51,8,128]{2,1,0:T(8,128)S(1)} %get-tuple-element.16), channel_id=1, source_target_pairs={{0,16},{16,32},{32,48},{48,64},{64,80},{80,96},{96,112},{112,128},... | collective-permute-start | bytes 626696 | tf_op jit(solution)/shard_map/ppermute | solution.py:307
  39.0 1.9 %collective-permute-start.3 = (f32[51,8,128]{2,1,0:T(8,128)S(1)}, f32[51,8,128]{2,1,0:T(8,128)S(1)}, u32[]{:S(2)}, u32[]{:S(2)}) collective-permute-start(f32[51,8,128]{2,1,0:T(8,128)S(1)} %get-tuple-element.17), channel_id=1, source_target_pairs={{16,0},{32,16},{48,32},{64,48},{80,64},{96,80},{112,96},{128,112},... | collective-permute-start | bytes 626696 | tf_op jit(solution)/shard_map/ppermute | solution.py:308
  40.9 0.1 pad_add_fusion.place_ref
  41.0 2.9 %collective-permute-done.2.top_ref = f32[51,8,128]{2,1,0:T(8,128)S(1)} collective-permute-done((f32[51,8,128]{2,1,0:T(8,128)S(1)}, f32[51,8,128]{2,1,0:T(8,128)S(1)}, u32[]{:S(2)}, u32[]{:S(2)}) %collective-permute-start.2) | collective-permute-done | bytes 208928 | tf_op jit(solution)/shard_map/ppermute | solution.py:307
  43.9 7.3 %collective-permute-done.3.bottom_ref = f32[51,8,128]{2,1,0:T(8,128)S(1)} collective-permute-done((f32[51,8,128]{2,1,0:T(8,128)S(1)}, f32[51,8,128]{2,1,0:T(8,128)S(1)}, u32[]{:S(2)}, u32[]{:S(2)}) %collective-permute-start.3) | collective-permute-done | bytes 208928 | tf_op jit(solution)/shard_map/ppermute | solution.py:308
  51.2 37.4 %shard_map.80 = (f32[256,128]{1,0:T(8,128)}, f32[256,128]{1,0:T(8,128)}) custom-call(s32[4]{0:T(128)S(1)} %pad_add_fusion.place_ref, f32[32,8,128]{2,1,0:T(8,128)S(1)} %get-tuple-element.11.head_ref, f32[32,8,128]{2,1,0:T(8,128)S(1)} %get-tuple-element.12.cond_ref, f32[32,8,128]{2,1,0:T(8,128)S(1)} %get-tuple-element.14.main_ref, ...), custom_call_target="tpu_custom_call" | custom-call | flops 1048576 | bytes 1048576 | tf_op jit(solution)/shard_map/pallas_call | solution.py:311
  (2 shorter events, 0.0 us)
Async XLA Ops:
  0.6 0.7 copy-start.4
  1.3 0.9 %copy-start = (f32[1,1,16,32,128]{4,3,2,1,0:T(8,128)S(1)}, f32[1,1,16,32,128]{4,3,2,1,0:T(8,128)}, u32[]{:S(2)}) copy-start(f32[1,1,16,32,128]{4,3,2,1,0:T(8,128)} %param.9) | copy-start | bytes 786436
  3.6 17.5 %copy-start.5 = (s32[1,1,16,32]{3,2,1,0:T(8,128)S(1)}, s32[1,1,16,32]{3,2,1,0:T(8,128)}, u32[]{:S(2)}) copy-start(s32[1,1,16,32]{3,2,1,0:T(8,128)} %param.11) | copy-start | bytes 6148
  3.6 17.6 %copy-start.1 = (f32[8,32,128]{2,1,0:T(8,128)S(1)}, f32[8,32,128]{2,1,0:T(8,128)}, u32[]{:S(2)}) copy-start(f32[8,32,128]{2,1,0:T(8,128)} %param.6) | copy-start | bytes 393220
  3.6 17.6 %copy-start.2 = (s32[8,32,128]{2,1,0:T(8,128)S(1)}, s32[8,32,128]{2,1,0:T(8,128)}, u32[]{:S(2)}) copy-start(s32[8,32,128]{2,1,0:T(8,128)} %param.7) | copy-start | bytes 393220
  3.6 30.6 %all-to-all-start = ((f32[16,40,128]{2,1,0:T(8,128)}), f32[16,40,128]{2,1,0:T(8,128)S(1)}, u32[]{:S(2)}, u32[]{:S(2)}) async-start(f32[16,40,128]{2,1,0:T(8,128)} %shard_map.78), calls=%async_computation | async-start | bytes 655360 | tf_op jit(solution)/shard_map/all_to_all | solution.py:295
  21.2 0.7 copy-start.3
  22.7 5.8 %collective-permute-start = (f32[17,8,128]{2,1,0:T(8,128)S(1)}, f32[17,8,128]{2,1,0:T(8,128)S(1)}, u32[]{:S(2)}, u32[]{:S(2)}) collective-permute-start(f32[17,8,128]{2,1,0:T(8,128)S(1)} %get-tuple-element.13), channel_id=1, source_target_pairs={{0,1},{1,2},{2,3},{3,4},{4,5},{5,6},{6,7},{7,8},{8,9},{9,10},{10,1... | collective-permute-start | bytes 208904 | tf_op jit(solution)/shard_map/ppermute | solution.py:301
  26.2 5.9 %collective-permute-start.1 = (f32[17,8,128]{2,1,0:T(8,128)S(1)}, f32[17,8,128]{2,1,0:T(8,128)S(1)}, u32[]{:S(2)}, u32[]{:S(2)}) collective-permute-start(f32[17,8,128]{2,1,0:T(8,128)S(1)} %get-tuple-element.13), channel_id=1, source_target_pairs={{1,0},{2,1},{3,2},{4,3},{5,4},{6,5},{7,6},{8,7},{9,8},{10,9},{11,1... | collective-permute-start | bytes 208904 | tf_op jit(solution)/shard_map/ppermute | solution.py:302
  34.7 9.2 %collective-permute-start.2 = (f32[51,8,128]{2,1,0:T(8,128)S(1)}, f32[51,8,128]{2,1,0:T(8,128)S(1)}, u32[]{:S(2)}, u32[]{:S(2)}) collective-permute-start(f32[51,8,128]{2,1,0:T(8,128)S(1)} %get-tuple-element.16), channel_id=1, source_target_pairs={{0,16},{16,32},{32,48},{48,64},{64,80},{80,96},{96,112},{112,128},... | collective-permute-start | bytes 626696 | tf_op jit(solution)/shard_map/ppermute | solution.py:307
  39.0 12.2 %collective-permute-start.3 = (f32[51,8,128]{2,1,0:T(8,128)S(1)}, f32[51,8,128]{2,1,0:T(8,128)S(1)}, u32[]{:S(2)}, u32[]{:S(2)}) collective-permute-start(f32[51,8,128]{2,1,0:T(8,128)S(1)} %get-tuple-element.17), channel_id=1, source_target_pairs={{16,0},{32,16},{48,32},{64,48},{80,64},{96,80},{112,96},{128,112},... | collective-permute-start | bytes 626696 | tf_op jit(solution)/shard_map/ppermute | solution.py:308

commit v2 on v1

v2 whole, which is shorter than its diff:
```python
import jax
import jax.numpy as jnp
from jax import lax
from jax.experimental import pallas as pl
from jax.experimental.pallas import tpu as pltpu
from jax.sharding import PartitionSpec as P

NZ, CY, CX, SLOTS = 8, 32, 128, 32
OMEGA = 0.8
NU1, NU2, NUC = 2, 2, 4
HY, HX = 14, 16
RY = 12
ROWS = CY + 2 * HY
LANES = 2 * CX
F32 = jnp.float32


def lane_of(shape):
    return lax.broadcasted_iota(jnp.int32, shape, len(shape) - 1)


def packed(rows, lane):
    out = None
    for q, row in enumerate(rows):
        turned = pltpu.roll(row, 32 * q + 16, 1)
        out = turned if q == 0 else jnp.where(lane // 32 == q, turned, out)
    return out


def unpacked(block, q, lane):
    turned = pltpu.roll(block, (CX - 32 * q - 16) % CX, 1)
    return jnp.where((lane < HX) | (lane >= CX - HX), turned, 0.0)


def outgoing_kernel(count_hbm, partials_hbm, out_hbm, count_ref, partials_ref, out_ref, count_sem, in_sems, out_sems):
    ncols = partials_ref.shape[0]
    part = ncols // 4
    counts = pltpu.make_async_copy(count_hbm, count_ref, count_sem)
    counts.start()
    arriving = []
    for c in range(4):
        piece = pl.ds(c * part, part)
        arriving.append(pltpu.make_async_copy(partials_hbm.at[piece], partials_ref.at[piece], in_sems.at[c]))
        arriving[c].start()
    counts.wait()
    lane = lane_of((8, CX))
    slot = lax.broadcasted_iota(jnp.int32, (8, CX), 0)
    zero = jnp.zeros((8, CX), F32)
    strips, leaving, sent = [zero], [], 0
    for d in range(ncols):
        if d % part == 0:
            arriving[d // part].wait()
        rows = []
        for q in range(SLOTS // 8):
            row = jnp.where(slot + 8 * q < count_ref[d], partials_ref[d, 8 * q : 8 * q + 8, :], 0.0)
            out_ref[d, 8 * q : 8 * q + 8, :] = row
            rows.append(row)
        strips.append(packed(rows, lane))
        if d == ncols - 1:
            strips.append(zero)
        ready = d + 1 if d == ncols - 1 else d
        for i in range(max(0, d - 1), ready):
            out_ref[i, SLOTS : SLOTS + 8, :] = jnp.where(lane % 32 < HX, strips[i], strips[i + 2])
        if d % part == part - 1:
            piece = pl.ds(sent, ready - sent)
            leaving.append(pltpu.make_async_copy(out_ref.at[piece], out_hbm.at[piece], out_sems.at[d // part]))
            leaving[-1].start()
            sent = ready
    for copy in leaving:
        copy.wait()


def fields_kernel(class_cond_ref, head_ref, class_ref, ids_ref, head_out, cond_out, strip_out):
    lane = lane_of((8, CX))
    values = [class_cond_ref[c] for c in range(8)]
    for block in range(CY // 4):
        heads, conds = [], []
        for q in range(4):
            y = 4 * block + q
            head = head_ref[pl.ds(y, NZ, stride=CY), :]
            kind = class_ref[pl.ds(y, NZ, stride=CY), :]
            cond = jnp.full((8, CX), values[0], F32)
            for c in range(1, 8):
                cond = jnp.where(kind == c, values[c], cond)
            head_out[y] = head
            cond_out[y] = cond
            heads.append(head)
            conds.append(cond)
        strip_out[block] = packed(heads, lane)
        strip_out[CY // 4 + block] = packed(conds, lane)
    strip_out[CY // 2] = ids_ref[...]


def recharge_kernel(incoming_ref, ids_ref, left_ref, right_ref, head_ref, cond_ref, main_out, halo_out, up_out, down_out):
    ncols = incoming_ref.shape[0]
    total = ncols * SLOTS
    chunk = min(256, total)
    senders = chunk // SLOTS
    lane = lane_of((8, CX))
    row = lax.broadcasted_iota(jnp.int32, (NZ * CY, chunk), 0)
    block_of = ((row % NZ) * CY + row // NZ).astype(F32)

    def onehot(ids, m):
        flat = jnp.concatenate([ids[r : r + 1, :] for r in range(m * chunk // CX, (m + 1) * chunk // CX)], axis=1)
        return jnp.where(block_of == flat, 1.0, 0.0).astype(jnp.bfloat16)

    def halves(values):
        high = values.astype(jnp.bfloat16)
        low = (values - high.astype(F32)).astype(jnp.bfloat16)
        return jnp.concatenate([high, low], axis=1)

    own, left, right = ids_ref[...], left_ref[CY // 2], right_ref[CY // 2]
    main = jnp.zeros((NZ * CY, LANES), F32)
    from_left = jnp.zeros((NZ * CY, LANES), F32)
    from_right = jnp.zeros((NZ * CY, LANES), F32)
    for m in range(total // chunk):
        values = incoming_ref[m * senders : (m + 1) * senders, 0:SLOTS, :].reshape(chunk, CX)
        main = main + jnp.dot(onehot(own, m), halves(values), preferred_element_type=F32)
        strips = []
        for s in range(m * senders, (m + 1) * senders):
            strip = incoming_ref[s, SLOTS : SLOTS + 8, :]
            strips += [pltpu.roll(strip, (CX - 32 * q - 16) % CX, 1) for q in range(4)]
        edges = halves(jnp.concatenate(strips, axis=0))
        from_left = from_left + jnp.dot(onehot(left, m), edges, preferred_element_type=F32)
        from_right = from_right + jnp.dot(onehot(right, m), edges, preferred_element_type=F32)
    main = (main[:, :CX] + main[:, CX:]).reshape(CY, NZ, CX)
    from_left = (from_left[:, :CX] + from_left[:, CX:]).reshape(CY, NZ, CX)
    from_right = (from_right[:, :CX] + from_right[:, CX:]).reshape(CY, NZ, CX)
    wide = lane_of((CY, NZ, CX))
    halo = jnp.where(wide >= CX - HX, from_left, jnp.where(wide < HX, from_right, 0.0))
    main_out[...] = main
    halo_out[...] = halo
    for out, first, strip0 in ((up_out, 0, 0), (down_out, CY - HY, CY // 4 - 4)):
        skip = first and HY - RY
        out[0:HY] = head_ref[first : first + HY]
        out[HY : 2 * HY] = cond_ref[first : first + HY]
        out[2 * HY : 2 * HY + RY] = main[first + skip : first + skip + RY]
        base = 2 * HY + RY
        for i in range(4):
            for f in range(2):
                at = f * (CY // 4) + strip0 + i
                out[base + 4 * f + i] = jnp.where(lane % 32 < HX, left_ref[at], right_ref[at])
        for i in range(RY // 4):
            y = first + skip + 4 * i
            out[base + 8 + i] = packed([halo[y + q] for q in range(4)], lane)


SENT = 2 * HY + RY + 8 + RY // 4


def span(first, last):
    return list(range(first, last + 1))


NEEDED = {
    "u0": (span(1, 58), span(14, 45)),
    "half": (span(1, 58), span(14, 45)),
    "source": (span(2, 57), span(14, 45)),
    "fx": (span(2, 57), span(14, 45)),
    "fy": (span(1, 57), span(14, 44)),
    "fz": (span(2, 57), span(14, 45)),
    "weight": (span(2, 57), span(15, 44)),
    "u1": (span(2, 57), span(15, 44)),
    "u2": (span(3, 56), span(16, 43)),
    "c_half": (span(1, 28), span(7, 22)),
    "c_fx": (span(2, 27), span(7, 22)),
    "c_fy": (span(1, 27), span(7, 21)),
    "c_fz": (span(2, 27), span(7, 22)),
    "c_weight": (span(2, 27), span(8, 21)),
    "c_source": (span(2, 27), span(9, 20)),
    "c_u0": (span(2, 27), span(9, 20)),
    "c_u1": (span(3, 26), span(10, 19)),
    "c_u2": (span(4, 25), span(11, 18)),
    "c_u3": (span(5, 24), span(12, 17)),
    "u3": (span(11, 48), span(24, 35)),
    "u4": (span(12, 47), span(25, 34)),
    "u5": (span(13, 46), span(26, 33)),
    "residual": (span(14, 45), span(27, 32)),
}
EARLY, LATE = {}, {}
for _name, (_every, _own) in NEEDED.items():
    for _r in _every:
        _into = EARLY if _r in _own else LATE
        _into[_name, _r] = len(_into)


class Cycle:
    def __init__(self, place_ref, early, late=None):
        self.early, self.late = early, late
        self.lane = lane_of((1, NZ, LANES))
        layer = lax.broadcasted_iota(jnp.int32, (1, NZ, LANES), 1)
        self.below = jnp.where(layer < NZ - 1, 1.0, 0.0)
        self.even = self.lane % 2 == 0
        g, d, ngroups, ncols = place_ref[0], place_ref[1], place_ref[2], place_ref[3]
        right = jnp.where(d < ncols - 1, CX + HX, CX)
        left = jnp.where(d > 0, LANES - HX, LANES)
        columns = jnp.where((self.lane < right) | (self.lane >= left), OMEGA, 0.0)
        above, under = jnp.where(g > 0, 1.0, 0.0), jnp.where(g < ngroups - 1, 1.0, 0.0)
        self.inside = (columns * above, columns, columns * under)

    def ranges(self, name):
        every, own = NEEDED[name]
        if self.late is None:
            return [(own[0], len(own), 1)]
        return [(every[0], own[0] - every[0], 0), (own[-1] + 1, every[-1] - own[-1], 2)]

    def get(self, name, r, n):
        parts, at = [], r
        while at < r + n:
            ref, rows = (self.early, EARLY) if (name, at) in EARLY else (self.late, LATE)
            many = 1
            while at + many < r + n and rows.get((name, at + many)) == rows[name, at] + many:
                many += 1
            parts.append(ref[pl.ds(rows[name, at], many)])
            at += many
        return parts[0] if len(parts) == 1 else jnp.concatenate(parts, axis=0)

    def put(self, name, r, n, value):
        if self.late is None:
            self.early[pl.ds(EARLY[name, r], n)] = value
        else:
            self.late[pl.ds(LATE[name, r], n)] = value

    def put_parts(self, name, r, main, halo):
        ref, at = (self.early, EARLY[name, r]) if self.late is None else (self.late, LATE[name, r])
        ref[at, :, 0:CX] = main
        ref[at, :, CX:LANES] = halo

    def turn(self, x, by):
        return pltpu.roll(x, by % LANES, 2)

    def turn_z(self, x, by):
        return pltpu.roll(x, by % NZ, 1)

    def pairs(self, x):
        two = x.reshape(x.shape[0] // 2, 2, NZ, LANES)
        two = two[:, 0] + two[:, 1]
        return two + jnp.where(self.even, self.turn(two, -1), self.turn(two, 1))

    def coefficients(self, mark, shift, zweight, own):
        for r, n, _ in self.ranges(mark + "fx"):
            k = self.get(mark + "half", r, n)
            self.put(mark + "fx", r, n, k + self.turn(k, -shift))
            self.put(mark + "fz", r, n, (k + self.turn_z(k, -1)) * (zweight * self.below))
        for r, n, _ in self.ranges(mark + "fy"):
            k = self.get(mark + "half", r, n + 1)
            self.put(mark + "fy", r, n, k[:-1] + k[1:])
        for r, n, part in self.ranges(mark + "weight"):
            pieces = [(r, n, part)]
            if part == 0:
                pieces = [(r, own[0] - r, 0), (own[0], r + n - own[0], 1)]
            elif part == 2:
                pieces = [(r, own[1] + 1 - r, 1), (own[1] + 1, r + n - own[1] - 1, 2)]
            for at, many, which in pieces:
                x, z = self.get(mark + "fx", at, many), self.get(mark + "fz", at, many)
                y = self.get(mark + "fy", at - 1, many + 1)
                total = (x + self.turn(x, shift)) + (y[1:] + y[:-1]) + (z + self.turn_z(z, 1))
                scale = self.inside[which]
                self.put(mark + "weight", at, many, scale / jnp.where(scale > 0.0, total, 1.0))

    def operator(self, u, mark, shift, r, n):
        v = self.get(u, r - 1, n + 2)
        own = v[1:-1]
        x = self.get(mark + "fx", r, n) * (own - self.turn(own, -shift))
        y = self.get(mark + "fy", r - 1, n + 1) * (v[:-1] - v[1:])
        z = self.get(mark + "fz", r, n) * (self.turn_z(own, -1) - own)
        return own, (x - self.turn(x, shift)) + (y[1:] - y[:-1]) + (z - self.turn_z(z, 1))

    def sweep(self, old, new, mark, shift):
        for r, n, _ in self.ranges(new):
            own, applied = self.operator(old, mark, shift, r, n)
            left = self.get(mark + "source", r, n) - applied
            self.put(new, r, n, own + self.get(mark + "weight", r, n) * left)

    def run(self, done):
        self.coefficients("", 1, 1.0, (HY, HY + CY - 1))
        self.sweep("u0", "u1", "", 1)
        self.sweep("u1", "u2", "", 1)
        for c, n, _ in self.ranges("c_half"):
            self.put("c_half", c, n, 0.25 * self.pairs(self.get("half", 2 * c, 2 * n)))
        self.coefficients("c_", 2, 4.0, (HY // 2, HY // 2 + CY // 2 - 1))
        for c, n, _ in self.ranges("c_source"):
            _, applied = self.operator("u2", "", 1, 2 * c, 2 * n)
            summed = self.pairs(self.get("source", 2 * c, 2 * n) - applied)
            self.put("c_source", c, n, summed)
            self.put("c_u0", c, n, self.get("c_weight", c, n) * summed)
        for i in range(1, NUC):
            self.sweep("c_u%d" % (i - 1), "c_u%d" % i, "c_", 2)
        for r, n, _ in self.ranges("u3"):
            c, many = r // 2, (r + n - 1) // 2 - r // 2 + 1
            added = self.get("c_u%d" % (NUC - 1), c, many)
            added = jnp.broadcast_to(added[:, None], (many, 2, NZ, LANES)).reshape(2 * many, NZ, LANES)
            self.put("u3", r, n, self.get("u2", r, n) + added[r % 2 : r % 2 + n])
        self.sweep("u3", "u4", "", 1)
        self.sweep("u4", "u5", "", 1)
        done()
        for r, n, _ in self.ranges("residual"):
            _, applied = self.operator("u5", "", 1, r, n)
            self.put("residual", r, n, self.get("source", r, n) - applied)


def early_kernel(place_ref, head_ref, cond_ref, main_ref, halo_ref, left_ref, right_ref, early):
    cycle = Cycle(place_ref, early)
    lane = lane_of((8, CX))
    for i in range(CY // 4):
        at = CY // 4 + i
        heads = jnp.where(lane % 32 < HX, left_ref[i], right_ref[i])
        conds = 0.5 * jnp.where(lane % 32 < HX, left_ref[at], right_ref[at])
        for q in range(4):
            y = 4 * i + q
            cycle.put_parts("u0", HY + y, head_ref[y], unpacked(heads, q, lane))
            cycle.put_parts("half", HY + y, 0.5 * cond_ref[y], unpacked(conds, q, lane))
            cycle.put_parts("source", HY + y, main_ref[y], halo_ref[y])
    cycle.run(lambda: None)


def late_kernel(place_ref, top_ref, bottom_ref, early, head_hbm, residual_hbm, late, head_ref, residual_ref, sems):
    cycle = Cycle(place_ref, early, late)
    lane = lane_of((8, CX))
    base = 2 * HY + RY
    for ref, first, shift, skip in ((top_ref, 0, 2, HY - RY), (bottom_ref, HY + CY, 0, 0)):
        for i in range(HY):
            at, q = (i + shift) // 4, (i + shift) % 4
            if first + i in NEEDED["u0"][0]:
                cycle.put_parts("u0", first + i, ref[i], unpacked(ref[base + at], q, lane))
                half = 0.5 * ref[HY + i]
                cycle.put_parts("half", first + i, half, 0.5 * unpacked(ref[base + 4 + at], q, lane))
        for i in range(RY):
            edge = unpacked(ref[base + 8 + i // 4], i % 4, lane)
            cycle.put_parts("source", first + skip + i, ref[2 * HY + i], edge)
    copies = [
        pltpu.make_async_copy(head_ref, head_hbm, sems.at[0]),
        pltpu.make_async_copy(residual_ref, residual_hbm, sems.at[1]),
    ]

    def head_done():
        for y in range(CY):
            head_ref[pl.ds(y, NZ, stride=CY), :] = cycle.get("u5", HY + y, 1)[0, :, 0:CX]
        copies[0].start()

    cycle.run(head_done)
    for y in range(CY):
        residual_ref[pl.ds(y, NZ, stride=CY), :] = cycle.get("residual", HY + y, 1)[0, :, 0:CX]
    copies[1].start()
    for copy in copies:
        copy.wait()


VMEM = pl.BlockSpec(memory_space=pltpu.VMEM)
SMEM = pl.BlockSpec(memory_space=pltpu.SMEM)
HBM = pl.BlockSpec(memory_space=pltpu.HBM)


def call(kernel, ins, outs, scratch=(), out=VMEM, limit=32 << 20, flops=1 << 20, nbytes=1 << 20):
    return pl.pallas_call(
        kernel,
        out_shape=tuple(jax.ShapeDtypeStruct(s, F32) for s in outs),
        in_specs=ins,
        out_specs=tuple(out for _ in outs),
        scratch_shapes=scratch,
        cost_estimate=pl.CostEstimate(flops=flops, bytes_accessed=nbytes, transcendentals=0),
        compiler_params=pltpu.CompilerParams(vmem_limit_bytes=limit),
    )


def forward(count):
    return [(i, i + 1) for i in range(count - 1)]


def backward(count):
    return [(i + 1, i) for i in range(count - 1)]


def early_call(place, head, cond, main, halo, left, right):
    return call(early_kernel, [SMEM] + [VMEM] * 6, [(len(EARLY), NZ, LANES)])(
        place, head, cond, main, halo, left, right
    )[0]


def late_call(place, top, bottom, early):
    flat = (NZ * CY, CX)
    scratch = [pltpu.VMEM((len(LATE), NZ, LANES), F32)] + [pltpu.VMEM(flat, F32)] * 2 + [pltpu.SemaphoreType.DMA((2,))]
    return call(late_kernel, [SMEM] + [VMEM] * 3, [flat] * 2, scratch, HBM)(place, top, bottom, early)


def body(head_start, class_map, class_cond, partials, send_count, recv_block):
    ngroups, ncols = lax.axis_size("rows"), lax.axis_size("cols")
    row, sent = (CY, NZ, CX), (SENT, 8, CX)
    scratch = [
        pltpu.SMEM((ncols,), jnp.int32),
        pltpu.VMEM((ncols, SLOTS, CX), F32),
        pltpu.VMEM((ncols, SLOTS + 8, CX), F32),
        pltpu.SemaphoreType.DMA,
        pltpu.SemaphoreType.DMA((4,)),
        pltpu.SemaphoreType.DMA((4,)),
    ]
    payload = call(outgoing_kernel, [HBM, HBM], [(ncols, SLOTS + 8, CX)], scratch, HBM, limit=64 << 20)(
        send_count.reshape(ncols), partials.reshape(ncols, SLOTS, CX)
    )[0]
    incoming = lax.all_to_all(payload, "cols", split_axis=0, concat_axis=0, tiled=True)
    ids = recv_block.astype(F32).reshape(ncols * SLOTS // CX, CX)
    ids = jnp.pad(ids, ((0, 8 - ids.shape[0]), (0, 0)))
    head, cond, strip = call(fields_kernel, [SMEM] + [VMEM] * 3, [row, row, (CY // 2 + 1, 8, CX)])(
        class_cond, head_start.reshape(NZ * CY, CX), class_map.reshape(NZ * CY, CX), ids
    )
    left = lax.ppermute(strip, "cols", forward(ncols))
    right = lax.ppermute(strip, "cols", backward(ncols))
    main, halo, up, down = call(recharge_kernel, [VMEM] * 6, [row, row, sent, sent])(
        incoming, ids, left, right, head, cond
    )
    top = lax.ppermute(down, "rows", forward(ngroups))
    bottom = lax.ppermute(up, "rows", backward(ngroups))
    place = jnp.stack([lax.axis_index("rows"), lax.axis_index("cols"), ngroups, ncols]).astype(jnp.int32)
    early = early_call(place, head, cond, main, halo, left, right)
    out = late_call(place, top, bottom, early)
    return tuple(o.reshape(NZ, CY, CX) for o in out)


def solution(mesh):
    placed = (
        P(None, "rows", "cols"),
        P(None, "rows", "cols"),
        P(),
        P("rows", "cols", None, None, None),
        P("rows", "cols", None),
        P("rows", "cols", None, None),
    )
    return jax.shard_map(
        body,
        mesh=mesh,
        in_specs=placed,
        out_specs=(P(None, "rows", "cols"), P(None, "rows", "cols")),
        check_vma=False,
    )
```

time: 89 us -> 54.5 us (0.61)
  Pallas kernels: 40 us -> 9.66 us
  waiting for transfers between devices: 16.3 us -> 11.2 us
    pallas_call x4 -> x5, Pallas kernels: 40 us -> 9.66 us  [the longest x1 4.07 us: late_call(): call(late_kernel, [SMEM] + [VMEM] * 3, [flat] * 2, scratch, HBM)]
    ppermute x1, waiting for transfers between devices: 3.71 us -> 0.99 us  [body(): right = lax.ppermute(strip, 'cols', backward(ncols))]
    ppermute x1, waiting for transfers between devices: 2.89 us -> 0.43 us  [body(): top = lax.ppermute(down, 'rows', forward(ngroups))]
    unnamed x12 -> x6, local copies, waits for them, and re-layouts: 2.25 us -> 2.46 us
  transfers between devices with their start and end apart: 5 -> 5, of which waited for: 5 -> 5; matrix products, arithmetic and copies ran while one was open for 0% -> 2% of each run, Pallas kernels for 1% -> 6%
where the time goes in v2:
time: 54.5 us; the launch traced here: 54.1 us
  starting transfers between devices  29.2 us (54%)
  waiting for transfers between devices  11.2 us (21%)
  Pallas kernels  9.66 us (18%)
  local copies, waits for them, and re-layouts  2.55 us (5%)
  other arithmetic  0.78 us (1%)
  between operations  0.7 us (1%)
    all_to_all x1, starting transfers between devices, body(): lax.all_to_all(payload, 'cols', split_axis=0, concat_axis=0, tiled=True)  17.4 us
    ppermute x1, waiting for transfers between devices, body(): bottom = lax.ppermute(up, 'rows', backward(ngroups))  7.33 us
    ppermute x1, starting transfers between devices, body(): top = lax.ppermute(down, 'rows', forward(ngroups))  4.33 us
    pallas_call x1, Pallas kernels, late_call(): call(late_kernel, [SMEM] + [VMEM] * 3, [flat] * 2, scratch, HBM)  4.07 us
    ppermute x1, starting transfers between devices, body(): left = lax.ppermute(strip, 'cols', forward(ncols))  3.55 us
    unnamed x6, local copies, waits for them, and re-layouts  2.46 us
    pallas_call x1, Pallas kernels, early_call(): call(early_kernel, [SMEM] + [VMEM] * 6, [(len(EARLY), NZ, LANES)])  2.45 us
    all_to_all x1, waiting for transfers between devices, body(): lax.all_to_all(payload, 'cols', split_axis=0, concat_axis=0, tiled=True)  2.11 us
  transfers between devices with their start and end apart: 5, of which 5 were waited for; matrix products, arithmetic and copies ran while one was open for 2% of the time, Pallas kernels for 6%

profile of v2, /device:TPU:63, one launch (start us, length us, event | category | flops | bytes accessed | tf_op | source)
XLA Modules:
  0.0 54.1 jit_solution(6526730003613664860)
XLA Ops:
  0.6 1.9 %shard_map.77 = f32[16,40,128]{2,1,0:T(8,128)} custom-call(s32[16]{0:T(128)} %bitcast.13, f32[16,32,128]{2,1,0:T(8,128)} %bitcast.12), custom_call_target="tpu_custom_call" | custom-call | flops 1048576 | bytes 1048576 | tf_op jit(solution)/shard_map/pallas_call | solution.py:397
  2.5 17.4 %all-to-all-start = ((f32[16,40,128]{2,1,0:T(8,128)}), f32[16,40,128]{2,1,0:T(8,128)S(1)}, u32[]{:S(2)}, u32[]{:S(2)}) async-start(f32[16,40,128]{2,1,0:T(8,128)} %shard_map.77), calls=%async_computation | async-start | bytes 655360 | tf_op jit(solution)/shard_map/all_to_all | solution.py:400
  19.9 0.7 %convert_element_type.5 = f32[1,1,16,32]{3,2,1,0:T(8,128)S(1)} convert(s32[1,1,16,32]{3,2,1,0:T(8,128)} %param.11) | non-fusion elementwise | flops 512 | bytes 4096 | tf_op jit(solution)/shard_map/convert_element_type | solution.py:401
  20.6 0.1 reshape.27
  20.7 0.0 copy-start
  20.7 0.9 %copy-done = f32[8,32,128]{2,1,0:T(8,128)S(1)} copy-done((f32[8,32,128]{2,1,0:T(8,128)S(1)}, f32[8,32,128]{2,1,0:T(8,128)}, u32[]{:S(2)}) %copy-start) | copy-done | bytes 131096
  21.6 0.0 copy-start.1
  21.6 0.9 %copy-done.1 = s32[8,32,128]{2,1,0:T(8,128)S(1)} copy-done((s32[8,32,128]{2,1,0:T(8,128)S(1)}, s32[8,32,128]{2,1,0:T(8,128)}, u32[]{:S(2)}) %copy-start.1) | copy-done | bytes 131096
  22.5 0.0 copy-start.2
  22.5 0.7 %copy-done.2 = f32[8]{0:T(128)S(1)} copy-done((f32[8]{0:T(128)S(1)}, f32[8]{0:T(128)}, u32[]{:S(2)}) %copy-start.2) | copy-done | bytes 56
  23.2 0.8 %shard_map.78 = (f32[32,8,128]{2,1,0:T(8,128)S(1)}, f32[32,8,128]{2,1,0:T(8,128)S(1)}, f32[17,8,128]{2,1,0:T(8,128)S(1)}) custom-call(f32[8]{0:T(128)S(1)} %copy-done.2, f32[256,128]{1,0:T(8,128)S(1)} %bitcast.10, s32[256,128]{1,0:T(8,128)S(1)} %bitcast.11, f32[8,128]{1,0:T(8,128)S(1)} %pad.4.ids_ref), custom_call_target="tpu_custom_call" | custom-call | flops 1048576 | bytes 1048576 | tf_op jit(solution)/shard_map/pallas_call | solution.py:403
  24.0 2.0 %collective-permute-start.1 = (f32[17,8,128]{2,1,0:T(8,128)S(1)}, f32[17,8,128]{2,1,0:T(8,128)S(1)}, u32[]{:S(2)}, u32[]{:S(2)}) collective-permute-start(f32[17,8,128]{2,1,0:T(8,128)S(1)} %get-tuple-element.11), channel_id=1, source_target_pairs={{1,0},{2,1},{3,2},{4,3},{5,4},{6,5},{7,6},{8,7},{9,8},{10,9},{11,1... | collective-permute-start | bytes 208904 | tf_op jit(solution)/shard_map/ppermute | solution.py:407
  26.0 3.6 %collective-permute-start = (f32[17,8,128]{2,1,0:T(8,128)S(1)}, f32[17,8,128]{2,1,0:T(8,128)S(1)}, u32[]{:S(2)}, u32[]{:S(2)}) collective-permute-start(f32[17,8,128]{2,1,0:T(8,128)S(1)} %get-tuple-element.11), channel_id=1, source_target_pairs={{0,1},{1,2},{2,3},{3,4},{4,5},{5,6},{6,7},{7,8},{8,9},{9,10},{10,1... | collective-permute-start | bytes 208904 | tf_op jit(solution)/shard_map/ppermute | solution.py:406
  29.5 1.0 %collective-permute-done.1.right_ref = f32[17,8,128]{2,1,0:T(8,128)S(1)} collective-permute-done((f32[17,8,128]{2,1,0:T(8,128)S(1)}, f32[17,8,128]{2,1,0:T(8,128)S(1)}, u32[]{:S(2)}, u32[]{:S(2)}) %collective-permute-start.1) | collective-permute-done | bytes 69664 | tf_op jit(solution)/shard_map/ppermute | solution.py:407
  30.5 0.4 collective-permute-done.left_ref
  30.9 2.1 %all-to-all-done.incoming_ref = f32[16,40,128]{2,1,0:T(8,128)S(1)} async-done(((f32[16,40,128]{2,1,0:T(8,128)}), f32[16,40,128]{2,1,0:T(8,128)S(1)}, u32[]{:S(2)}, u32[]{:S(2)}) %all-to-all-start) | async-done | bytes 327712 | tf_op jit(solution)/shard_map/all_to_all | solution.py:400
  33.0 0.4 shard_map.79
  33.5 4.3 %collective-permute-start.2 = (f32[51,8,128]{2,1,0:T(8,128)S(1)}, f32[51,8,128]{2,1,0:T(8,128)S(1)}, u32[]{:S(2)}, u32[]{:S(2)}) collective-permute-start(f32[51,8,128]{2,1,0:T(8,128)S(1)} %get-tuple-element.14), channel_id=1, source_target_pairs={{0,16},{16,32},{32,48},{48,64},{64,80},{80,96},{96,112},{112,128},... | collective-permute-start | bytes 626696 | tf_op jit(solution)/shard_map/ppermute | solution.py:411
  37.8 1.9 %collective-permute-start.3 = (f32[51,8,128]{2,1,0:T(8,128)S(1)}, f32[51,8,128]{2,1,0:T(8,128)S(1)}, u32[]{:S(2)}, u32[]{:S(2)}) collective-permute-start(f32[51,8,128]{2,1,0:T(8,128)S(1)} %get-tuple-element.15), channel_id=1, source_target_pairs={{16,0},{32,16},{48,32},{64,48},{80,64},{96,80},{112,96},{128,112},... | collective-permute-start | bytes 626696 | tf_op jit(solution)/shard_map/ppermute | solution.py:412
  39.7 0.1 pad_add_fusion.place_ref
  39.8 2.5 %shard_map.80.early = f32[440,8,256]{2,1,0:T(8,128)S(1)} custom-call(s32[4]{0:T(128)S(1)} %pad_add_fusion.place_ref, f32[32,8,128]{2,1,0:T(8,128)S(1)} %get-tuple-element.12.head_ref, f32[32,8,128]{2,1,0:T(8,128)S(1)} %get-tuple-element.13.cond_ref, f32[32,8,128]{2,1,0:T(8,128)S(1)} %get-tuple-element.16.main_ref, ...), custom_call_target="tpu_custom_call" | custom-call | flops 1048576 | bytes 1048576 | tf_op jit(solution)/shard_map/pallas_call | solution.py:375
  42.3 0.4 collective-permute-done.2.top_ref
  42.7 7.3 %collective-permute-done.3.bottom_ref = f32[51,8,128]{2,1,0:T(8,128)S(1)} collective-permute-done((f32[51,8,128]{2,1,0:T(8,128)S(1)}, f32[51,8,128]{2,1,0:T(8,128)S(1)}, u32[]{:S(2)}, u32[]{:S(2)}) %collective-permute-start.3) | collective-permute-done | bytes 208928 | tf_op jit(solution)/shard_map/ppermute | solution.py:412
  50.0 4.1 %shard_map.81 = (f32[256,128]{1,0:T(8,128)}, f32[256,128]{1,0:T(8,128)}) custom-call(s32[4]{0:T(128)S(1)} %pad_add_fusion.place_ref, f32[51,8,128]{2,1,0:T(8,128)S(1)} %collective-permute-done.2.top_ref, f32[51,8,128]{2,1,0:T(8,128)S(1)} %collective-permute-done.3.bottom_ref, f32[440,8,256]{2,1,0:T(8,128)S(1)} %shard_map.80.early), custom_call_target="tpu_custom_call" | custom-call | flops 1048576 | bytes 1048576 | tf_op jit(solution)/shard_map/pallas_call | solution.py:383
  (1 shorter events, 0.0 us)
Async XLA Ops:
  2.5 30.4 %all-to-all-start = ((f32[16,40,128]{2,1,0:T(8,128)}), f32[16,40,128]{2,1,0:T(8,128)S(1)}, u32[]{:S(2)}, u32[]{:S(2)}) async-start(f32[16,40,128]{2,1,0:T(8,128)} %shard_map.77), calls=%async_computation | async-start | bytes 655360 | tf_op jit(solution)/shard_map/all_to_all | solution.py:400
  20.7 0.9 %copy-start = (f32[8,32,128]{2,1,0:T(8,128)S(1)}, f32[8,32,128]{2,1,0:T(8,128)}, u32[]{:S(2)}) copy-start(f32[8,32,128]{2,1,0:T(8,128)} %param.6) | copy-start | bytes 393220
  21.6 0.9 %copy-start.1 = (s32[8,32,128]{2,1,0:T(8,128)S(1)}, s32[8,32,128]{2,1,0:T(8,128)}, u32[]{:S(2)}) copy-start(s32[8,32,128]{2,1,0:T(8,128)} %param.7) | copy-start | bytes 393220
  22.5 0.7 %copy-start.2 = (f32[8]{0:T(128)S(1)}, f32[8]{0:T(128)}, u32[]{:S(2)}) copy-start(f32[8]{0:T(128)} %class_cond_ref.1) | copy-start | bytes 100
  24.0 6.6 %collective-permute-start.1 = (f32[17,8,128]{2,1,0:T(8,128)S(1)}, f32[17,8,128]{2,1,0:T(8,128)S(1)}, u32[]{:S(2)}, u32[]{:S(2)}) collective-permute-start(f32[17,8,128]{2,1,0:T(8,128)S(1)} %get-tuple-element.11), channel_id=1, source_target_pairs={{1,0},{2,1},{3,2},{4,3},{5,4},{6,5},{7,6},{8,7},{9,8},{10,9},{11,1... | collective-permute-start | bytes 208904 | tf_op jit(solution)/shard_map/ppermute | solution.py:407
  26.0 4.9 %collective-permute-start = (f32[17,8,128]{2,1,0:T(8,128)S(1)}, f32[17,8,128]{2,1,0:T(8,128)S(1)}, u32[]{:S(2)}, u32[]{:S(2)}) collective-permute-start(f32[17,8,128]{2,1,0:T(8,128)S(1)} %get-tuple-element.11), channel_id=1, source_target_pairs={{0,1},{1,2},{2,3},{3,4},{4,5},{5,6},{6,7},{7,8},{8,9},{9,10},{10,1... | collective-permute-start | bytes 208904 | tf_op jit(solution)/shard_map/ppermute | solution.py:406
  33.5 9.2 %collective-permute-start.2 = (f32[51,8,128]{2,1,0:T(8,128)S(1)}, f32[51,8,128]{2,1,0:T(8,128)S(1)}, u32[]{:S(2)}, u32[]{:S(2)}) collective-permute-start(f32[51,8,128]{2,1,0:T(8,128)S(1)} %get-tuple-element.14), channel_id=1, source_target_pairs={{0,16},{16,32},{32,48},{48,64},{64,80},{80,96},{96,112},{112,128},... | collective-permute-start | bytes 626696 | tf_op jit(solution)/shard_map/ppermute | solution.py:411
  37.8 12.2 %collective-permute-start.3 = (f32[51,8,128]{2,1,0:T(8,128)S(1)}, f32[51,8,128]{2,1,0:T(8,128)S(1)}, u32[]{:S(2)}, u32[]{:S(2)}) collective-permute-start(f32[51,8,128]{2,1,0:T(8,128)S(1)} %get-tuple-element.15), channel_id=1, source_target_pairs={{16,0},{32,16},{48,32},{64,48},{80,64},{96,80},{112,96},{128,112},... | collective-permute-start | bytes 626696 | tf_op jit(solution)/shard_map/ppermute | solution.py:412

commit v3 on v2

--- a/solution.py
+++ b/solution.py
@@ -5,7 +5,7 @@
 from jax.experimental.pallas import tpu as pltpu
 from jax.sharding import PartitionSpec as P
 
-NZ, CY, CX, SLOTS = 8, 32, 128, 32
+NZ, CY, CX, SLOTS, NCLASS = 8, 32, 128, 32, 8
 OMEGA = 0.8
 NU1, NU2, NUC = 2, 2, 4
 HY, HX = 14, 16
@@ -70,7 +70,16 @@
         copy.wait()
 
 
-def fields_kernel(class_cond_ref, head_ref, class_ref, ids_ref, head_out, cond_out, strip_out):
+def fields_kernel(class_cond_hbm, head_hbm, class_hbm, ids_hbm, head_out, cond_out, strip_out,
+                  class_cond_ref, head_ref, class_ref, ids_ref, sems):
+    pairs = (
+        (head_hbm, head_ref), (class_hbm, class_ref), (class_cond_hbm, class_cond_ref), (ids_hbm, ids_ref)
+    )
+    copies = [pltpu.make_async_copy(a, b, sems.at[i]) for i, (a, b) in enumerate(pairs)]
+    for copy in copies:
+        copy.start()
+    for copy in copies:
+        copy.wait()
     lane = lane_of((8, CX))
     values = [class_cond_ref[c] for c in range(8)]
     for block in range(CY // 4):
@@ -88,10 +97,25 @@
             conds.append(cond)
         strip_out[block] = packed(heads, lane)
         strip_out[CY // 4 + block] = packed(conds, lane)
-    strip_out[CY // 2] = ids_ref[...]
-
-
-def recharge_kernel(incoming_ref, ids_ref, left_ref, right_ref, head_ref, cond_ref, main_out, halo_out, up_out, down_out):
+    ids = ids_ref[...].astype(F32)
+    count = ids.shape[0] // 4
+    strip_out[CY // 2] = jnp.zeros((8, CX), F32)
+    for r in range(count):
+        strip_out[CY // 2, r : r + 1, :] = jnp.concatenate([ids[4 * r + q : 4 * r + q + 1, :] for q in range(4)], axis=1)
+
+
+def rows_kernel(head_ref, cond_ref, left_ref, right_ref, up_out, down_out):
+    lane = lane_of((8, CX))
+    for out, first, strip0 in ((up_out, 0, 0), (down_out, CY - HY, CY // 4 - 4)):
+        out[0:HY] = head_ref[first : first + HY]
+        out[HY : 2 * HY] = cond_ref[first : first + HY]
+        for i in range(4):
+            for f in range(2):
+                at = f * (CY // 4) + strip0 + i
+                out[2 * HY + 4 * f + i] = jnp.where(lane % 32 < HX, left_ref[at], right_ref[at])
+
+
+def recharge_kernel(incoming_ref, own_ref, left_ref, right_ref, main_out, halo_out, up_out, down_out):
     ncols = incoming_ref.shape[0]
     total = ncols * SLOTS
     chunk = min(256, total)
@@ -109,7 +133,7 @@
         low = (values - high.astype(F32)).astype(jnp.bfloat16)
         return jnp.concatenate([high, low], axis=1)
 
-    own, left, right = ids_ref[...], left_ref[CY // 2], right_ref[CY // 2]
+    own, left, right = own_ref[CY // 2], left_ref[CY // 2], right_ref[CY // 2]
     main = jnp.zeros((NZ * CY, LANES), F32)
     from_left = jnp.zeros((NZ * CY, LANES), F32)
     from_right = jnp.zeros((NZ * CY, LANES), F32)
@@ -130,22 +154,14 @@
     halo = jnp.where(wide >= CX - HX, from_left, jnp.where(wide < HX, from_right, 0.0))
     main_out[...] = main
     halo_out[...] = halo
-    for out, first, strip0 in ((up_out, 0, 0), (down_out, CY - HY, CY // 4 - 4)):
-        skip = first and HY - RY
-        out[0:HY] = head_ref[first : first + HY]
-        out[HY : 2 * HY] = cond_ref[first : first + HY]
-        out[2 * HY : 2 * HY + RY] = main[first + skip : first + skip + RY]
-        base = 2 * HY + RY
-        for i in range(4):
-            for f in range(2):
-                at = f * (CY // 4) + strip0 + i
-                out[base + 4 * f + i] = jnp.where(lane % 32 < HX, left_ref[at], right_ref[at])
+    for out, first in ((up_out, 0), (down_out, CY - RY)):
+        out[0:RY] = main[first : first + RY]
         for i in range(RY // 4):
-            y = first + skip + 4 * i
-            out[base + 8 + i] = packed([halo[y + q] for q in range(4)], lane)
-
-
-SENT = 2 * HY + RY + 8 + RY // 4
+            y = first + 4 * i
+            out[RY + i] = packed([halo[y + q] for q in range(4)], lane)
+
+
+FIELD_ROWS, RECHARGE_ROWS = 2 * HY + 8, RY + RY // 4
 
 
 def span(first, last):
@@ -153,20 +169,22 @@
 
 
 NEEDED = {
-    "u0": (span(1, 58), span(14, 45)),
-    "half": (span(1, 58), span(14, 45)),
+    "u0": (span(1, 58), span(1, 58)),
+    "half": (span(1, 58), span(1, 58)),
     "source": (span(2, 57), span(14, 45)),
-    "fx": (span(2, 57), span(14, 45)),
-    "fy": (span(1, 57), span(14, 44)),
-    "fz": (span(2, 57), span(14, 45)),
-    "weight": (span(2, 57), span(15, 44)),
+    "fx": (span(2, 57), span(2, 57)),
+    "fy": (span(1, 57), span(1, 57)),
+    "fz": (span(2, 57), span(2, 57)),
+    "weight": (span(2, 57), span(2, 57)),
+    "above": (span(2, 14), span(2, 14)),
+    "below": (span(45, 57), span(45, 57)),
     "u1": (span(2, 57), span(15, 44)),
     "u2": (span(3, 56), span(16, 43)),
-    "c_half": (span(1, 28), span(7, 22)),
-    "c_fx": (span(2, 27), span(7, 22)),
-    "c_fy": (span(1, 27), span(7, 21)),
-    "c_fz": (span(2, 27), span(7, 22)),
-    "c_weight": (span(2, 27), span(8, 21)),
+    "c_half": (span(1, 28), span(1, 28)),
+    "c_fx": (span(2, 27), span(2, 27)),
+    "c_fy": (span(1, 27), span(1, 27)),
+    "c_fz": (span(2, 27), span(2, 27)),
+    "c_weight": (span(2, 27), span(2, 27)),
     "c_source": (span(2, 27), span(9, 20)),
     "c_u0": (span(2, 27), span(9, 20)),
     "c_u1": (span(3, 26), span(10, 19)),
@@ -201,8 +219,8 @@
     def ranges(self, name):
         every, own = NEEDED[name]
         if self.late is None:
-            return [(own[0], len(own), 1)]
-        return [(every[0], own[0] - every[0], 0), (own[-1] + 1, every[-1] - own[-1], 2)]
+            return [(own[0], len(own))]
+        return [(every[0], own[0] - every[0]), (own[-1] + 1, every[-1] - own[-1])]
 
     def get(self, name, r, n):
         parts, at = [], r
@@ -238,25 +256,20 @@
         return two + jnp.where(self.even, self.turn(two, -1), self.turn(two, 1))
 
     def coefficients(self, mark, shift, zweight, own):
-        for r, n, _ in self.ranges(mark + "fx"):
-            k = self.get(mark + "half", r, n)
-            self.put(mark + "fx", r, n, k + self.turn(k, -shift))
-            self.put(mark + "fz", r, n, (k + self.turn_z(k, -1)) * (zweight * self.below))
-        for r, n, _ in self.ranges(mark + "fy"):
-            k = self.get(mark + "half", r, n + 1)
-            self.put(mark + "fy", r, n, k[:-1] + k[1:])
-        for r, n, part in self.ranges(mark + "weight"):
-            pieces = [(r, n, part)]
-            if part == 0:
-                pieces = [(r, own[0] - r, 0), (own[0], r + n - own[0], 1)]
-            elif part == 2:
-                pieces = [(r, own[1] + 1 - r, 1), (own[1] + 1, r + n - own[1] - 1, 2)]
-            for at, many, which in pieces:
-                x, z = self.get(mark + "fx", at, many), self.get(mark + "fz", at, many)
-                y = self.get(mark + "fy", at - 1, many + 1)
-                total = (x + self.turn(x, shift)) + (y[1:] + y[:-1]) + (z + self.turn_z(z, 1))
-                scale = self.inside[which]
-                self.put(mark + "weight", at, many, scale / jnp.where(scale > 0.0, total, 1.0))
+        r, n = self.ranges(mark + "fx")[0]
+        k = self.get(mark + "half", r, n)
+        self.put(mark + "fx", r, n, k + self.turn(k, -shift))
+        self.put(mark + "fz", r, n, (k + self.turn_z(k, -1)) * (zweight * self.below))
+        r, n = self.ranges(mark + "fy")[0]
+        k = self.get(mark + "half", r, n + 1)
+        self.put(mark + "fy", r, n, k[:-1] + k[1:])
+        r, n = self.ranges(mark + "weight")[0]
+        for at, end, scale in zip((r,) + own, own + (r + n,), self.inside):
+            many = end - at
+            x, z = self.get(mark + "fx", at, many), self.get(mark + "fz", at, many)
+            y = self.get(mark + "fy", at - 1, many + 1)
+            total = (x + self.turn(x, shift)) + (y[1:] + y[:-1]) + (z + self.turn_z(z, 1))
+            self.put(mark + "weight", at, many, scale / jnp.where(scale > 0.0, total, 1.0))
 
     def operator(self, u, mark, shift, r, n):
         v = self.get(u, r - 1, n + 2)
@@ -267,26 +280,35 @@
         return own, (x - self.turn(x, shift)) + (y[1:] - y[:-1]) + (z - self.turn_z(z, 1))
 
     def sweep(self, old, new, mark, shift):
-        for r, n, _ in self.ranges(new):
+        for r, n in self.ranges(new):
             own, applied = self.operator(old, mark, shift, r, n)
             left = self.get(mark + "source", r, n) - applied
             self.put(new, r, n, own + self.get(mark + "weight", r, n) * left)
 
     def run(self, done):
-        self.coefficients("", 1, 1.0, (HY, HY + CY - 1))
-        self.sweep("u0", "u1", "", 1)
+        if self.late is None:
+            self.coefficients("", 1, 1.0, (HY, HY + CY))
+            self.sweep("u0", "u1", "", 1)
+            c, n = self.ranges("c_half")[0]
+            self.put("c_half", c, n, 0.25 * self.pairs(self.get("half", 2 * c, 2 * n)))
+            self.coefficients("c_", 2, 4.0, (HY // 2, HY // 2 + CY // 2))
+            for name in ("above", "below"):
+                r, n = self.ranges(name)[0]
+                own, applied = self.operator("u0", "", 1, r, n)
+                self.put(name, r, n, own - self.get("weight", r, n) * applied)
+        else:
+            for name, (r, n) in zip(("above", "below"), self.ranges("u1")):
+                added = self.get("weight", r, n) * self.get("source", r, n)
+                self.put("u1", r, n, self.get(name, r, n) + added)
         self.sweep("u1", "u2", "", 1)
-        for c, n, _ in self.ranges("c_half"):
-            self.put("c_half", c, n, 0.25 * self.pairs(self.get("half", 2 * c, 2 * n)))
-        self.coefficients("c_", 2, 4.0, (HY // 2, HY // 2 + CY // 2 - 1))
-        for c, n, _ in self.ranges("c_source"):
+        for c, n in self.ranges("c_source"):
             _, applied = self.operator("u2", "", 1, 2 * c, 2 * n)
             summed = self.pairs(self.get("source", 2 * c, 2 * n) - applied)
             self.put("c_source", c, n, summed)
             self.put("c_u0", c, n, self.get("c_weight", c, n) * summed)
         for i in range(1, NUC):
             self.sweep("c_u%d" % (i - 1), "c_u%d" % i, "c_", 2)
-        for r, n, _ in self.ranges("u3"):
+        for r, n in self.ranges("u3"):
             c, many = r // 2, (r + n - 1) // 2 - r // 2 + 1
             added = self.get("c_u%d" % (NUC - 1), c, many)
             added = jnp.broadcast_to(added[:, None], (many, 2, NZ, LANES)).reshape(2 * many, NZ, LANES)
@@ -294,12 +316,12 @@
         self.sweep("u3", "u4", "", 1)
         self.sweep("u4", "u5", "", 1)
         done()
-        for r, n, _ in self.ranges("residual"):
+        for r, n in self.ranges("residual"):
             _, applied = self.operator("u5", "", 1, r, n)
             self.put("residual", r, n, self.get("source", r, n) - applied)
 
 
-def early_kernel(place_ref, head_ref, cond_ref, main_ref, halo_ref, left_ref, right_ref, early):
+def early_kernel(place_ref, head_ref, cond_ref, main_ref, halo_ref, left_ref, right_ref, top_ref, bottom_ref, early):
     cycle = Cycle(place_ref, early)
     lane = lane_of((8, CX))
     for i in range(CY // 4):
@@ -311,23 +333,22 @@
             cycle.put_parts("u0", HY + y, head_ref[y], unpacked(heads, q, lane))
             cycle.put_parts("half", HY + y, 0.5 * cond_ref[y], unpacked(conds, q, lane))
             cycle.put_parts("source", HY + y, main_ref[y], halo_ref[y])
-    cycle.run(lambda: None)
-
-
-def late_kernel(place_ref, top_ref, bottom_ref, early, head_hbm, residual_hbm, late, head_ref, residual_ref, sems):
-    cycle = Cycle(place_ref, early, late)
-    lane = lane_of((8, CX))
-    base = 2 * HY + RY
-    for ref, first, shift, skip in ((top_ref, 0, 2, HY - RY), (bottom_ref, HY + CY, 0, 0)):
+    for ref, first, shift in ((top_ref, 0, 2), (bottom_ref, HY + CY, 0)):
         for i in range(HY):
             at, q = (i + shift) // 4, (i + shift) % 4
             if first + i in NEEDED["u0"][0]:
-                cycle.put_parts("u0", first + i, ref[i], unpacked(ref[base + at], q, lane))
+                cycle.put_parts("u0", first + i, ref[i], unpacked(ref[2 * HY + at], q, lane))
                 half = 0.5 * ref[HY + i]
-                cycle.put_parts("half", first + i, half, 0.5 * unpacked(ref[base + 4 + at], q, lane))
+                cycle.put_parts("half", first + i, half, 0.5 * unpacked(ref[2 * HY + 4 + at], q, lane))
+    cycle.run(lambda: None)
+
+
+def late_kernel(place_ref, top_ref, bottom_ref, early, head_hbm, residual_hbm, late, head_ref, residual_ref, sems):
+    cycle = Cycle(place_ref, early, late)
+    lane = lane_of((8, CX))
+    for ref, first in ((top_ref, HY - RY), (bottom_ref, HY + CY)):
         for i in range(RY):
-            edge = unpacked(ref[base + 8 + i // 4], i % 4, lane)
-            cycle.put_parts("source", first + skip + i, ref[2 * HY + i], edge)
+            cycle.put_parts("source", first + i, ref[i], unpacked(ref[RY + i // 4], i % 4, lane))
     copies = [
         pltpu.make_async_copy(head_ref, head_hbm, sems.at[0]),
         pltpu.make_async_copy(residual_ref, residual_hbm, sems.at[1]),
@@ -351,7 +372,11 @@
 HBM = pl.BlockSpec(memory_space=pltpu.HBM)
 
 
-def call(kernel, ins, outs, scratch=(), out=VMEM, limit=32 << 20, flops=1 << 20, nbytes=1 << 20):
+def in_hbm(x):
+    return pltpu.with_memory_space_constraint(x, pltpu.HBM)
+
+
+def call(kernel, ins, outs, scratch=(), out=VMEM, flops=1 << 20, nbytes=1 << 20):
     return pl.pallas_call(
         kernel,
         out_shape=tuple(jax.ShapeDtypeStruct(s, F32) for s in outs),
@@ -359,7 +384,7 @@
         out_specs=tuple(out for _ in outs),
         scratch_shapes=scratch,
         cost_estimate=pl.CostEstimate(flops=flops, bytes_accessed=nbytes, transcendentals=0),
-        compiler_params=pltpu.CompilerParams(vmem_limit_bytes=limit),
+        compiler_params=pltpu.CompilerParams(vmem_limit_bytes=32 << 20),
     )
 
 
@@ -371,9 +396,9 @@
     return [(i + 1, i) for i in range(count - 1)]
 
 
-def early_call(place, head, cond, main, halo, left, right):
-    return call(early_kernel, [SMEM] + [VMEM] * 6, [(len(EARLY), NZ, LANES)])(
-        place, head, cond, main, halo, left, right
+def early_call(place, head, cond, main, halo, left, right, top, bottom):
+    return call(early_kernel, [SMEM] + [VMEM] * 8, [(len(EARLY), NZ, LANES)])(
+        place, head, cond, main, halo, left, right, top, bottom
     )[0]
 
 
@@ -385,7 +410,7 @@
 
 def body(head_start, class_map, class_cond, partials, send_count, recv_block):
     ngroups, ncols = lax.axis_size("rows"), lax.axis_size("cols")
-    row, sent = (CY, NZ, CX), (SENT, 8, CX)
+    row = (CY, NZ, CX)
     scratch = [
         pltpu.SMEM((ncols,), jnp.int32),
         pltpu.VMEM((ncols, SLOTS, CX), F32),
@@ -394,25 +419,34 @@
         pltpu.SemaphoreType.DMA((4,)),
         pltpu.SemaphoreType.DMA((4,)),
     ]
-    payload = call(outgoing_kernel, [HBM, HBM], [(ncols, SLOTS + 8, CX)], scratch, HBM, limit=64 << 20)(
-        send_count.reshape(ncols), partials.reshape(ncols, SLOTS, CX)
+    payload = call(outgoing_kernel, [HBM, HBM], [(ncols, SLOTS + 8, CX)], scratch, HBM)(
+        in_hbm(send_count.reshape(ncols)), in_hbm(partials.reshape(ncols, SLOTS, CX))
     )[0]
     incoming = lax.all_to_all(payload, "cols", split_axis=0, concat_axis=0, tiled=True)
-    ids = recv_block.astype(F32).reshape(ncols * SLOTS // CX, CX)
-    ids = jnp.pad(ids, ((0, 8 - ids.shape[0]), (0, 0)))
-    head, cond, strip = call(fields_kernel, [SMEM] + [VMEM] * 3, [row, row, (CY // 2 + 1, 8, CX)])(
-        class_cond, head_start.reshape(NZ * CY, CX), class_map.reshape(NZ * CY, CX), ids
+    flat = (NZ * CY, CX)
+    scratch = [
+        pltpu.SMEM((NCLASS,), F32),
+        pltpu.VMEM(flat, F32),
+        pltpu.VMEM(flat, jnp.int32),
+        pltpu.VMEM((ncols, SLOTS), jnp.int32),
+        pltpu.SemaphoreType.DMA((4,)),
+    ]
+    head, cond, strip = call(fields_kernel, [HBM] * 4, [row, row, (CY // 2 + 1, 8, CX)], scratch)(
+        *(in_hbm(x) for x in (class_cond, head_start.reshape(flat), class_map.reshape(flat), recv_block.reshape(ncols, SLOTS)))
     )
     left = lax.ppermute(strip, "cols", forward(ncols))
     right = lax.ppermute(strip, "cols", backward(ncols))
-    main, halo, up, down = call(recharge_kernel, [VMEM] * 6, [row, row, sent, sent])(
-        incoming, ids, left, right, head, cond
-    )
+    up, down = call(rows_kernel, [VMEM] * 4, [(FIELD_ROWS, 8, CX)] * 2)(head, cond, left, right)
     top = lax.ppermute(down, "rows", forward(ngroups))
     bottom = lax.ppermute(up, "rows", backward(ngroups))
+    main, halo, up, down = call(recharge_kernel, [VMEM] * 4, [row, row] + [(RECHARGE_ROWS, 8, CX)] * 2)(
+        incoming, strip, left, right
+    )
+    top_source = lax.ppermute(down, "rows", forward(ngroups))
+    bottom_source = lax.ppermute(up, "rows", backward(ngroups))
     place = jnp.stack([lax.axis_index("rows"), lax.axis_index("cols"), ngroups, ncols]).astype(jnp.int32)
-    early = early_call(place, head, cond, main, halo, left, right)
-    out = late_call(place, top, bottom, early)
+    early = early_call(place, head, cond, main, halo, left, right, top, bottom)
+    out = late_call(place, top_source, bottom_source, early)
     return tuple(o.reshape(NZ, CY, CX) for o in out)
 
 

time: 54.5 us -> 56.2 us (1.031)
  starting transfers between devices: 29.2 us -> 37.8 us
  waiting for transfers between devices: 11.2 us -> 7.15 us
  local copies, waits for them, and re-layouts: 2.55 us -> 0 us
  other arithmetic: 0.78 us -> 0.08 us
    ppermute x0 -> x2, starting transfers between devices: none -> 8.61 us  [the longest x1 6.69 us: body(): top_source = lax.ppermute(down, 'rows', forward(ngroups))]
    ppermute x1, waiting for transfers between devices: 7.33 us -> 0.01 us  [body(): bottom = lax.ppermute(up, 'rows', backward(ngroups))]
    ppermute x0 -> x2, waiting for transfers between devices: none -> 3.38 us  [the longest x1 3.38 us: body(): bottom_source = lax.ppermute(up, 'rows', backward(ngroups))]
    ppermute x1, waiting for transfers between devices: 0.99 us -> 3.75 us  [body(): right = lax.ppermute(strip, 'cols', backward(ncols))]
    unnamed x6 -> x0, local copies, waits for them, and re-layouts: 2.46 us -> none
    all_to_all x1, waiting for transfers between devices: 2.11 us -> 0.01 us  [body(): lax.all_to_all(payload, 'cols', split_axis=0, concat_axis=0, tiled=True)]
    pallas_call x4 -> x5, Pallas kernels: 5.59 us -> 6.52 us  [the longest x1 2.87 us: early_call(): call(early_kernel, [SMEM] + [VMEM] * 8, [(len(EARLY), NZ, LANES)])]
    convert_element_type x1 -> x0, other arithmetic: 0.7 us -> none  [body(): ids = recv_block.astype(F32).reshape(ncols * SLOTS // CX, CX)]
  transfers between devices with their start and end apart: 5 -> 7, of which waited for: 5 -> 2; matrix products, arithmetic and copies ran while one was open for 2% -> 0% of each run, Pallas kernels for 6% -> 8%
where the time goes in v3:
time: 56.2 us; the launch traced here: 55.8 us
  starting transfers between devices  37.8 us (67%)
  Pallas kernels  10 us (18%)
  waiting for transfers between devices  7.15 us (13%)
  between operations  0.73 us (1%)
    all_to_all x1, starting transfers between devices, body(): lax.all_to_all(payload, 'cols', split_axis=0, concat_axis=0, tiled=True)  17.4 us
    ppermute x1, starting transfers between devices, body(): top_source = lax.ppermute(down, 'rows', forward(ngroups))  6.69 us
    ppermute x1, starting transfers between devices, body(): top = lax.ppermute(down, 'rows', forward(ngroups))  4.33 us
    ppermute x1, waiting for transfers between devices, body(): right = lax.ppermute(strip, 'cols', backward(ncols))  3.75 us
    ppermute x1, starting transfers between devices, body(): left = lax.ppermute(strip, 'cols', forward(ncols))  3.55 us
    pallas_call x1, Pallas kernels, late_call(): call(late_kernel, [SMEM] + [VMEM] * 3, [flat] * 2, scratch, HBM)  3.51 us
    ppermute x1, waiting for transfers between devices, body(): bottom_source = lax.ppermute(up, 'rows', backward(ngroups))  3.38 us
    pallas_call x1, Pallas kernels, early_call(): call(early_kernel, [SMEM] + [VMEM] * 8, [(len(EARLY), NZ, LANES)])  2.87 us
  transfers between devices with their start and end apart: 7, of which 2 were waited for; matrix products, arithmetic and copies ran while one was open for 0% of the time, Pallas kernels for 8%

profile of v3, /device:TPU:63, one launch (start us, length us, event | category | flops | bytes accessed | tf_op | source)
XLA Modules:
  0.0 55.8 jit_solution(16302521425089963528)
XLA Ops:
  0.6 1.9 %shard_map.77 = f32[16,40,128]{2,1,0:T(8,128)} custom-call(s32[16]{0:T(128)} %bitcast.13, f32[16,32,128]{2,1,0:T(8,128)} %bitcast.9), custom_call_target="tpu_custom_call" | custom-call | flops 1048576 | bytes 1048576 | tf_op jit(solution)/shard_map/pallas_call | solution.py:422
  2.5 17.4 %all-to-all-start = ((f32[16,40,128]{2,1,0:T(8,128)}), f32[16,40,128]{2,1,0:T(8,128)S(1)}, u32[]{:S(2)}, u32[]{:S(2)}) async-start(f32[16,40,128]{2,1,0:T(8,128)} %shard_map.77), calls=%async_computation | async-start | bytes 655360 | tf_op jit(solution)/shard_map/all_to_all | solution.py:425
  19.9 1.3 %shard_map.78 = (f32[32,8,128]{2,1,0:T(8,128)S(1)}, f32[32,8,128]{2,1,0:T(8,128)S(1)}, f32[17,8,128]{2,1,0:T(8,128)S(1)}) custom-call(f32[8]{0:T(128)} %class_cond_hbm.1, f32[256,128]{1,0:T(8,128)} %bitcast.10, s32[256,128]{1,0:T(8,128)} %bitcast.11, s32[16,32]{1,0:T(8,128)} %bitcast.12), custom_call_target="tpu_custom_call" | custom-call | flops 1048576 | bytes 1048576 | tf_op jit(solution)/shard_map/pallas_call | solution.py:434
  21.2 2.0 %collective-permute-start.1 = (f32[17,8,128]{2,1,0:T(8,128)S(1)}, f32[17,8,128]{2,1,0:T(8,128)S(1)}, u32[]{:S(2)}, u32[]{:S(2)}) collective-permute-start(f32[17,8,128]{2,1,0:T(8,128)S(1)} %get-tuple-element.13.own_ref), channel_id=1, source_target_pairs={{1,0},{2,1},{3,2},{4,3},{5,4},{6,5},{7,6},{8,7},{9,8},{10,9},{11,1... | collective-permute-start | bytes 208904 | tf_op jit(solution)/shard_map/ppermute | solution.py:438
  23.2 3.5 %collective-permute-start = (f32[17,8,128]{2,1,0:T(8,128)S(1)}, f32[17,8,128]{2,1,0:T(8,128)S(1)}, u32[]{:S(2)}, u32[]{:S(2)}) collective-permute-start(f32[17,8,128]{2,1,0:T(8,128)S(1)} %get-tuple-element.13.own_ref), channel_id=1, source_target_pairs={{0,1},{1,2},{2,3},{3,4},{4,5},{5,6},{6,7},{7,8},{8,9},{9,10},{10,1... | collective-permute-start | bytes 208904 | tf_op jit(solution)/shard_map/ppermute | solution.py:437
  26.8 3.8 %collective-permute-done.1.right_ref = f32[17,8,128]{2,1,0:T(8,128)S(1)} collective-permute-done((f32[17,8,128]{2,1,0:T(8,128)S(1)}, f32[17,8,128]{2,1,0:T(8,128)S(1)}, u32[]{:S(2)}, u32[]{:S(2)}) %collective-permute-start.1) | collective-permute-done | bytes 69664 | tf_op jit(solution)/shard_map/ppermute | solution.py:438
  30.5 0.0 collective-permute-done.left_ref
  30.6 4.3 %collective-permute-start.4 = (f32[36,8,128]{2,1,0:T(8,128)S(1)}, f32[36,8,128]{2,1,0:T(8,128)S(1)}, u32[]{:S(2)}, u32[]{:S(2)}) collective-permute-start(f32[36,8,128]{2,1,0:T(8,128)S(1)} %get-tuple-element.20), channel_id=1, source_target_pairs={{0,16},{16,32},{32,48},{48,64},{64,80},{80,96},{96,112},{112,128},... | collective-permute-start | bytes 442376 | tf_op jit(solution)/shard_map/ppermute | solution.py:440
  34.9 1.9 %collective-permute-start.5 = (f32[36,8,128]{2,1,0:T(8,128)S(1)}, f32[36,8,128]{2,1,0:T(8,128)S(1)}, u32[]{:S(2)}, u32[]{:S(2)}) collective-permute-start(f32[36,8,128]{2,1,0:T(8,128)S(1)} %get-tuple-element.21), channel_id=1, source_target_pairs={{16,0},{32,16},{48,32},{64,48},{80,64},{96,80},{112,96},{128,112},... | collective-permute-start | bytes 442376 | tf_op jit(solution)/shard_map/ppermute | solution.py:441
  36.8 0.0 all-to-all-done.incoming_ref
  36.8 0.4 shard_map.79
  37.3 6.7 %collective-permute-start.2 = (f32[15,8,128]{2,1,0:T(8,128)S(1)}, f32[15,8,128]{2,1,0:T(8,128)S(1)}, u32[]{:S(2)}, u32[]{:S(2)}) collective-permute-start(f32[15,8,128]{2,1,0:T(8,128)S(1)} %get-tuple-element.14), channel_id=1, source_target_pairs={{0,16},{16,32},{32,48},{48,64},{64,80},{80,96},{96,112},{112,128},... | collective-permute-start | bytes 184328 | tf_op jit(solution)/shard_map/ppermute | solution.py:445
  44.0 1.9 %collective-permute-start.3 = (f32[15,8,128]{2,1,0:T(8,128)S(1)}, f32[15,8,128]{2,1,0:T(8,128)S(1)}, u32[]{:S(2)}, u32[]{:S(2)}) collective-permute-start(f32[15,8,128]{2,1,0:T(8,128)S(1)} %get-tuple-element.15), channel_id=1, source_target_pairs={{16,0},{32,16},{48,32},{64,48},{80,64},{96,80},{112,96},{128,112},... | collective-permute-start | bytes 184328 | tf_op jit(solution)/shard_map/ppermute | solution.py:446
  45.9 0.1 pad_add_fusion.place_ref
  46.0 0.0 collective-permute-done.4.top_ref
  46.0 0.0 collective-permute-done.5.bottom_ref
  46.0 2.9 %shard_map.81.early = f32[674,8,256]{2,1,0:T(8,128)S(1)} custom-call(s32[4]{0:T(128)S(1)} %pad_add_fusion.place_ref, f32[32,8,128]{2,1,0:T(8,128)S(1)} %get-tuple-element.16.head_ref, f32[32,8,128]{2,1,0:T(8,128)S(1)} %get-tuple-element.17.cond_ref, f32[32,8,128]{2,1,0:T(8,128)S(1)} %get-tuple-element.18.main_ref, ...), custom_call_target="tpu_custom_call" | custom-call | flops 1048576 | bytes 1048576 | tf_op jit(solution)/shard_map/pallas_call | solution.py:400
  48.9 0.0 collective-permute-done.2.top_ref
  48.9 3.4 %collective-permute-done.3.bottom_ref = f32[15,8,128]{2,1,0:T(8,128)S(1)} collective-permute-done((f32[15,8,128]{2,1,0:T(8,128)S(1)}, f32[15,8,128]{2,1,0:T(8,128)S(1)}, u32[]{:S(2)}, u32[]{:S(2)}) %collective-permute-start.3) | collective-permute-done | bytes 61472 | tf_op jit(solution)/shard_map/ppermute | solution.py:446
  52.3 3.5 %shard_map.82 = (f32[256,128]{1,0:T(8,128)}, f32[256,128]{1,0:T(8,128)}) custom-call(s32[4]{0:T(128)S(1)} %pad_add_fusion.place_ref, f32[15,8,128]{2,1,0:T(8,128)S(1)} %collective-permute-done.2.top_ref, f32[15,8,128]{2,1,0:T(8,128)S(1)} %collective-permute-done.3.bottom_ref, f32[674,8,256]{2,1,0:T(8,128)S(1)} %shard_map.81.early), custom_call_target="tpu_custom_call" | custom-call | flops 1048576 | bytes 1048576 | tf_op jit(solution)/shard_map/pallas_call | solution.py:408
  (1 shorter events, 0.0 us)
Async XLA Ops:
  2.5 34.3 %all-to-all-start = ((f32[16,40,128]{2,1,0:T(8,128)}), f32[16,40,128]{2,1,0:T(8,128)S(1)}, u32[]{:S(2)}, u32[]{:S(2)}) async-start(f32[16,40,128]{2,1,0:T(8,128)} %shard_map.77), calls=%async_computation | async-start | bytes 655360 | tf_op jit(solution)/shard_map/all_to_all | solution.py:425
  21.2 9.3 %collective-permute-start.1 = (f32[17,8,128]{2,1,0:T(8,128)S(1)}, f32[17,8,128]{2,1,0:T(8,128)S(1)}, u32[]{:S(2)}, u32[]{:S(2)}) collective-permute-start(f32[17,8,128]{2,1,0:T(8,128)S(1)} %get-tuple-element.13.own_ref), channel_id=1, source_target_pairs={{1,0},{2,1},{3,2},{4,3},{5,4},{6,5},{7,6},{8,7},{9,8},{10,9},{11,1... | collective-permute-start | bytes 208904 | tf_op jit(solution)/shard_map/ppermute | solution.py:438
  23.2 7.3 %collective-permute-start = (f32[17,8,128]{2,1,0:T(8,128)S(1)}, f32[17,8,128]{2,1,0:T(8,128)S(1)}, u32[]{:S(2)}, u32[]{:S(2)}) collective-permute-start(f32[17,8,128]{2,1,0:T(8,128)S(1)} %get-tuple-element.13.own_ref), channel_id=1, source_target_pairs={{0,1},{1,2},{2,3},{3,4},{4,5},{5,6},{6,7},{7,8},{8,9},{9,10},{10,1... | collective-permute-start | bytes 208904 | tf_op jit(solution)/shard_map/ppermute | solution.py:437
  30.6 15.4 %collective-permute-start.4 = (f32[36,8,128]{2,1,0:T(8,128)S(1)}, f32[36,8,128]{2,1,0:T(8,128)S(1)}, u32[]{:S(2)}, u32[]{:S(2)}) collective-permute-start(f32[36,8,128]{2,1,0:T(8,128)S(1)} %get-tuple-element.20), channel_id=1, source_target_pairs={{0,16},{16,32},{32,48},{48,64},{64,80},{80,96},{96,112},{112,128},... | collective-permute-start | bytes 442376 | tf_op jit(solution)/shard_map/ppermute | solution.py:440
  34.9 11.1 %collective-permute-start.5 = (f32[36,8,128]{2,1,0:T(8,128)S(1)}, f32[36,8,128]{2,1,0:T(8,128)S(1)}, u32[]{:S(2)}, u32[]{:S(2)}) collective-permute-start(f32[36,8,128]{2,1,0:T(8,128)S(1)} %get-tuple-element.21), channel_id=1, source_target_pairs={{16,0},{32,16},{48,32},{64,48},{80,64},{96,80},{112,96},{128,112},... | collective-permute-start | bytes 442376 | tf_op jit(solution)/shard_map/ppermute | solution.py:441
  37.3 11.6 %collective-permute-start.2 = (f32[15,8,128]{2,1,0:T(8,128)S(1)}, f32[15,8,128]{2,1,0:T(8,128)S(1)}, u32[]{:S(2)}, u32[]{:S(2)}) collective-permute-start(f32[15,8,128]{2,1,0:T(8,128)S(1)} %get-tuple-element.14), channel_id=1, source_target_pairs={{0,16},{16,32},{32,48},{48,64},{64,80},{80,96},{96,112},{112,128},... | collective-permute-start | bytes 184328 | tf_op jit(solution)/shard_map/ppermute | solution.py:445
  44.0 8.3 %collective-permute-start.3 = (f32[15,8,128]{2,1,0:T(8,128)S(1)}, f32[15,8,128]{2,1,0:T(8,128)S(1)}, u32[]{:S(2)}, u32[]{:S(2)}) collective-permute-start(f32[15,8,128]{2,1,0:T(8,128)S(1)} %get-tuple-element.15), channel_id=1, source_target_pairs={{16,0},{32,16},{48,32},{64,48},{80,64},{96,80},{112,96},{128,112},... | collective-permute-start | bytes 184328 | tf_op jit(solution)/shard_map/ppermute | solution.py:446

commit v4 on v2

--- a/solution.py
+++ b/solution.py
@@ -1,3 +1,5 @@
+import functools
+
 import jax
 import jax.numpy as jnp
 from jax import lax
@@ -5,7 +7,7 @@
 from jax.experimental.pallas import tpu as pltpu
 from jax.sharding import PartitionSpec as P
 
-NZ, CY, CX, SLOTS = 8, 32, 128, 32
+NZ, CY, CX, SLOTS, NCLASS = 8, 32, 128, 32, 8
 OMEGA = 0.8
 NU1, NU2, NUC = 2, 2, 4
 HY, HX = 14, 16
@@ -70,7 +72,16 @@
         copy.wait()
 
 
-def fields_kernel(class_cond_ref, head_ref, class_ref, ids_ref, head_out, cond_out, strip_out):
+def fields_kernel(class_cond_hbm, head_hbm, class_hbm, ids_hbm, head_out, cond_out, strip_out,
+                  class_cond_ref, head_ref, class_ref, ids_ref, sems):
+    pairs = (
+        (head_hbm, head_ref), (class_hbm, class_ref), (class_cond_hbm, class_cond_ref), (ids_hbm, ids_ref)
+    )
+    copies = [pltpu.make_async_copy(a, b, sems.at[i]) for i, (a, b) in enumerate(pairs)]
+    for copy in copies:
+        copy.start()
+    for copy in copies:
+        copy.wait()
     lane = lane_of((8, CX))
     values = [class_cond_ref[c] for c in range(8)]
     for block in range(CY // 4):
@@ -88,10 +99,14 @@
             conds.append(cond)
         strip_out[block] = packed(heads, lane)
         strip_out[CY // 4 + block] = packed(conds, lane)
-    strip_out[CY // 2] = ids_ref[...]
-
-
-def recharge_kernel(incoming_ref, ids_ref, left_ref, right_ref, head_ref, cond_ref, main_out, halo_out, up_out, down_out):
+    ids = ids_ref[...].astype(F32)
+    count = ids.shape[0] // 4
+    strip_out[CY // 2] = jnp.zeros((8, CX), F32)
+    for r in range(count):
+        strip_out[CY // 2, r : r + 1, :] = jnp.concatenate([ids[4 * r + q : 4 * r + q + 1, :] for q in range(4)], axis=1)
+
+
+def recharge_kernel(incoming_ref, own_ref, left_ref, right_ref, head_ref, cond_ref, main_out, halo_out, up_out, down_out):
     ncols = incoming_ref.shape[0]
     total = ncols * SLOTS
     chunk = min(256, total)
@@ -109,7 +124,7 @@
         low = (values - high.astype(F32)).astype(jnp.bfloat16)
         return jnp.concatenate([high, low], axis=1)
 
-    own, left, right = ids_ref[...], left_ref[CY // 2], right_ref[CY // 2]
+    own, left, right = own_ref[CY // 2], left_ref[CY // 2], right_ref[CY // 2]
     main = jnp.zeros((NZ * CY, LANES), F32)
     from_left = jnp.zeros((NZ * CY, LANES), F32)
     from_right = jnp.zeros((NZ * CY, LANES), F32)
@@ -177,16 +192,16 @@
     "u5": (span(13, 46), span(26, 33)),
     "residual": (span(14, 45), span(27, 32)),
 }
-EARLY, LATE = {}, {}
+EARLY, LATE = {}, ({}, {})
 for _name, (_every, _own) in NEEDED.items():
     for _r in _every:
-        _into = EARLY if _r in _own else LATE
+        _into = EARLY if _r in _own else LATE[0 if _r < _own[0] else 1]
         _into[_name, _r] = len(_into)
 
 
 class Cycle:
-    def __init__(self, place_ref, early, late=None):
-        self.early, self.late = early, late
+    def __init__(self, place_ref, early, late=None, side=None):
+        self.early, self.late, self.side = early, late, side
         self.lane = lane_of((1, NZ, LANES))
         layer = lax.broadcasted_iota(jnp.int32, (1, NZ, LANES), 1)
         self.below = jnp.where(layer < NZ - 1, 1.0, 0.0)
@@ -202,12 +217,14 @@
         every, own = NEEDED[name]
         if self.late is None:
             return [(own[0], len(own), 1)]
-        return [(every[0], own[0] - every[0], 0), (own[-1] + 1, every[-1] - own[-1], 2)]
+        if self.side == 0:
+            return [(every[0], own[0] - every[0], 0)]
+        return [(own[-1] + 1, every[-1] - own[-1], 2)]
 
     def get(self, name, r, n):
         parts, at = [], r
         while at < r + n:
-            ref, rows = (self.early, EARLY) if (name, at) in EARLY else (self.late, LATE)
+            ref, rows = (self.early, EARLY) if (name, at) in EARLY else (self.late, LATE[self.side])
             many = 1
             while at + many < r + n and rows.get((name, at + many)) == rows[name, at] + many:
                 many += 1
@@ -219,10 +236,10 @@
         if self.late is None:
             self.early[pl.ds(EARLY[name, r], n)] = value
         else:
-            self.late[pl.ds(LATE[name, r], n)] = value
+            self.late[pl.ds(LATE[self.side][name, r], n)] = value
 
     def put_parts(self, name, r, main, halo):
-        ref, at = (self.early, EARLY[name, r]) if self.late is None else (self.late, LATE[name, r])
+        ref, at = (self.early, EARLY[name, r]) if self.late is None else (self.late, LATE[self.side][name, r])
         ref[at, :, 0:CX] = main
         ref[at, :, CX:LANES] = halo
 
@@ -314,33 +331,37 @@
     cycle.run(lambda: None)
 
 
-def late_kernel(place_ref, top_ref, bottom_ref, early, head_hbm, residual_hbm, late, head_ref, residual_ref, sems):
-    cycle = Cycle(place_ref, early, late)
+def late_kernel(side, place_ref, sent_ref, early, *refs):
+    head_hbm, residual_hbm, late, head_ref, residual_ref, sems = refs[-6:]
+    cycle = Cycle(place_ref, early, late, side)
     lane = lane_of((8, CX))
     base = 2 * HY + RY
-    for ref, first, shift, skip in ((top_ref, 0, 2, HY - RY), (bottom_ref, HY + CY, 0, 0)):
-        for i in range(HY):
-            at, q = (i + shift) // 4, (i + shift) % 4
-            if first + i in NEEDED["u0"][0]:
-                cycle.put_parts("u0", first + i, ref[i], unpacked(ref[base + at], q, lane))
-                half = 0.5 * ref[HY + i]
-                cycle.put_parts("half", first + i, half, 0.5 * unpacked(ref[base + 4 + at], q, lane))
-        for i in range(RY):
-            edge = unpacked(ref[base + 8 + i // 4], i % 4, lane)
-            cycle.put_parts("source", first + skip + i, ref[2 * HY + i], edge)
+    first, shift, skip = ((0, 2, HY - RY), (HY + CY, 0, 0))[side]
+    for i in range(HY):
+        at, q = (i + shift) // 4, (i + shift) % 4
+        if first + i in NEEDED["u0"][0]:
+            cycle.put_parts("u0", first + i, sent_ref[i], unpacked(sent_ref[base + at], q, lane))
+            half = 0.5 * sent_ref[HY + i]
+            cycle.put_parts("half", first + i, half, 0.5 * unpacked(sent_ref[base + 4 + at], q, lane))
+    for i in range(RY):
+        edge = unpacked(sent_ref[base + 8 + i // 4], i % 4, lane)
+        cycle.put_parts("source", first + skip + i, sent_ref[2 * HY + i], edge)
+    own = pl.ds(side * (CY // 2), CY // 2)
     copies = [
-        pltpu.make_async_copy(head_ref, head_hbm, sems.at[0]),
-        pltpu.make_async_copy(residual_ref, residual_hbm, sems.at[1]),
+        pltpu.make_async_copy(head_ref, head_hbm.at[:, own, :], sems.at[0]),
+        pltpu.make_async_copy(residual_ref, residual_hbm.at[:, own, :], sems.at[1]),
     ]
 
+    def leave(name, ref):
+        for y in range(CY // 2):
+            ref[:, y, :] = cycle.get(name, HY + side * (CY // 2) + y, 1)[0, :, 0:CX]
+
     def head_done():
-        for y in range(CY):
-            head_ref[pl.ds(y, NZ, stride=CY), :] = cycle.get("u5", HY + y, 1)[0, :, 0:CX]
+        leave("u5", head_ref)
         copies[0].start()
 
     cycle.run(head_done)
-    for y in range(CY):
-        residual_ref[pl.ds(y, NZ, stride=CY), :] = cycle.get("residual", HY + y, 1)[0, :, 0:CX]
+    leave("residual", residual_ref)
     copies[1].start()
     for copy in copies:
         copy.wait()
@@ -351,15 +372,20 @@
 HBM = pl.BlockSpec(memory_space=pltpu.HBM)
 
 
-def call(kernel, ins, outs, scratch=(), out=VMEM, limit=32 << 20, flops=1 << 20, nbytes=1 << 20):
+def in_hbm(x):
+    return pltpu.with_memory_space_constraint(x, pltpu.HBM)
+
+
+def call(kernel, ins, outs, scratch=(), out=VMEM, aliases={}, flops=1 << 20, nbytes=1 << 20):
     return pl.pallas_call(
         kernel,
         out_shape=tuple(jax.ShapeDtypeStruct(s, F32) for s in outs),
         in_specs=ins,
         out_specs=tuple(out for _ in outs),
         scratch_shapes=scratch,
+        input_output_aliases=aliases,
         cost_estimate=pl.CostEstimate(flops=flops, bytes_accessed=nbytes, transcendentals=0),
-        compiler_params=pltpu.CompilerParams(vmem_limit_bytes=limit),
+        compiler_params=pltpu.CompilerParams(vmem_limit_bytes=32 << 20),
     )
 
 
@@ -377,10 +403,16 @@
     )[0]
 
 
-def late_call(place, top, bottom, early):
-    flat = (NZ * CY, CX)
-    scratch = [pltpu.VMEM((len(LATE), NZ, LANES), F32)] + [pltpu.VMEM(flat, F32)] * 2 + [pltpu.SemaphoreType.DMA((2,))]
-    return call(late_kernel, [SMEM] + [VMEM] * 3, [flat] * 2, scratch, HBM)(place, top, bottom, early)
+def late_call(side, place, sent, early, outs=()):
+    half = pltpu.VMEM((NZ, CY // 2, CX), F32)
+    return call(
+        functools.partial(late_kernel, side),
+        [SMEM] + [VMEM] * 2 + [HBM] * len(outs),
+        [(NZ, CY, CX)] * 2,
+        [pltpu.VMEM((len(LATE[side]), NZ, LANES), F32), half, half, pltpu.SemaphoreType.DMA((2,))],
+        HBM,
+        {3: 0, 4: 1} if outs else {},
+    )(place, sent, early, *outs)
 
 
 def body(head_start, class_map, class_cond, partials, send_count, recv_block):
@@ -394,26 +426,33 @@
         pltpu.SemaphoreType.DMA((4,)),
         pltpu.SemaphoreType.DMA((4,)),
     ]
-    payload = call(outgoing_kernel, [HBM, HBM], [(ncols, SLOTS + 8, CX)], scratch, HBM, limit=64 << 20)(
-        send_count.reshape(ncols), partials.reshape(ncols, SLOTS, CX)
+    payload = call(outgoing_kernel, [HBM, HBM], [(ncols, SLOTS + 8, CX)], scratch, HBM)(
+        in_hbm(send_count.reshape(ncols)), in_hbm(partials.reshape(ncols, SLOTS, CX))
     )[0]
     incoming = lax.all_to_all(payload, "cols", split_axis=0, concat_axis=0, tiled=True)
-    ids = recv_block.astype(F32).reshape(ncols * SLOTS // CX, CX)
-    ids = jnp.pad(ids, ((0, 8 - ids.shape[0]), (0, 0)))
-    head, cond, strip = call(fields_kernel, [SMEM] + [VMEM] * 3, [row, row, (CY // 2 + 1, 8, CX)])(
-        class_cond, head_start.reshape(NZ * CY, CX), class_map.reshape(NZ * CY, CX), ids
+    flat = (NZ * CY, CX)
+    scratch = [
+        pltpu.SMEM((NCLASS,), F32),
+        pltpu.VMEM(flat, F32),
+        pltpu.VMEM(flat, jnp.int32),
+        pltpu.VMEM((ncols, SLOTS), jnp.int32),
+        pltpu.SemaphoreType.DMA((4,)),
+    ]
+    fields = (class_cond, head_start.reshape(flat), class_map.reshape(flat), recv_block.reshape(ncols, SLOTS))
+    head, cond, strip = call(fields_kernel, [HBM] * 4, [row, row, (CY // 2 + 1, 8, CX)], scratch)(
+        *(in_hbm(x) for x in fields)
     )
     left = lax.ppermute(strip, "cols", forward(ncols))
     right = lax.ppermute(strip, "cols", backward(ncols))
     main, halo, up, down = call(recharge_kernel, [VMEM] * 6, [row, row, sent, sent])(
-        incoming, ids, left, right, head, cond
+        incoming, strip, left, right, head, cond
     )
     top = lax.ppermute(down, "rows", forward(ngroups))
     bottom = lax.ppermute(up, "rows", backward(ngroups))
     place = jnp.stack([lax.axis_index("rows"), lax.axis_index("cols"), ngroups, ncols]).astype(jnp.int32)
     early = early_call(place, head, cond, main, halo, left, right)
-    out = late_call(place, top, bottom, early)
-    return tuple(o.reshape(NZ, CY, CX) for o in out)
+    outs = late_call(0, place, top, early)
+    return tuple(late_call(1, place, bottom, early, outs))
 
 
 def solution(mesh):

time: 54.5 us -> 53.1 us (0.974)
  local copies, waits for them, and re-layouts: 2.55 us -> 0 us
  Pallas kernels: 9.66 us -> 11.5 us
  other arithmetic: 0.78 us -> 0.08 us
    ppermute x1, waiting for transfers between devices: 7.33 us -> 4.55 us  [body(): bottom = lax.ppermute(up, 'rows', backward(ngroups))]
    ppermute x1, waiting for transfers between devices: 0.99 us -> 3.75 us  [body(): right = lax.ppermute(strip, 'cols', backward(ncols))]
    unnamed x6 -> x0, local copies, waits for them, and re-layouts: 2.46 us -> none
    pallas_call x3 -> x4, Pallas kernels: 6.76 us -> 8.7 us  [the longest x2 5.52 us: late_call(): call(functools.partial(late_kernel, side), [SMEM] + [VMEM] * 2 + [HBM] *...]
    convert_element_type x1 -> x0, other arithmetic: 0.7 us -> none  [body(): ids = recv_block.astype(F32).reshape(ncols * SLOTS // CX, CX)]
  transfers between devices with their start and end apart: 5 -> 5, of which waited for: 5 -> 4; matrix products, arithmetic and copies ran while one was open for 2% -> 0% of each run, Pallas kernels for 6% -> 12%
where the time goes in v4:
time: 53.1 us; the launch traced here: 52.8 us
  starting transfers between devices  29.2 us (55%)
  Pallas kernels  11.5 us (22%)
  waiting for transfers between devices  11.3 us (21%)
  between operations  0.7 us (1%)
    all_to_all x1, starting transfers between devices, body(): lax.all_to_all(payload, 'cols', split_axis=0, concat_axis=0, tiled=True)  17.4 us
    pallas_call x2, Pallas kernels, late_call(): call(functools.partial(late_kernel, side), [SMEM] + [VMEM] * 2 + [HBM] *...  5.52 us
    ppermute x1, waiting for transfers between devices, body(): bottom = lax.ppermute(up, 'rows', backward(ngroups))  4.55 us
    ppermute x1, starting transfers between devices, body(): top = lax.ppermute(down, 'rows', forward(ngroups))  4.33 us
    ppermute x1, waiting for transfers between devices, body(): right = lax.ppermute(strip, 'cols', backward(ncols))  3.75 us
    ppermute x1, starting transfers between devices, body(): left = lax.ppermute(strip, 'cols', forward(ncols))  3.55 us
    all_to_all x1, waiting for transfers between devices, body(): lax.all_to_all(payload, 'cols', split_axis=0, concat_axis=0, tiled=True)  2.46 us
    pallas_call x1, Pallas kernels, early_call(): call(early_kernel, [SMEM] + [VMEM] * 6, [(len(EARLY), NZ, LANES)])  2.4 us
  transfers between devices with their start and end apart: 5, of which 4 were waited for; matrix products, arithmetic and copies ran while one was open for 0% of the time, Pallas kernels for 12%

profile of v4, /device:TPU:63, one launch (start us, length us, event | category | flops | bytes accessed | tf_op | source)
XLA Modules:
  0.0 52.8 jit_solution(6210982278370787325)
XLA Ops:
  0.6 1.9 %shard_map.77 = f32[16,40,128]{2,1,0:T(8,128)} custom-call(s32[16]{0:T(128)} %bitcast.11, f32[16,32,128]{2,1,0:T(8,128)} %bitcast.7), custom_call_target="tpu_custom_call" | custom-call | flops 1048576 | bytes 1048576 | tf_op jit(solution)/shard_map/pallas_call | solution.py:429
  2.6 17.4 %all-to-all-start = ((f32[16,40,128]{2,1,0:T(8,128)}), f32[16,40,128]{2,1,0:T(8,128)S(1)}, u32[]{:S(2)}, u32[]{:S(2)}) async-start(f32[16,40,128]{2,1,0:T(8,128)} %shard_map.77), calls=%async_computation | async-start | bytes 655360 | tf_op jit(solution)/shard_map/all_to_all | solution.py:432
  19.9 1.3 %shard_map.78 = (f32[32,8,128]{2,1,0:T(8,128)S(1)}, f32[32,8,128]{2,1,0:T(8,128)S(1)}, f32[17,8,128]{2,1,0:T(8,128)S(1)}) custom-call(f32[8]{0:T(128)} %class_cond_hbm.1, f32[256,128]{1,0:T(8,128)} %bitcast.8, s32[256,128]{1,0:T(8,128)} %bitcast.9, s32[16,32]{1,0:T(8,128)} %bitcast.10), custom_call_target="tpu_custom_call" | custom-call | flops 1048576 | bytes 1048576 | tf_op jit(solution)/shard_map/pallas_call | solution.py:442
  21.2 2.0 %collective-permute-start.1 = (f32[17,8,128]{2,1,0:T(8,128)S(1)}, f32[17,8,128]{2,1,0:T(8,128)S(1)}, u32[]{:S(2)}, u32[]{:S(2)}) collective-permute-start(f32[17,8,128]{2,1,0:T(8,128)S(1)} %get-tuple-element.11.own_ref), channel_id=1, source_target_pairs={{1,0},{2,1},{3,2},{4,3},{5,4},{6,5},{7,6},{8,7},{9,8},{10,9},{11,1... | collective-permute-start | bytes 208904 | tf_op jit(solution)/shard_map/ppermute | solution.py:446
  23.2 3.5 %collective-permute-start = (f32[17,8,128]{2,1,0:T(8,128)S(1)}, f32[17,8,128]{2,1,0:T(8,128)S(1)}, u32[]{:S(2)}, u32[]{:S(2)}) collective-permute-start(f32[17,8,128]{2,1,0:T(8,128)S(1)} %get-tuple-element.11.own_ref), channel_id=1, source_target_pairs={{0,1},{1,2},{2,3},{3,4},{4,5},{5,6},{6,7},{7,8},{8,9},{9,10},{10,1... | collective-permute-start | bytes 208904 | tf_op jit(solution)/shard_map/ppermute | solution.py:445
  26.8 3.8 %collective-permute-done.1.right_ref = f32[17,8,128]{2,1,0:T(8,128)S(1)} collective-permute-done((f32[17,8,128]{2,1,0:T(8,128)S(1)}, f32[17,8,128]{2,1,0:T(8,128)S(1)}, u32[]{:S(2)}, u32[]{:S(2)}) %collective-permute-start.1) | collective-permute-done | bytes 69664 | tf_op jit(solution)/shard_map/ppermute | solution.py:446
  30.5 0.0 collective-permute-done.left_ref
  30.5 2.5 %all-to-all-done.incoming_ref = f32[16,40,128]{2,1,0:T(8,128)S(1)} async-done(((f32[16,40,128]{2,1,0:T(8,128)}), f32[16,40,128]{2,1,0:T(8,128)S(1)}, u32[]{:S(2)}, u32[]{:S(2)}) %all-to-all-start) | async-done | bytes 327712 | tf_op jit(solution)/shard_map/all_to_all | solution.py:432
  33.0 0.4 shard_map.79
  33.5 4.3 %collective-permute-start.3 = (f32[51,8,128]{2,1,0:T(8,128)S(1)}, f32[51,8,128]{2,1,0:T(8,128)S(1)}, u32[]{:S(2)}, u32[]{:S(2)}) collective-permute-start(f32[51,8,128]{2,1,0:T(8,128)S(1)} %get-tuple-element.17), channel_id=1, source_target_pairs={{0,16},{16,32},{32,48},{48,64},{64,80},{80,96},{96,112},{112,128},... | collective-permute-start | bytes 626696 | tf_op jit(solution)/shard_map/ppermute | solution.py:450
  37.8 1.9 %collective-permute-start.2 = (f32[51,8,128]{2,1,0:T(8,128)S(1)}, f32[51,8,128]{2,1,0:T(8,128)S(1)}, u32[]{:S(2)}, u32[]{:S(2)}) collective-permute-start(f32[51,8,128]{2,1,0:T(8,128)S(1)} %get-tuple-element.14), channel_id=1, source_target_pairs={{16,0},{32,16},{48,32},{64,48},{80,64},{96,80},{112,96},{128,112},... | collective-permute-start | bytes 626696 | tf_op jit(solution)/shard_map/ppermute | solution.py:451
  39.7 0.1 pad_add_fusion.place_ref
  39.8 2.4 %shard_map.80.early = f32[440,8,256]{2,1,0:T(8,128)S(1)} custom-call(s32[4]{0:T(128)S(1)} %pad_add_fusion.place_ref, f32[32,8,128]{2,1,0:T(8,128)S(1)} %get-tuple-element.12.head_ref, f32[32,8,128]{2,1,0:T(8,128)S(1)} %get-tuple-element.13.cond_ref, f32[32,8,128]{2,1,0:T(8,128)S(1)} %get-tuple-element.15.main_ref, ...), custom_call_target="tpu_custom_call" | custom-call | flops 1048576 | bytes 1048576 | tf_op jit(solution)/shard_map/pallas_call | solution.py:401
  42.2 0.5 collective-permute-done.3.sent_ref
  42.7 2.8 %shard_map.81 = (f32[8,32,128]{2,1,0:T(8,128)}, f32[8,32,128]{2,1,0:T(8,128)}) custom-call(s32[4]{0:T(128)S(1)} %pad_add_fusion.place_ref, f32[51,8,128]{2,1,0:T(8,128)S(1)} %collective-permute-done.3.sent_ref, f32[440,8,256]{2,1,0:T(8,128)S(1)} %shard_map.80.early), custom_call_target="tpu_custom_call" | custom-call | flops 1048576 | bytes 1048576 | tf_op jit(solution)/shard_map/pallas_call | solution.py:408
  45.5 4.5 %collective-permute-done.2.sent_ref = f32[51,8,128]{2,1,0:T(8,128)S(1)} collective-permute-done((f32[51,8,128]{2,1,0:T(8,128)S(1)}, f32[51,8,128]{2,1,0:T(8,128)S(1)}, u32[]{:S(2)}, u32[]{:S(2)}) %collective-permute-start.2) | collective-permute-done | bytes 208928 | tf_op jit(solution)/shard_map/ppermute | solution.py:451
  50.0 2.7 %shard_map.82 = (f32[8,32,128]{2,1,0:T(8,128)}, f32[8,32,128]{2,1,0:T(8,128)}) custom-call(s32[4]{0:T(128)S(1)} %pad_add_fusion.place_ref, f32[51,8,128]{2,1,0:T(8,128)S(1)} %collective-permute-done.2.sent_ref, f32[440,8,256]{2,1,0:T(8,128)S(1)} %shard_map.80.early, ...), custom_call_target="tpu_custom_call", output_to_operand_aliasing={{0}: (3, {}), {1}: (4, {})} | custom-call | flops 1048576 | bytes 1048576 | tf_op jit(solution)/shard_map/pallas_call | solution.py:408
Async XLA Ops:
  2.6 30.4 %all-to-all-start = ((f32[16,40,128]{2,1,0:T(8,128)}), f32[16,40,128]{2,1,0:T(8,128)S(1)}, u32[]{:S(2)}, u32[]{:S(2)}) async-start(f32[16,40,128]{2,1,0:T(8,128)} %shard_map.77), calls=%async_computation | async-start | bytes 655360 | tf_op jit(solution)/shard_map/all_to_all | solution.py:432
  21.2 9.3 %collective-permute-start.1 = (f32[17,8,128]{2,1,0:T(8,128)S(1)}, f32[17,8,128]{2,1,0:T(8,128)S(1)}, u32[]{:S(2)}, u32[]{:S(2)}) collective-permute-start(f32[17,8,128]{2,1,0:T(8,128)S(1)} %get-tuple-element.11.own_ref), channel_id=1, source_target_pairs={{1,0},{2,1},{3,2},{4,3},{5,4},{6,5},{7,6},{8,7},{9,8},{10,9},{11,1... | collective-permute-start | bytes 208904 | tf_op jit(solution)/shard_map/ppermute | solution.py:446
  23.2 7.3 %collective-permute-start = (f32[17,8,128]{2,1,0:T(8,128)S(1)}, f32[17,8,128]{2,1,0:T(8,128)S(1)}, u32[]{:S(2)}, u32[]{:S(2)}) collective-permute-start(f32[17,8,128]{2,1,0:T(8,128)S(1)} %get-tuple-element.11.own_ref), channel_id=1, source_target_pairs={{0,1},{1,2},{2,3},{3,4},{4,5},{5,6},{6,7},{7,8},{8,9},{9,10},{10,1... | collective-permute-start | bytes 208904 | tf_op jit(solution)/shard_map/ppermute | solution.py:445
  33.5 9.2 %collective-permute-start.3 = (f32[51,8,128]{2,1,0:T(8,128)S(1)}, f32[51,8,128]{2,1,0:T(8,128)S(1)}, u32[]{:S(2)}, u32[]{:S(2)}) collective-permute-start(f32[51,8,128]{2,1,0:T(8,128)S(1)} %get-tuple-element.17), channel_id=1, source_target_pairs={{0,16},{16,32},{32,48},{48,64},{64,80},{80,96},{96,112},{112,128},... | collective-permute-start | bytes 626696 | tf_op jit(solution)/shard_map/ppermute | solution.py:450
  37.8 12.2 %collective-permute-start.2 = (f32[51,8,128]{2,1,0:T(8,128)S(1)}, f32[51,8,128]{2,1,0:T(8,128)S(1)}, u32[]{:S(2)}, u32[]{:S(2)}) collective-permute-start(f32[51,8,128]{2,1,0:T(8,128)S(1)} %get-tuple-element.14), channel_id=1, source_target_pairs={{16,0},{32,16},{48,32},{64,48},{80,64},{96,80},{112,96},{128,112},... | collective-permute-start | bytes 626696 | tf_op jit(solution)/shard_map/ppermute | solution.py:451

commit v5 on v4

--- a/solution.py
+++ b/solution.py
@@ -72,7 +72,7 @@
         copy.wait()
 
 
-def fields_kernel(class_cond_hbm, head_hbm, class_hbm, ids_hbm, head_out, cond_out, strip_out,
+def fields_kernel(class_cond_hbm, head_hbm, class_hbm, ids_hbm, head_out, cond_out, right_out, left_out,
                   class_cond_ref, head_ref, class_ref, ids_ref, sems):
     pairs = (
         (head_hbm, head_ref), (class_hbm, class_ref), (class_cond_hbm, class_cond_ref), (ids_hbm, ids_ref)
@@ -84,6 +84,7 @@
         copy.wait()
     lane = lane_of((8, CX))
     values = [class_cond_ref[c] for c in range(8)]
+    blocks = []
     for block in range(CY // 4):
         heads, conds = [], []
         for q in range(4):
@@ -97,13 +98,30 @@
             cond_out[y] = cond
             heads.append(head)
             conds.append(cond)
-        strip_out[block] = packed(heads, lane)
-        strip_out[CY // 4 + block] = packed(conds, lane)
+        blocks.append((packed(heads, lane), packed(conds, lane)))
+    near = lane % 32 < HX
+    for f in range(2):
+        for i in range(CY // 8):
+            one, two = blocks[2 * i][f], blocks[2 * i + 1][f]
+            right_out[f * (CY // 8) + i] = jnp.where(near, one, pltpu.roll(two, HX, 1))
+            left_out[f * (CY // 8) + i] = jnp.where(near, pltpu.roll(one, CX - HX, 1), two)
     ids = ids_ref[...].astype(F32)
     count = ids.shape[0] // 4
-    strip_out[CY // 2] = jnp.zeros((8, CX), F32)
-    for r in range(count):
-        strip_out[CY // 2, r : r + 1, :] = jnp.concatenate([ids[4 * r + q : 4 * r + q + 1, :] for q in range(4)], axis=1)
+    for out in (right_out, left_out):
+        out[STRIP - 1] = jnp.zeros((8, CX), F32)
+        for r in range(count):
+            row = jnp.concatenate([ids[4 * r + q : 4 * r + q + 1, :] for q in range(4)], axis=1)
+            out[STRIP - 1, r : r + 1, :] = row
+
+
+STRIP = CY // 4 + 1
+
+
+def four_rows(left_ref, right_ref, f, i, lane):
+    left, right = left_ref[f * (CY // 8) + i // 2], right_ref[f * (CY // 8) + i // 2]
+    if i % 2 == 0:
+        return jnp.where(lane % 32 < HX, left, pltpu.roll(right, HX, 1))
+    return jnp.where(lane % 32 < HX, pltpu.roll(left, CX - HX, 1), right)
 
 
 def recharge_kernel(incoming_ref, own_ref, left_ref, right_ref, head_ref, cond_ref, main_out, halo_out, up_out, down_out):
@@ -124,7 +142,7 @@
         low = (values - high.astype(F32)).astype(jnp.bfloat16)
         return jnp.concatenate([high, low], axis=1)
 
-    own, left, right = own_ref[CY // 2], left_ref[CY // 2], right_ref[CY // 2]
+    own, left, right = own_ref[STRIP - 1], left_ref[STRIP - 1], right_ref[STRIP - 1]
     main = jnp.zeros((NZ * CY, LANES), F32)
     from_left = jnp.zeros((NZ * CY, LANES), F32)
     from_right = jnp.zeros((NZ * CY, LANES), F32)
@@ -153,8 +171,7 @@
         base = 2 * HY + RY
         for i in range(4):
             for f in range(2):
-                at = f * (CY // 4) + strip0 + i
-                out[base + 4 * f + i] = jnp.where(lane % 32 < HX, left_ref[at], right_ref[at])
+                out[base + 4 * f + i] = four_rows(left_ref, right_ref, f, strip0 + i, lane)
         for i in range(RY // 4):
             y = first + skip + 4 * i
             out[base + 8 + i] = packed([halo[y + q] for q in range(4)], lane)
@@ -320,9 +337,8 @@
     cycle = Cycle(place_ref, early)
     lane = lane_of((8, CX))
     for i in range(CY // 4):
-        at = CY // 4 + i
-        heads = jnp.where(lane % 32 < HX, left_ref[i], right_ref[i])
-        conds = 0.5 * jnp.where(lane % 32 < HX, left_ref[at], right_ref[at])
+        heads = four_rows(left_ref, right_ref, 0, i, lane)
+        conds = 0.5 * four_rows(left_ref, right_ref, 1, i, lane)
         for q in range(4):
             y = 4 * i + q
             cycle.put_parts("u0", HY + y, head_ref[y], unpacked(heads, q, lane))
@@ -332,7 +348,19 @@
 
 
 def late_kernel(side, place_ref, sent_ref, early, *refs):
-    head_hbm, residual_hbm, late, head_ref, residual_ref, sems = refs[-6:]
+    copies = []
+    if side == 0:
+        head_ref, residual_ref, late = refs
+    else:
+        upper_head, upper_residual, head_hbm, residual_hbm, late, head_ref, residual_ref, sems = refs
+        top, bottom = pl.ds(0, CY // 2), pl.ds(CY // 2, CY // 2)
+        pairs = (
+            (upper_head, head_hbm.at[:, top, :]), (upper_residual, residual_hbm.at[:, top, :]),
+            (head_ref, head_hbm.at[:, bottom, :]), (residual_ref, residual_hbm.at[:, bottom, :]),
+        )
+        copies = [pltpu.make_async_copy(a, b, sems.at[i]) for i, (a, b) in enumerate(pairs)]
+        copies[0].start()
+        copies[1].start()
     cycle = Cycle(place_ref, early, late, side)
     lane = lane_of((8, CX))
     base = 2 * HY + RY
@@ -346,23 +374,19 @@
     for i in range(RY):
         edge = unpacked(sent_ref[base + 8 + i // 4], i % 4, lane)
         cycle.put_parts("source", first + skip + i, sent_ref[2 * HY + i], edge)
-    own = pl.ds(side * (CY // 2), CY // 2)
-    copies = [
-        pltpu.make_async_copy(head_ref, head_hbm.at[:, own, :], sems.at[0]),
-        pltpu.make_async_copy(residual_ref, residual_hbm.at[:, own, :], sems.at[1]),
-    ]
-
     def leave(name, ref):
         for y in range(CY // 2):
             ref[:, y, :] = cycle.get(name, HY + side * (CY // 2) + y, 1)[0, :, 0:CX]
 
     def head_done():
         leave("u5", head_ref)
-        copies[0].start()
+        for copy in copies[2:3]:
+            copy.start()
 
     cycle.run(head_done)
     leave("residual", residual_ref)
-    copies[1].start()
+    for copy in copies[3:]:
+        copy.start()
     for copy in copies:
         copy.wait()
 
@@ -376,14 +400,13 @@
     return pltpu.with_memory_space_constraint(x, pltpu.HBM)
 
 
-def call(kernel, ins, outs, scratch=(), out=VMEM, aliases={}, flops=1 << 20, nbytes=1 << 20):
+def call(kernel, ins, outs, scratch=(), out=VMEM, flops=1 << 20, nbytes=1 << 20):
     return pl.pallas_call(
         kernel,
         out_shape=tuple(jax.ShapeDtypeStruct(s, F32) for s in outs),
         in_specs=ins,
         out_specs=tuple(out for _ in outs),
         scratch_shapes=scratch,
-        input_output_aliases=aliases,
         cost_estimate=pl.CostEstimate(flops=flops, bytes_accessed=nbytes, transcendentals=0),
         compiler_params=pltpu.CompilerParams(vmem_limit_bytes=32 << 20),
     )
@@ -403,16 +426,14 @@
     )[0]
 
 
-def late_call(side, place, sent, early, outs=()):
-    half = pltpu.VMEM((NZ, CY // 2, CX), F32)
-    return call(
-        functools.partial(late_kernel, side),
-        [SMEM] + [VMEM] * 2 + [HBM] * len(outs),
-        [(NZ, CY, CX)] * 2,
-        [pltpu.VMEM((len(LATE[side]), NZ, LANES), F32), half, half, pltpu.SemaphoreType.DMA((2,))],
-        HBM,
-        {3: 0, 4: 1} if outs else {},
-    )(place, sent, early, *outs)
+def late_call(side, place, sent, early, upper=()):
+    half = (NZ, CY // 2, CX)
+    late = pltpu.VMEM((len(LATE[side]), NZ, LANES), F32)
+    kernel, ins = functools.partial(late_kernel, side), [SMEM] + [VMEM] * (2 + len(upper))
+    if side == 0:
+        return call(kernel, ins, [half] * 2, [late])(place, sent, early)
+    scratch = [late] + [pltpu.VMEM(half, F32)] * 2 + [pltpu.SemaphoreType.DMA((4,))]
+    return call(kernel, ins, [(NZ, CY, CX)] * 2, scratch, HBM)(place, sent, early, *upper)
 
 
 def body(head_start, class_map, class_cond, partials, send_count, recv_block):
@@ -439,20 +460,20 @@
         pltpu.SemaphoreType.DMA((4,)),
     ]
     fields = (class_cond, head_start.reshape(flat), class_map.reshape(flat), recv_block.reshape(ncols, SLOTS))
-    head, cond, strip = call(fields_kernel, [HBM] * 4, [row, row, (CY // 2 + 1, 8, CX)], scratch)(
+    head, cond, to_right, to_left = call(fields_kernel, [HBM] * 4, [row, row] + [(STRIP, 8, CX)] * 2, scratch)(
         *(in_hbm(x) for x in fields)
     )
-    left = lax.ppermute(strip, "cols", forward(ncols))
-    right = lax.ppermute(strip, "cols", backward(ncols))
+    left = lax.ppermute(to_right, "cols", forward(ncols))
+    right = lax.ppermute(to_left, "cols", backward(ncols))
     main, halo, up, down = call(recharge_kernel, [VMEM] * 6, [row, row, sent, sent])(
-        incoming, strip, left, right, head, cond
+        incoming, to_right, left, right, head, cond
     )
     top = lax.ppermute(down, "rows", forward(ngroups))
     bottom = lax.ppermute(up, "rows", backward(ngroups))
     place = jnp.stack([lax.axis_index("rows"), lax.axis_index("cols"), ngroups, ncols]).astype(jnp.int32)
     early = early_call(place, head, cond, main, halo, left, right)
-    outs = late_call(0, place, top, early)
-    return tuple(late_call(1, place, bottom, early, outs))
+    upper = late_call(0, place, top, early)
+    return tuple(late_call(1, place, bottom, early, upper))
 
 
 def solution(mesh):

time: 53.1 us -> 53.1 us (level)
    ppermute x1, waiting for transfers between devices: 4.55 us -> 5.17 us  [body(): bottom = lax.ppermute(up, 'rows', backward(ngroups))]
    pallas_call x3, Pallas kernels: 6.78 us -> 6.22 us  [the longest x1 2.77 us: late_call(): call(kernel, ins, [(NZ, CY, CX)] * 2, scratch, HBM)]
  transfers between devices with their start and end apart: 5 -> 5, of which waited for: 4 -> 4; matrix products, arithmetic and copies ran while one was open for 0% -> 0% of each run, Pallas kernels for 12% -> 11%
where the time goes in v5:
time: 53.1 us; the launch traced here: 52.8 us
  starting transfers between devices  29.2 us (55%)
  waiting for transfers between devices  11.7 us (22%)
  Pallas kernels  11.1 us (21%)
  between operations  0.7 us (1%)
    all_to_all x1, starting transfers between devices, body(): lax.all_to_all(payload, 'cols', split_axis=0, concat_axis=0, tiled=True)  17.4 us
    ppermute x1, waiting for transfers between devices, body(): bottom = lax.ppermute(up, 'rows', backward(ngroups))  5.17 us
    ppermute x1, starting transfers between devices, body(): top = lax.ppermute(down, 'rows', forward(ngroups))  4.33 us
    ppermute x1, starting transfers between devices, body(): left = lax.ppermute(to_right, 'cols', forward(ncols))  3.55 us
    ppermute x1, waiting for transfers between devices, body(): right = lax.ppermute(to_left, 'cols', backward(ncols))  3.33 us
    all_to_all x1, waiting for transfers between devices, body(): lax.all_to_all(payload, 'cols', split_axis=0, concat_axis=0, tiled=True)  2.82 us
    pallas_call x1, Pallas kernels, late_call(): call(kernel, ins, [(NZ, CY, CX)] * 2, scratch, HBM)  2.77 us
    pallas_call x1, Pallas kernels, early_call(): call(early_kernel, [SMEM] + [VMEM] * 6, [(len(EARLY), NZ, LANES)])  2.5 us
  transfers between devices with their start and end apart: 5, of which 4 were waited for; matrix products, arithmetic and copies ran while one was open for 0% of the time, Pallas kernels for 11%

profile of v5, /device:TPU:63, one launch (start us, length us, event | category | flops | bytes accessed | tf_op | source)
XLA Modules:
  0.0 52.8 jit_solution(6018553931038919724)
XLA Ops:
  0.6 1.9 %shard_map.77 = f32[16,40,128]{2,1,0:T(8,128)} custom-call(s32[16]{0:T(128)} %bitcast.11, f32[16,32,128]{2,1,0:T(8,128)} %bitcast.7), custom_call_target="tpu_custom_call" | custom-call | flops 1048576 | bytes 1048576 | tf_op jit(solution)/shard_map/pallas_call | solution.py:450
  2.6 17.4 %all-to-all-start = ((f32[16,40,128]{2,1,0:T(8,128)}), f32[16,40,128]{2,1,0:T(8,128)S(1)}, u32[]{:S(2)}, u32[]{:S(2)}) async-start(f32[16,40,128]{2,1,0:T(8,128)} %shard_map.77), calls=%async_computation | async-start | bytes 655360 | tf_op jit(solution)/shard_map/all_to_all | solution.py:453
  19.9 1.3 %shard_map.78 = (f32[32,8,128]{2,1,0:T(8,128)S(1)}, f32[32,8,128]{2,1,0:T(8,128)S(1)}, f32[9,8,128]{2,1,0:T(8,128)S(1)}, f32[9,8,128]{2,1,0:T(8,128)S(1)}) custom-call(f32[8]{0:T(128)} %class_cond_hbm.1, f32[256,128]{1,0:T(8,128)} %bitcast.8, s32[256,128]{1,0:T(8,128)} %bitcast.9, s32[16,32]{1,0:T(8,128)} %bitcast.10), custom_call_target="tpu_custom_call" | custom-call | flops 1048576 | bytes 1048576 | tf_op jit(solution)/shard_map/pallas_call | solution.py:463
  21.3 2.0 %collective-permute-start.1 = (f32[9,8,128]{2,1,0:T(8,128)S(1)}, f32[9,8,128]{2,1,0:T(8,128)S(1)}, u32[]{:S(2)}, u32[]{:S(2)}) collective-permute-start(f32[9,8,128]{2,1,0:T(8,128)S(1)} %get-tuple-element.13), channel_id=1, source_target_pairs={{1,0},{2,1},{3,2},{4,3},{5,4},{6,5},{7,6},{8,7},{9,8},{10,9},{11,1... | collective-permute-start | bytes 110600 | tf_op jit(solution)/shard_map/ppermute | solution.py:467
  23.3 3.5 %collective-permute-start = (f32[9,8,128]{2,1,0:T(8,128)S(1)}, f32[9,8,128]{2,1,0:T(8,128)S(1)}, u32[]{:S(2)}, u32[]{:S(2)}) collective-permute-start(f32[9,8,128]{2,1,0:T(8,128)S(1)} %get-tuple-element.12.own_ref), channel_id=1, source_target_pairs={{0,1},{1,2},{2,3},{3,4},{4,5},{5,6},{6,7},{7,8},{8,9},{9,10},{10,1... | collective-permute-start | bytes 110600 | tf_op jit(solution)/shard_map/ppermute | solution.py:466
  26.9 3.3 %collective-permute-done.1.right_ref = f32[9,8,128]{2,1,0:T(8,128)S(1)} collective-permute-done((f32[9,8,128]{2,1,0:T(8,128)S(1)}, f32[9,8,128]{2,1,0:T(8,128)S(1)}, u32[]{:S(2)}, u32[]{:S(2)}) %collective-permute-start.1) | collective-permute-done | bytes 36896 | tf_op jit(solution)/shard_map/ppermute | solution.py:467
  30.2 0.0 collective-permute-done.left_ref
  30.2 2.8 %all-to-all-done.incoming_ref = f32[16,40,128]{2,1,0:T(8,128)S(1)} async-done(((f32[16,40,128]{2,1,0:T(8,128)}), f32[16,40,128]{2,1,0:T(8,128)S(1)}, u32[]{:S(2)}, u32[]{:S(2)}) %all-to-all-start) | async-done | bytes 327712 | tf_op jit(solution)/shard_map/all_to_all | solution.py:453
  33.0 0.4 shard_map.79
  33.5 4.3 %collective-permute-start.3 = (f32[51,8,128]{2,1,0:T(8,128)S(1)}, f32[51,8,128]{2,1,0:T(8,128)S(1)}, u32[]{:S(2)}, u32[]{:S(2)}) collective-permute-start(f32[51,8,128]{2,1,0:T(8,128)S(1)} %get-tuple-element.19), channel_id=1, source_target_pairs={{0,16},{16,32},{32,48},{48,64},{64,80},{80,96},{96,112},{112,128},... | collective-permute-start | bytes 626696 | tf_op jit(solution)/shard_map/ppermute | solution.py:471
  37.8 1.9 %collective-permute-start.2 = (f32[51,8,128]{2,1,0:T(8,128)S(1)}, f32[51,8,128]{2,1,0:T(8,128)S(1)}, u32[]{:S(2)}, u32[]{:S(2)}) collective-permute-start(f32[51,8,128]{2,1,0:T(8,128)S(1)} %get-tuple-element.16), channel_id=1, source_target_pairs={{16,0},{32,16},{48,32},{64,48},{80,64},{96,80},{112,96},{128,112},... | collective-permute-start | bytes 626696 | tf_op jit(solution)/shard_map/ppermute | solution.py:472
  39.7 0.1 pad_add_fusion.place_ref
  39.8 2.5 %shard_map.80.early = f32[440,8,256]{2,1,0:T(8,128)S(1)} custom-call(s32[4]{0:T(128)S(1)} %pad_add_fusion.place_ref, f32[32,8,128]{2,1,0:T(8,128)S(1)} %get-tuple-element.14.head_ref, f32[32,8,128]{2,1,0:T(8,128)S(1)} %get-tuple-element.15.cond_ref, f32[32,8,128]{2,1,0:T(8,128)S(1)} %get-tuple-element.17.main_ref, ...), custom_call_target="tpu_custom_call" | custom-call | flops 1048576 | bytes 1048576 | tf_op jit(solution)/shard_map/pallas_call | solution.py:424
  42.3 0.4 collective-permute-done.3.sent_ref
  42.7 2.1 %shard_map.81 = (f32[8,16,128]{2,1,0:T(8,128)S(1)}, f32[8,16,128]{2,1,0:T(8,128)S(1)}) custom-call(s32[4]{0:T(128)S(1)} %pad_add_fusion.place_ref, f32[51,8,128]{2,1,0:T(8,128)S(1)} %collective-permute-done.3.sent_ref, f32[440,8,256]{2,1,0:T(8,128)S(1)} %shard_map.80.early), custom_call_target="tpu_custom_call" | custom-call | flops 1048576 | bytes 1048576 | tf_op jit(solution)/shard_map/pallas_call | solution.py:434
  44.9 5.2 %collective-permute-done.2.sent_ref = f32[51,8,128]{2,1,0:T(8,128)S(1)} collective-permute-done((f32[51,8,128]{2,1,0:T(8,128)S(1)}, f32[51,8,128]{2,1,0:T(8,128)S(1)}, u32[]{:S(2)}, u32[]{:S(2)}) %collective-permute-start.2) | collective-permute-done | bytes 208928 | tf_op jit(solution)/shard_map/ppermute | solution.py:472
  50.0 2.8 %shard_map.82 = (f32[8,32,128]{2,1,0:T(8,128)}, f32[8,32,128]{2,1,0:T(8,128)}) custom-call(s32[4]{0:T(128)S(1)} %pad_add_fusion.place_ref, f32[51,8,128]{2,1,0:T(8,128)S(1)} %collective-permute-done.2.sent_ref, f32[440,8,256]{2,1,0:T(8,128)S(1)} %shard_map.80.early, f32[8,16,128]{2,1,0:T(8,128)S(1)} %get-tuple-element.20.refs_0_, ...), custom_call_target="tpu_custom_call" | custom-call | flops 1048576 | bytes 1048576 | tf_op jit(solution)/shard_map/pallas_call | solution.py:436
Async XLA Ops:
  2.6 30.5 %all-to-all-start = ((f32[16,40,128]{2,1,0:T(8,128)}), f32[16,40,128]{2,1,0:T(8,128)S(1)}, u32[]{:S(2)}, u32[]{:S(2)}) async-start(f32[16,40,128]{2,1,0:T(8,128)} %shard_map.77), calls=%async_computation | async-start | bytes 655360 | tf_op jit(solution)/shard_map/all_to_all | solution.py:453
  21.3 8.9 %collective-permute-start.1 = (f32[9,8,128]{2,1,0:T(8,128)S(1)}, f32[9,8,128]{2,1,0:T(8,128)S(1)}, u32[]{:S(2)}, u32[]{:S(2)}) collective-permute-start(f32[9,8,128]{2,1,0:T(8,128)S(1)} %get-tuple-element.13), channel_id=1, source_target_pairs={{1,0},{2,1},{3,2},{4,3},{5,4},{6,5},{7,6},{8,7},{9,8},{10,9},{11,1... | collective-permute-start | bytes 110600 | tf_op jit(solution)/shard_map/ppermute | solution.py:467
  23.3 6.9 %collective-permute-start = (f32[9,8,128]{2,1,0:T(8,128)S(1)}, f32[9,8,128]{2,1,0:T(8,128)S(1)}, u32[]{:S(2)}, u32[]{:S(2)}) collective-permute-start(f32[9,8,128]{2,1,0:T(8,128)S(1)} %get-tuple-element.12.own_ref), channel_id=1, source_target_pairs={{0,1},{1,2},{2,3},{3,4},{4,5},{5,6},{6,7},{7,8},{8,9},{9,10},{10,1... | collective-permute-start | bytes 110600 | tf_op jit(solution)/shard_map/ppermute | solution.py:466
  33.5 9.3 %collective-permute-start.3 = (f32[51,8,128]{2,1,0:T(8,128)S(1)}, f32[51,8,128]{2,1,0:T(8,128)S(1)}, u32[]{:S(2)}, u32[]{:S(2)}) collective-permute-start(f32[51,8,128]{2,1,0:T(8,128)S(1)} %get-tuple-element.19), channel_id=1, source_target_pairs={{0,16},{16,32},{32,48},{48,64},{64,80},{80,96},{96,112},{112,128},... | collective-permute-start | bytes 626696 | tf_op jit(solution)/shard_map/ppermute | solution.py:471
  37.8 12.2 %collective-permute-start.2 = (f32[51,8,128]{2,1,0:T(8,128)S(1)}, f32[51,8,128]{2,1,0:T(8,128)S(1)}, u32[]{:S(2)}, u32[]{:S(2)}) collective-permute-start(f32[51,8,128]{2,1,0:T(8,128)S(1)} %get-tuple-element.16), channel_id=1, source_target_pairs={{16,0},{32,16},{48,32},{64,48},{80,64},{96,80},{112,96},{128,112},... | collective-permute-start | bytes 626696 | tf_op jit(solution)/shard_map/ppermute | solution.py:472

commit v6 on v5

--- a/solution.py
+++ b/solution.py
@@ -72,7 +72,7 @@
         copy.wait()
 
 
-def fields_kernel(class_cond_hbm, head_hbm, class_hbm, ids_hbm, head_out, cond_out, right_out, left_out,
+def fields_kernel(class_cond_hbm, head_hbm, class_hbm, ids_hbm, head_out, cond_out, right_out, left_out, edge_out,
                   class_cond_ref, head_ref, class_ref, ids_ref, sems):
     pairs = (
         (head_hbm, head_ref), (class_hbm, class_ref), (class_cond_hbm, class_cond_ref), (ids_hbm, ids_ref)
@@ -96,6 +96,9 @@
                 cond = jnp.where(kind == c, values[c], cond)
             head_out[y] = head
             cond_out[y] = cond
+            if y < HY:
+                edge_out[y] = head
+                edge_out[HY + y] = cond
             heads.append(head)
             conds.append(cond)
         blocks.append((packed(heads, lane), packed(conds, lane)))
@@ -124,7 +127,8 @@
     return jnp.where(lane % 32 < HX, pltpu.roll(left, CX - HX, 1), right)
 
 
-def recharge_kernel(incoming_ref, own_ref, left_ref, right_ref, head_ref, cond_ref, main_out, halo_out, up_out, down_out):
+def recharge_kernel(incoming_ref, own_ref, left_ref, right_ref, head_ref, cond_ref, _,
+                    main_out, halo_out, up_out, down_out):
     ncols = incoming_ref.shape[0]
     total = ncols * SLOTS
     chunk = min(256, total)
@@ -163,12 +167,13 @@
     halo = jnp.where(wide >= CX - HX, from_left, jnp.where(wide < HX, from_right, 0.0))
     main_out[...] = main
     halo_out[...] = halo
-    for out, first, strip0 in ((up_out, 0, 0), (down_out, CY - HY, CY // 4 - 4)):
+    for out, first, strip0, base in ((up_out, 0, 0, 0), (down_out, CY - HY, CY // 4 - 4, 2 * HY)):
         skip = first and HY - RY
-        out[0:HY] = head_ref[first : first + HY]
-        out[HY : 2 * HY] = cond_ref[first : first + HY]
-        out[2 * HY : 2 * HY + RY] = main[first + skip : first + skip + RY]
-        base = 2 * HY + RY
+        if base:
+            out[0:HY] = head_ref[first : first + HY]
+            out[HY : 2 * HY] = cond_ref[first : first + HY]
+        out[base : base + RY] = main[first + skip : first + skip + RY]
+        base = base + RY
         for i in range(4):
             for f in range(2):
                 out[base + 4 * f + i] = four_rows(left_ref, right_ref, f, strip0 + i, lane)
@@ -177,7 +182,8 @@
             out[base + 8 + i] = packed([halo[y + q] for q in range(4)], lane)
 
 
-SENT = 2 * HY + RY + 8 + RY // 4
+EDGE, UP = 2 * HY, RY + 8 + RY // 4
+DOWN = EDGE + UP
 
 
 def span(first, last):
@@ -351,8 +357,9 @@
     copies = []
     if side == 0:
         head_ref, residual_ref, late = refs
+        edge_ref = sent_ref
     else:
-        upper_head, upper_residual, head_hbm, residual_hbm, late, head_ref, residual_ref, sems = refs
+        edge_ref, upper_head, upper_residual, head_hbm, residual_hbm, late, head_ref, residual_ref, sems = refs
         top, bottom = pl.ds(0, CY // 2), pl.ds(CY // 2, CY // 2)
         pairs = (
             (upper_head, head_hbm.at[:, top, :]), (upper_residual, residual_hbm.at[:, top, :]),
@@ -363,17 +370,18 @@
         copies[1].start()
     cycle = Cycle(place_ref, early, late, side)
     lane = lane_of((8, CX))
-    base = 2 * HY + RY
+    base, source = (EDGE + RY, EDGE) if side == 0 else (RY, 0)
     first, shift, skip = ((0, 2, HY - RY), (HY + CY, 0, 0))[side]
     for i in range(HY):
         at, q = (i + shift) // 4, (i + shift) % 4
         if first + i in NEEDED["u0"][0]:
-            cycle.put_parts("u0", first + i, sent_ref[i], unpacked(sent_ref[base + at], q, lane))
-            half = 0.5 * sent_ref[HY + i]
+            cycle.put_parts("u0", first + i, edge_ref[i], unpacked(sent_ref[base + at], q, lane))
+            half = 0.5 * edge_ref[HY + i]
             cycle.put_parts("half", first + i, half, 0.5 * unpacked(sent_ref[base + 4 + at], q, lane))
     for i in range(RY):
         edge = unpacked(sent_ref[base + 8 + i // 4], i % 4, lane)
-        cycle.put_parts("source", first + skip + i, sent_ref[2 * HY + i], edge)
+        cycle.put_parts("source", first + skip + i, sent_ref[source + i], edge)
+
     def leave(name, ref):
         for y in range(CY // 2):
             ref[:, y, :] = cycle.get(name, HY + side * (CY // 2) + y, 1)[0, :, 0:CX]
@@ -394,6 +402,7 @@
 VMEM = pl.BlockSpec(memory_space=pltpu.VMEM)
 SMEM = pl.BlockSpec(memory_space=pltpu.SMEM)
 HBM = pl.BlockSpec(memory_space=pltpu.HBM)
+ANY = pl.BlockSpec(memory_space=pl.ANY)
 
 
 def in_hbm(x):
@@ -426,19 +435,19 @@
     )[0]
 
 
-def late_call(side, place, sent, early, upper=()):
+def late_call(side, place, sent, early, others=()):
     half = (NZ, CY // 2, CX)
     late = pltpu.VMEM((len(LATE[side]), NZ, LANES), F32)
-    kernel, ins = functools.partial(late_kernel, side), [SMEM] + [VMEM] * (2 + len(upper))
+    kernel, ins = functools.partial(late_kernel, side), [SMEM] + [VMEM] * (2 + len(others))
     if side == 0:
         return call(kernel, ins, [half] * 2, [late])(place, sent, early)
     scratch = [late] + [pltpu.VMEM(half, F32)] * 2 + [pltpu.SemaphoreType.DMA((4,))]
-    return call(kernel, ins, [(NZ, CY, CX)] * 2, scratch, HBM)(place, sent, early, *upper)
+    return call(kernel, ins, [(NZ, CY, CX)] * 2, scratch, HBM)(place, sent, early, *others)
 
 
 def body(head_start, class_map, class_cond, partials, send_count, recv_block):
     ngroups, ncols = lax.axis_size("rows"), lax.axis_size("cols")
-    row, sent = (CY, NZ, CX), (SENT, 8, CX)
+    row = (CY, NZ, CX)
     scratch = [
         pltpu.SMEM((ncols,), jnp.int32),
         pltpu.VMEM((ncols, SLOTS, CX), F32),
@@ -460,20 +469,22 @@
         pltpu.SemaphoreType.DMA((4,)),
     ]
     fields = (class_cond, head_start.reshape(flat), class_map.reshape(flat), recv_block.reshape(ncols, SLOTS))
-    head, cond, to_right, to_left = call(fields_kernel, [HBM] * 4, [row, row] + [(STRIP, 8, CX)] * 2, scratch)(
+    sizes = [row, row] + [(STRIP, 8, CX)] * 2 + [(EDGE, 8, CX)]
+    head, cond, to_right, to_left, edge = call(fields_kernel, [HBM] * 4, sizes, scratch)(
         *(in_hbm(x) for x in fields)
     )
     left = lax.ppermute(to_right, "cols", forward(ncols))
     right = lax.ppermute(to_left, "cols", backward(ncols))
-    main, halo, up, down = call(recharge_kernel, [VMEM] * 6, [row, row, sent, sent])(
-        incoming, to_right, left, right, head, cond
+    edge = lax.ppermute(edge, "rows", backward(ngroups))
+    main, halo, up, down = call(recharge_kernel, [VMEM] * 6 + [ANY], [row, row, (UP, 8, CX), (DOWN, 8, CX)])(
+        incoming, to_right, left, right, head, cond, edge
     )
     top = lax.ppermute(down, "rows", forward(ngroups))
     bottom = lax.ppermute(up, "rows", backward(ngroups))
     place = jnp.stack([lax.axis_index("rows"), lax.axis_index("cols"), ngroups, ncols]).astype(jnp.int32)
     early = early_call(place, head, cond, main, halo, left, right)
     upper = late_call(0, place, top, early)
-    return tuple(late_call(1, place, bottom, early, upper))
+    return tuple(late_call(1, place, bottom, early, (edge, *upper)))
 
 
 def solution(mesh):

time: 53.1 us -> 50.9 us (0.959)
  the two profiles are of different devices: /device:TPU:63 before, /device:TPU:65 now
where the time goes in v6:
time: 50.9 us; the launch traced here: 50.5 us
  starting transfers between devices  36 us (71%)
  Pallas kernels  11.1 us (22%)
  waiting for transfers between devices  2.64 us (5%)
  between operations  0.73 us (1%)
    all_to_all x1, starting transfers between devices, body(): lax.all_to_all(payload, 'cols', split_axis=0, concat_axis=0, tiled=True)  17.4 us
    ppermute x1, starting transfers between devices, body(): bottom = lax.ppermute(up, 'rows', backward(ngroups))  5.48 us
    ppermute x1, starting transfers between devices, body(): edge = lax.ppermute(edge, 'rows', backward(ngroups))  4.3 us
    ppermute x1, starting transfers between devices, body(): left = lax.ppermute(to_right, 'cols', forward(ncols))  3.45 us
    ppermute x1, starting transfers between devices, body(): top = lax.ppermute(down, 'rows', forward(ngroups))  3.12 us
    pallas_call x1, Pallas kernels, late_call(): call(kernel, ins, [(NZ, CY, CX)] * 2, scratch, HBM)  2.77 us
    pallas_call x1, Pallas kernels, early_call(): call(early_kernel, [SMEM] + [VMEM] * 6, [(len(EARLY), NZ, LANES)])  2.5 us
    ppermute x1, starting transfers between devices, body(): right = lax.ppermute(to_left, 'cols', backward(ncols))  2.27 us
  transfers between devices with their start and end apart: 6, of which 3 were waited for; matrix products, arithmetic and copies ran while one was open for 0% of the time, Pallas kernels for 12%

profile of v6, /device:TPU:65, one launch (start us, length us, event | category | flops | bytes accessed | tf_op | source)
XLA Modules:
  0.0 50.5 jit_solution(18430642935238969989)
XLA Ops:
  0.6 1.9 %shard_map.77 = f32[16,40,128]{2,1,0:T(8,128)} custom-call(s32[16]{0:T(128)} %bitcast.11, f32[16,32,128]{2,1,0:T(8,128)} %bitcast.7), custom_call_target="tpu_custom_call" | custom-call | flops 1048576 | bytes 1048576 | tf_op jit(solution)/shard_map/pallas_call | solution.py:459
  2.5 17.4 %all-to-all-start = ((f32[16,40,128]{2,1,0:T(8,128)}), f32[16,40,128]{2,1,0:T(8,128)S(1)}, u32[]{:S(2)}, u32[]{:S(2)}) async-start(f32[16,40,128]{2,1,0:T(8,128)} %shard_map.77), calls=%async_computation | async-start | bytes 655360 | tf_op jit(solution)/shard_map/all_to_all | solution.py:462
  19.9 1.3 %shard_map.78 = (f32[32,8,128]{2,1,0:T(8,128)S(1)}, f32[32,8,128]{2,1,0:T(8,128)S(1)}, f32[9,8,128]{2,1,0:T(8,128)S(1)}, f32[9,8,128]{2,1,0:T(8,128)S(1)}, f32[28,8,128]{2,1,0:T(8,128)S(1)}) custom-call(f32[8]{0:T(128)} %class_cond_hbm.1, f32[256,128]{1,0:T(8,128)} %bitcast.8, s32[256,128]{1,0:T(8,128)} %bitcast.9, s32[16,32]{1,0:T(8,128)} %bitcast.10), custom_call_target="tpu_custom_call" | custom-call | flops 1048576 | bytes 1048576 | tf_op jit(solution)/shard_map/pallas_call | solution.py:473
  21.3 4.3 %collective-permute-start.2 = (f32[28,8,128]{2,1,0:T(8,128)S(1)}, f32[28,8,128]{2,1,0:T(8,128)S(1)}, u32[]{:S(2)}, u32[]{:S(2)}) collective-permute-start(f32[28,8,128]{2,1,0:T(8,128)S(1)} %get-tuple-element.17), channel_id=1, source_target_pairs={{16,0},{32,16},{48,32},{64,48},{80,64},{96,80},{112,96},{128,112},... | collective-permute-start | bytes 344072 | tf_op jit(solution)/shard_map/ppermute | solution.py:478
  25.6 2.3 %collective-permute-start.1 = (f32[9,8,128]{2,1,0:T(8,128)S(1)}, f32[9,8,128]{2,1,0:T(8,128)S(1)}, u32[]{:S(2)}, u32[]{:S(2)}) collective-permute-start(f32[9,8,128]{2,1,0:T(8,128)S(1)} %get-tuple-element.14), channel_id=1, source_target_pairs={{1,0},{2,1},{3,2},{4,3},{5,4},{6,5},{7,6},{8,7},{9,8},{10,9},{11,1... | collective-permute-start | bytes 110600 | tf_op jit(solution)/shard_map/ppermute | solution.py:477
  27.9 3.4 %collective-permute-start = (f32[9,8,128]{2,1,0:T(8,128)S(1)}, f32[9,8,128]{2,1,0:T(8,128)S(1)}, u32[]{:S(2)}, u32[]{:S(2)}) collective-permute-start(f32[9,8,128]{2,1,0:T(8,128)S(1)} %get-tuple-element.13.own_ref), channel_id=1, source_target_pairs={{0,1},{1,2},{2,3},{3,4},{4,5},{5,6},{6,7},{7,8},{8,9},{9,10},{10,1... | collective-permute-start | bytes 110600 | tf_op jit(solution)/shard_map/ppermute | solution.py:476
  31.3 0.0 collective-permute-done.1.right_ref
  31.3 1.0 %collective-permute-done.left_ref = f32[9,8,128]{2,1,0:T(8,128)S(1)} collective-permute-done((f32[9,8,128]{2,1,0:T(8,128)S(1)}, f32[9,8,128]{2,1,0:T(8,128)S(1)}, u32[]{:S(2)}, u32[]{:S(2)}) %collective-permute-start) | collective-permute-done | bytes 36896 | tf_op jit(solution)/shard_map/ppermute | solution.py:476
  32.4 0.0 collective-permute-done.2._.refs_0_
  32.4 0.6 %all-to-all-done.incoming_ref = f32[16,40,128]{2,1,0:T(8,128)S(1)} async-done(((f32[16,40,128]{2,1,0:T(8,128)}), f32[16,40,128]{2,1,0:T(8,128)S(1)}, u32[]{:S(2)}, u32[]{:S(2)}) %all-to-all-start) | async-done | bytes 327712 | tf_op jit(solution)/shard_map/all_to_all | solution.py:462
  33.0 0.4 shard_map.79
  33.4 3.1 %collective-permute-start.4 = (f32[51,8,128]{2,1,0:T(8,128)S(1)}, f32[51,8,128]{2,1,0:T(8,128)S(1)}, u32[]{:S(2)}, u32[]{:S(2)}) collective-permute-start(f32[51,8,128]{2,1,0:T(8,128)S(1)} %get-tuple-element.21), channel_id=1, source_target_pairs={{0,16},{16,32},{32,48},{48,64},{64,80},{80,96},{96,112},{112,128},... | collective-permute-start | bytes 626696 | tf_op jit(solution)/shard_map/ppermute | solution.py:482
  36.6 5.5 %collective-permute-start.3 = (f32[23,8,128]{2,1,0:T(8,128)S(1)}, f32[23,8,128]{2,1,0:T(8,128)S(1)}, u32[]{:S(2)}, u32[]{:S(2)}) collective-permute-start(f32[23,8,128]{2,1,0:T(8,128)S(1)} %get-tuple-element.18), channel_id=1, source_target_pairs={{16,0},{32,16},{48,32},{64,48},{80,64},{96,80},{112,96},{128,112},... | collective-permute-start | bytes 282632 | tf_op jit(solution)/shard_map/ppermute | solution.py:483
  42.1 0.1 pad_add_fusion.place_ref
  42.2 2.5 %shard_map.80.early = f32[440,8,256]{2,1,0:T(8,128)S(1)} custom-call(s32[4]{0:T(128)S(1)} %pad_add_fusion.place_ref, f32[32,8,128]{2,1,0:T(8,128)S(1)} %get-tuple-element.15.head_ref, f32[32,8,128]{2,1,0:T(8,128)S(1)} %get-tuple-element.16.cond_ref, f32[32,8,128]{2,1,0:T(8,128)S(1)} %get-tuple-element.19.main_ref, ...), custom_call_target="tpu_custom_call" | custom-call | flops 1048576 | bytes 1048576 | tf_op jit(solution)/shard_map/pallas_call | solution.py:433
  44.7 1.0 %collective-permute-done.4.sent_ref = f32[51,8,128]{2,1,0:T(8,128)S(1)} collective-permute-done((f32[51,8,128]{2,1,0:T(8,128)S(1)}, f32[51,8,128]{2,1,0:T(8,128)S(1)}, u32[]{:S(2)}, u32[]{:S(2)}) %collective-permute-start.4) | collective-permute-done | bytes 208928 | tf_op jit(solution)/shard_map/ppermute | solution.py:482
  45.6 2.1 %shard_map.81 = (f32[8,16,128]{2,1,0:T(8,128)S(1)}, f32[8,16,128]{2,1,0:T(8,128)S(1)}) custom-call(s32[4]{0:T(128)S(1)} %pad_add_fusion.place_ref, f32[51,8,128]{2,1,0:T(8,128)S(1)} %collective-permute-done.4.sent_ref, f32[440,8,256]{2,1,0:T(8,128)S(1)} %shard_map.80.early), custom_call_target="tpu_custom_call" | custom-call | flops 1048576 | bytes 1048576 | tf_op jit(solution)/shard_map/pallas_call | solution.py:443
  47.7 0.0 collective-permute-done.3.sent_ref
  47.8 2.8 %shard_map.82 = (f32[8,32,128]{2,1,0:T(8,128)}, f32[8,32,128]{2,1,0:T(8,128)}) custom-call(s32[4]{0:T(128)S(1)} %pad_add_fusion.place_ref, f32[23,8,128]{2,1,0:T(8,128)S(1)} %collective-permute-done.3.sent_ref, f32[440,8,256]{2,1,0:T(8,128)S(1)} %shard_map.80.early, f32[28,8,128]{2,1,0:T(8,128)S(1)} %collective-permute-done.2._.refs_0_, ...), custom_call_target="tpu_custom_call" | custom-call | flops 1048576 | bytes 1048576 | tf_op jit(solution)/shard_map/pallas_call | solution.py:445
Async XLA Ops:
  2.5 30.4 %all-to-all-start = ((f32[16,40,128]{2,1,0:T(8,128)}), f32[16,40,128]{2,1,0:T(8,128)S(1)}, u32[]{:S(2)}, u32[]{:S(2)}) async-start(f32[16,40,128]{2,1,0:T(8,128)} %shard_map.77), calls=%async_computation | async-start | bytes 655360 | tf_op jit(solution)/shard_map/all_to_all | solution.py:462
  21.3 11.1 %collective-permute-start.2 = (f32[28,8,128]{2,1,0:T(8,128)S(1)}, f32[28,8,128]{2,1,0:T(8,128)S(1)}, u32[]{:S(2)}, u32[]{:S(2)}) collective-permute-start(f32[28,8,128]{2,1,0:T(8,128)S(1)} %get-tuple-element.17), channel_id=1, source_target_pairs={{16,0},{32,16},{48,32},{64,48},{80,64},{96,80},{112,96},{128,112},... | collective-permute-start | bytes 344072 | tf_op jit(solution)/shard_map/ppermute | solution.py:478
  25.6 5.7 %collective-permute-start.1 = (f32[9,8,128]{2,1,0:T(8,128)S(1)}, f32[9,8,128]{2,1,0:T(8,128)S(1)}, u32[]{:S(2)}, u32[]{:S(2)}) collective-permute-start(f32[9,8,128]{2,1,0:T(8,128)S(1)} %get-tuple-element.14), channel_id=1, source_target_pairs={{1,0},{2,1},{3,2},{4,3},{5,4},{6,5},{7,6},{8,7},{9,8},{10,9},{11,1... | collective-permute-start | bytes 110600 | tf_op jit(solution)/shard_map/ppermute | solution.py:477
  27.9 4.5 %collective-permute-start = (f32[9,8,128]{2,1,0:T(8,128)S(1)}, f32[9,8,128]{2,1,0:T(8,128)S(1)}, u32[]{:S(2)}, u32[]{:S(2)}) collective-permute-start(f32[9,8,128]{2,1,0:T(8,128)S(1)} %get-tuple-element.13.own_ref), channel_id=1, source_target_pairs={{0,1},{1,2},{2,3},{3,4},{4,5},{5,6},{6,7},{7,8},{8,9},{9,10},{10,1... | collective-permute-start | bytes 110600 | tf_op jit(solution)/shard_map/ppermute | solution.py:476
  33.4 12.2 %collective-permute-start.4 = (f32[51,8,128]{2,1,0:T(8,128)S(1)}, f32[51,8,128]{2,1,0:T(8,128)S(1)}, u32[]{:S(2)}, u32[]{:S(2)}) collective-permute-start(f32[51,8,128]{2,1,0:T(8,128)S(1)} %get-tuple-element.21), channel_id=1, source_target_pairs={{0,16},{16,32},{32,48},{48,64},{64,80},{80,96},{96,112},{112,128},... | collective-permute-start | bytes 626696 | tf_op jit(solution)/shard_map/ppermute | solution.py:482
  36.6 11.2 %collective-permute-start.3 = (f32[23,8,128]{2,1,0:T(8,128)S(1)}, f32[23,8,128]{2,1,0:T(8,128)S(1)}, u32[]{:S(2)}, u32[]{:S(2)}) collective-permute-start(f32[23,8,128]{2,1,0:T(8,128)S(1)} %get-tuple-element.18), channel_id=1, source_target_pairs={{16,0},{32,16},{48,32},{64,48},{80,64},{96,80},{112,96},{128,112},... | collective-permute-start | bytes 282632 | tf_op jit(solution)/shard_map/ppermute | solution.py:483

commit v7 on v6

--- a/solution.py
+++ b/solution.py
@@ -11,7 +11,7 @@
 OMEGA = 0.8
 NU1, NU2, NUC = 2, 2, 4
 HY, HX = 14, 16
-RY = 12
+FY, RY = 13, 12
 ROWS = CY + 2 * HY
 LANES = 2 * CX
 F32 = jnp.float32
@@ -34,7 +34,9 @@
     return jnp.where((lane < HX) | (lane >= CX - HX), turned, 0.0)
 
 
-def outgoing_kernel(count_hbm, partials_hbm, out_hbm, count_ref, partials_ref, out_ref, count_sem, in_sems, out_sems):
+def outgoing_kernel(count_hbm, partials_hbm, class_cond_hbm, head_hbm, class_hbm, ids_hbm,
+                    out_hbm, table_ref, head_ref, class_ref, ids_ref,
+                    count_ref, class_cond_ref, partials_ref, out_ref, count_sem, in_sems, out_sems, field_sems):
     ncols = partials_ref.shape[0]
     part = ncols // 4
     counts = pltpu.make_async_copy(count_hbm, count_ref, count_sem)
@@ -44,6 +46,12 @@
         piece = pl.ds(c * part, part)
         arriving.append(pltpu.make_async_copy(partials_hbm.at[piece], partials_ref.at[piece], in_sems.at[c]))
         arriving[c].start()
+    pairs = (
+        (class_cond_hbm, class_cond_ref), (head_hbm, head_ref), (class_hbm, class_ref), (ids_hbm, ids_ref)
+    )
+    fields = [pltpu.make_async_copy(a, b, field_sems.at[i]) for i, (a, b) in enumerate(pairs)]
+    for copy in fields:
+        copy.start()
     counts.wait()
     lane = lane_of((8, CX))
     slot = lax.broadcasted_iota(jnp.int32, (8, CX), 0)
@@ -68,22 +76,17 @@
             leaving.append(pltpu.make_async_copy(out_ref.at[piece], out_hbm.at[piece], out_sems.at[d // part]))
             leaving[-1].start()
             sent = ready
+    for copy in fields:
+        copy.wait()
+    for c in range(NCLASS):
+        table_ref[c] = jnp.full((8, CX), class_cond_ref[c], F32)
     for copy in leaving:
         copy.wait()
 
 
-def fields_kernel(class_cond_hbm, head_hbm, class_hbm, ids_hbm, head_out, cond_out, right_out, left_out, edge_out,
-                  class_cond_ref, head_ref, class_ref, ids_ref, sems):
-    pairs = (
-        (head_hbm, head_ref), (class_hbm, class_ref), (class_cond_hbm, class_cond_ref), (ids_hbm, ids_ref)
-    )
-    copies = [pltpu.make_async_copy(a, b, sems.at[i]) for i, (a, b) in enumerate(pairs)]
-    for copy in copies:
-        copy.start()
-    for copy in copies:
-        copy.wait()
+def fields_kernel(table_ref, head_ref, class_ref, ids_ref, head_out, cond_out, right_out, left_out, edge_out):
     lane = lane_of((8, CX))
-    values = [class_cond_ref[c] for c in range(8)]
+    values = [table_ref[c] for c in range(NCLASS)]
     blocks = []
     for block in range(CY // 4):
         heads, conds = [], []
@@ -91,14 +94,14 @@
             y = 4 * block + q
             head = head_ref[pl.ds(y, NZ, stride=CY), :]
             kind = class_ref[pl.ds(y, NZ, stride=CY), :]
-            cond = jnp.full((8, CX), values[0], F32)
-            for c in range(1, 8):
+            cond = values[0]
+            for c in range(1, NCLASS):
                 cond = jnp.where(kind == c, values[c], cond)
             head_out[y] = head
             cond_out[y] = cond
-            if y < HY:
+            if y < FY:
                 edge_out[y] = head
-                edge_out[HY + y] = cond
+                edge_out[FY + y] = cond
             heads.append(head)
             conds.append(cond)
         blocks.append((packed(heads, lane), packed(conds, lane)))
@@ -167,11 +170,11 @@
     halo = jnp.where(wide >= CX - HX, from_left, jnp.where(wide < HX, from_right, 0.0))
     main_out[...] = main
     halo_out[...] = halo
-    for out, first, strip0, base in ((up_out, 0, 0, 0), (down_out, CY - HY, CY // 4 - 4, 2 * HY)):
+    for out, first, strip0, base in ((up_out, 0, 0, 0), (down_out, CY - HY, CY // 4 - 4, 2 * FY)):
         skip = first and HY - RY
         if base:
-            out[0:HY] = head_ref[first : first + HY]
-            out[HY : 2 * HY] = cond_ref[first : first + HY]
+            out[0:FY] = head_ref[CY - FY : CY]
+            out[FY : 2 * FY] = cond_ref[CY - FY : CY]
         out[base : base + RY] = main[first + skip : first + skip + RY]
         base = base + RY
         for i in range(4):
@@ -182,7 +185,7 @@
             out[base + 8 + i] = packed([halo[y + q] for q in range(4)], lane)
 
 
-EDGE, UP = 2 * HY, RY + 8 + RY // 4
+EDGE, UP = 2 * FY, RY + 8 + RY // 4
 DOWN = EDGE + UP
 
 
@@ -372,12 +375,12 @@
     lane = lane_of((8, CX))
     base, source = (EDGE + RY, EDGE) if side == 0 else (RY, 0)
     first, shift, skip = ((0, 2, HY - RY), (HY + CY, 0, 0))[side]
-    for i in range(HY):
+    for row in range(FY):
+        i = row + HY - FY if side == 0 else row
         at, q = (i + shift) // 4, (i + shift) % 4
-        if first + i in NEEDED["u0"][0]:
-            cycle.put_parts("u0", first + i, edge_ref[i], unpacked(sent_ref[base + at], q, lane))
-            half = 0.5 * edge_ref[HY + i]
-            cycle.put_parts("half", first + i, half, 0.5 * unpacked(sent_ref[base + 4 + at], q, lane))
+        cycle.put_parts("u0", first + i, edge_ref[row], unpacked(sent_ref[base + at], q, lane))
+        half = 0.5 * edge_ref[FY + row]
+        cycle.put_parts("half", first + i, half, 0.5 * unpacked(sent_ref[base + 4 + at], q, lane))
     for i in range(RY):
         edge = unpacked(sent_ref[base + 8 + i // 4], i % 4, lane)
         cycle.put_parts("source", first + skip + i, sent_ref[source + i], edge)
@@ -412,9 +415,9 @@
 def call(kernel, ins, outs, scratch=(), out=VMEM, flops=1 << 20, nbytes=1 << 20):
     return pl.pallas_call(
         kernel,
-        out_shape=tuple(jax.ShapeDtypeStruct(s, F32) for s in outs),
+        out_shape=tuple(jax.ShapeDtypeStruct(*s) if isinstance(s[0], tuple) else jax.ShapeDtypeStruct(s, F32) for s in outs),
         in_specs=ins,
-        out_specs=tuple(out for _ in outs),
+        out_specs=out if isinstance(out, tuple) else (out,) * len(outs),
         scratch_shapes=scratch,
         cost_estimate=pl.CostEstimate(flops=flops, bytes_accessed=nbytes, transcendentals=0),
         compiler_params=pltpu.CompilerParams(vmem_limit_bytes=32 << 20),
@@ -448,31 +451,27 @@
 def body(head_start, class_map, class_cond, partials, send_count, recv_block):
     ngroups, ncols = lax.axis_size("rows"), lax.axis_size("cols")
     row = (CY, NZ, CX)
+    flat = (NZ * CY, CX)
     scratch = [
         pltpu.SMEM((ncols,), jnp.int32),
+        pltpu.SMEM((NCLASS,), F32),
         pltpu.VMEM((ncols, SLOTS, CX), F32),
         pltpu.VMEM((ncols, SLOTS + 8, CX), F32),
         pltpu.SemaphoreType.DMA,
         pltpu.SemaphoreType.DMA((4,)),
         pltpu.SemaphoreType.DMA((4,)),
-    ]
-    payload = call(outgoing_kernel, [HBM, HBM], [(ncols, SLOTS + 8, CX)], scratch, HBM)(
-        in_hbm(send_count.reshape(ncols)), in_hbm(partials.reshape(ncols, SLOTS, CX))
-    )[0]
-    incoming = lax.all_to_all(payload, "cols", split_axis=0, concat_axis=0, tiled=True)
-    flat = (NZ * CY, CX)
-    scratch = [
-        pltpu.SMEM((NCLASS,), F32),
-        pltpu.VMEM(flat, F32),
-        pltpu.VMEM(flat, jnp.int32),
-        pltpu.VMEM((ncols, SLOTS), jnp.int32),
         pltpu.SemaphoreType.DMA((4,)),
     ]
-    fields = (class_cond, head_start.reshape(flat), class_map.reshape(flat), recv_block.reshape(ncols, SLOTS))
+    ids = (ncols, SLOTS)
+    given = (
+        send_count.reshape(ncols), partials.reshape(ncols, SLOTS, CX),
+        class_cond, head_start.reshape(flat), class_map.reshape(flat), recv_block.reshape(ids),
+    )
+    sizes = [(ncols, SLOTS + 8, CX), (NCLASS, 8, CX), flat, (flat, jnp.int32), (ids, jnp.int32)]
+    payload, *fields = call(outgoing_kernel, [HBM] * 6, sizes, scratch, (HBM,) + (VMEM,) * 4)(*map(in_hbm, given))
+    incoming = lax.all_to_all(payload, "cols", split_axis=0, concat_axis=0, tiled=True)
     sizes = [row, row] + [(STRIP, 8, CX)] * 2 + [(EDGE, 8, CX)]
-    head, cond, to_right, to_left, edge = call(fields_kernel, [HBM] * 4, sizes, scratch)(
-        *(in_hbm(x) for x in fields)
-    )
+    head, cond, to_right, to_left, edge = call(fields_kernel, [VMEM] * 4, sizes)(*fields)
     left = lax.ppermute(to_right, "cols", forward(ncols))
     right = lax.ppermute(to_left, "cols", backward(ncols))
     edge = lax.ppermute(edge, "rows", backward(ngroups))

time: 50.9 us -> 50.8 us (level)
  the two profiles are of different devices: /device:TPU:65 before, /device:TPU:63 now
where the time goes in v7:
time: 50.8 us; the launch traced here: 50.4 us
  starting transfers between devices  32.4 us (64%)
  Pallas kernels  10.2 us (20%)
  waiting for transfers between devices  6.95 us (14%)
  between operations  0.71 us (1%)
    all_to_all x1, starting transfers between devices, body(): lax.all_to_all(payload, 'cols', split_axis=0, concat_axis=0, tiled=True)  17.4 us
    ppermute x1, starting transfers between devices, body(): top = lax.ppermute(down, 'rows', forward(ngroups))  4.33 us
    ppermute x1, starting transfers between devices, body(): left = lax.ppermute(to_right, 'cols', forward(ncols))  3.45 us
    ppermute x1, starting transfers between devices, body(): edge = lax.ppermute(edge, 'rows', backward(ngroups))  3.08 us
    ppermute x1, waiting for transfers between devices, body(): bottom = lax.ppermute(up, 'rows', backward(ngroups))  2.9 us
    all_to_all x1, waiting for transfers between devices, body(): lax.all_to_all(payload, 'cols', split_axis=0, concat_axis=0, tiled=True)  2.81 us
    pallas_call x1, Pallas kernels, late_call(): call(kernel, ins, [(NZ, CY, CX)] * 2, scratch, HBM)  2.8 us
    pallas_call x1, Pallas kernels, early_call(): call(early_kernel, [SMEM] + [VMEM] * 6, [(len(EARLY), NZ, LANES)])  2.56 us
  transfers between devices with their start and end apart: 6, of which 4 were waited for; matrix products, arithmetic and copies ran while one was open for 0% of the time, Pallas kernels for 10%

profile of v7, /device:TPU:63, one launch (start us, length us, event | category | flops | bytes accessed | tf_op | source)
XLA Modules:
  0.0 50.4 jit_solution(17402447795749724167)
XLA Ops:
  0.6 2.0 %shard_map.77 = (f32[16,40,128]{2,1,0:T(8,128)}, f32[8,8,128]{2,1,0:T(8,128)S(1)}, f32[256,128]{1,0:T(8,128)S(1)}, s32[256,128]{1,0:T(8,128)S(1)}, s32[16,32]{1,0:T(8,128)S(1)}) custom-call(s32[16]{0:T(128)} %bitcast.11, f32[16,32,128]{2,1,0:T(8,128)} %bitcast.7, f32[8]{0:T(128)} %class_cond_hbm.1, f32[256,128]{1,0:T(8,128)} %bitcast.8, s32[256,128]{1,0:T(8,128)} %bitcast.9, ...), custom_call_target="tpu_custom_call" | custom-call | flops 1048576 | bytes 1048576 | tf_op jit(solution)/shard_map/pallas_call | solution.py:471
  2.6 17.4 %all-to-all-start = ((f32[16,40,128]{2,1,0:T(8,128)}), f32[16,40,128]{2,1,0:T(8,128)S(1)}, u32[]{:S(2)}, u32[]{:S(2)}) async-start(f32[16,40,128]{2,1,0:T(8,128)} %get-tuple-element.18), calls=%async_computation | async-start | bytes 655360 | tf_op jit(solution)/shard_map/all_to_all | solution.py:472
  20.0 0.3 shard_map.78
  20.3 3.1 %collective-permute-start.2 = (f32[26,8,128]{2,1,0:T(8,128)S(1)}, f32[26,8,128]{2,1,0:T(8,128)S(1)}, u32[]{:S(2)}, u32[]{:S(2)}) collective-permute-start(f32[26,8,128]{2,1,0:T(8,128)S(1)} %get-tuple-element.27), channel_id=1, source_target_pairs={{16,0},{32,16},{48,32},{64,48},{80,64},{96,80},{112,96},{128,112},... | collective-permute-start | bytes 319496 | tf_op jit(solution)/shard_map/ppermute | solution.py:477
  23.4 2.3 %collective-permute-start.1 = (f32[9,8,128]{2,1,0:T(8,128)S(1)}, f32[9,8,128]{2,1,0:T(8,128)S(1)}, u32[]{:S(2)}, u32[]{:S(2)}) collective-permute-start(f32[9,8,128]{2,1,0:T(8,128)S(1)} %get-tuple-element.24), channel_id=1, source_target_pairs={{1,0},{2,1},{3,2},{4,3},{5,4},{6,5},{7,6},{8,7},{9,8},{10,9},{11,1... | collective-permute-start | bytes 110600 | tf_op jit(solution)/shard_map/ppermute | solution.py:476
  25.7 3.4 %collective-permute-start = (f32[9,8,128]{2,1,0:T(8,128)S(1)}, f32[9,8,128]{2,1,0:T(8,128)S(1)}, u32[]{:S(2)}, u32[]{:S(2)}) collective-permute-start(f32[9,8,128]{2,1,0:T(8,128)S(1)} %get-tuple-element.23.own_ref), channel_id=1, source_target_pairs={{0,1},{1,2},{2,3},{3,4},{4,5},{5,6},{6,7},{7,8},{8,9},{9,10},{10,1... | collective-permute-start | bytes 110600 | tf_op jit(solution)/shard_map/ppermute | solution.py:475
  29.1 1.1 %collective-permute-done.1.right_ref = f32[9,8,128]{2,1,0:T(8,128)S(1)} collective-permute-done((f32[9,8,128]{2,1,0:T(8,128)S(1)}, f32[9,8,128]{2,1,0:T(8,128)S(1)}, u32[]{:S(2)}, u32[]{:S(2)}) %collective-permute-start.1) | collective-permute-done | bytes 36896 | tf_op jit(solution)/shard_map/ppermute | solution.py:476
  30.2 0.0 collective-permute-done.left_ref
  30.2 0.0 collective-permute-done.2._.refs_0_
  30.2 2.8 %all-to-all-done.incoming_ref = f32[16,40,128]{2,1,0:T(8,128)S(1)} async-done(((f32[16,40,128]{2,1,0:T(8,128)}), f32[16,40,128]{2,1,0:T(8,128)S(1)}, u32[]{:S(2)}, u32[]{:S(2)}) %all-to-all-start) | async-done | bytes 327712 | tf_op jit(solution)/shard_map/all_to_all | solution.py:472
  33.0 0.4 shard_map.79
  33.5 4.3 %collective-permute-start.4 = (f32[49,8,128]{2,1,0:T(8,128)S(1)}, f32[49,8,128]{2,1,0:T(8,128)S(1)}, u32[]{:S(2)}, u32[]{:S(2)}) collective-permute-start(f32[49,8,128]{2,1,0:T(8,128)S(1)} %get-tuple-element.31), channel_id=1, source_target_pairs={{0,16},{16,32},{32,48},{48,64},{64,80},{80,96},{96,112},{112,128},... | collective-permute-start | bytes 602120 | tf_op jit(solution)/shard_map/ppermute | solution.py:481
  37.8 1.9 %collective-permute-start.3 = (f32[23,8,128]{2,1,0:T(8,128)S(1)}, f32[23,8,128]{2,1,0:T(8,128)S(1)}, u32[]{:S(2)}, u32[]{:S(2)}) collective-permute-start(f32[23,8,128]{2,1,0:T(8,128)S(1)} %get-tuple-element.28), channel_id=1, source_target_pairs={{16,0},{32,16},{48,32},{64,48},{80,64},{96,80},{112,96},{128,112},... | collective-permute-start | bytes 282632 | tf_op jit(solution)/shard_map/ppermute | solution.py:482
  39.8 0.1 pad_add_fusion.place_ref
  39.8 2.6 %shard_map.80.early = f32[440,8,256]{2,1,0:T(8,128)S(1)} custom-call(s32[4]{0:T(128)S(1)} %pad_add_fusion.place_ref, f32[32,8,128]{2,1,0:T(8,128)S(1)} %get-tuple-element.25.head_ref, f32[32,8,128]{2,1,0:T(8,128)S(1)} %get-tuple-element.26.cond_ref, f32[32,8,128]{2,1,0:T(8,128)S(1)} %get-tuple-element.29.main_ref, ...), custom_call_target="tpu_custom_call" | custom-call | flops 1048576 | bytes 1048576 | tf_op jit(solution)/shard_map/pallas_call | solution.py:436
  42.4 0.1 collective-permute-done.4.sent_ref
  42.6 2.1 %shard_map.81 = (f32[8,16,128]{2,1,0:T(8,128)S(1)}, f32[8,16,128]{2,1,0:T(8,128)S(1)}) custom-call(s32[4]{0:T(128)S(1)} %pad_add_fusion.place_ref, f32[49,8,128]{2,1,0:T(8,128)S(1)} %collective-permute-done.4.sent_ref, f32[440,8,256]{2,1,0:T(8,128)S(1)} %shard_map.80.early), custom_call_target="tpu_custom_call" | custom-call | flops 1048576 | bytes 1048576 | tf_op jit(solution)/shard_map/pallas_call | solution.py:446
  44.7 2.9 %collective-permute-done.3.sent_ref = f32[23,8,128]{2,1,0:T(8,128)S(1)} collective-permute-done((f32[23,8,128]{2,1,0:T(8,128)S(1)}, f32[23,8,128]{2,1,0:T(8,128)S(1)}, u32[]{:S(2)}, u32[]{:S(2)}) %collective-permute-start.3) | collective-permute-done | bytes 94240 | tf_op jit(solution)/shard_map/ppermute | solution.py:482
  47.6 2.8 %shard_map.82 = (f32[8,32,128]{2,1,0:T(8,128)}, f32[8,32,128]{2,1,0:T(8,128)}) custom-call(s32[4]{0:T(128)S(1)} %pad_add_fusion.place_ref, f32[23,8,128]{2,1,0:T(8,128)S(1)} %collective-permute-done.3.sent_ref, f32[440,8,256]{2,1,0:T(8,128)S(1)} %shard_map.80.early, f32[26,8,128]{2,1,0:T(8,128)S(1)} %collective-permute-done.2._.refs_0_, ...), custom_call_target="tpu_custom_call" | custom-call | flops 1048576 | bytes 1048576 | tf_op jit(solution)/shard_map/pallas_call | solution.py:448
Async XLA Ops:
  2.6 30.4 %all-to-all-start = ((f32[16,40,128]{2,1,0:T(8,128)}), f32[16,40,128]{2,1,0:T(8,128)S(1)}, u32[]{:S(2)}, u32[]{:S(2)}) async-start(f32[16,40,128]{2,1,0:T(8,128)} %get-tuple-element.18), calls=%async_computation | async-start | bytes 655360 | tf_op jit(solution)/shard_map/all_to_all | solution.py:472
  20.3 9.9 %collective-permute-start.2 = (f32[26,8,128]{2,1,0:T(8,128)S(1)}, f32[26,8,128]{2,1,0:T(8,128)S(1)}, u32[]{:S(2)}, u32[]{:S(2)}) collective-permute-start(f32[26,8,128]{2,1,0:T(8,128)S(1)} %get-tuple-element.27), channel_id=1, source_target_pairs={{16,0},{32,16},{48,32},{64,48},{80,64},{96,80},{112,96},{128,112},... | collective-permute-start | bytes 319496 | tf_op jit(solution)/shard_map/ppermute | solution.py:477
  23.4 6.8 %collective-permute-start.1 = (f32[9,8,128]{2,1,0:T(8,128)S(1)}, f32[9,8,128]{2,1,0:T(8,128)S(1)}, u32[]{:S(2)}, u32[]{:S(2)}) collective-permute-start(f32[9,8,128]{2,1,0:T(8,128)S(1)} %get-tuple-element.24), channel_id=1, source_target_pairs={{1,0},{2,1},{3,2},{4,3},{5,4},{6,5},{7,6},{8,7},{9,8},{10,9},{11,1... | collective-permute-start | bytes 110600 | tf_op jit(solution)/shard_map/ppermute | solution.py:476
  25.7 4.6 %collective-permute-start = (f32[9,8,128]{2,1,0:T(8,128)S(1)}, f32[9,8,128]{2,1,0:T(8,128)S(1)}, u32[]{:S(2)}, u32[]{:S(2)}) collective-permute-start(f32[9,8,128]{2,1,0:T(8,128)S(1)} %get-tuple-element.23.own_ref), channel_id=1, source_target_pairs={{0,1},{1,2},{2,3},{3,4},{4,5},{5,6},{6,7},{7,8},{8,9},{9,10},{10,1... | collective-permute-start | bytes 110600 | tf_op jit(solution)/shard_map/ppermute | solution.py:475
  33.5 9.1 %collective-permute-start.4 = (f32[49,8,128]{2,1,0:T(8,128)S(1)}, f32[49,8,128]{2,1,0:T(8,128)S(1)}, u32[]{:S(2)}, u32[]{:S(2)}) collective-permute-start(f32[49,8,128]{2,1,0:T(8,128)S(1)} %get-tuple-element.31), channel_id=1, source_target_pairs={{0,16},{16,32},{32,48},{48,64},{64,80},{80,96},{96,112},{112,128},... | collective-permute-start | bytes 602120 | tf_op jit(solution)/shard_map/ppermute | solution.py:481
  37.8 9.8 %collective-permute-start.3 = (f32[23,8,128]{2,1,0:T(8,128)S(1)}, f32[23,8,128]{2,1,0:T(8,128)S(1)}, u32[]{:S(2)}, u32[]{:S(2)}) collective-permute-start(f32[23,8,128]{2,1,0:T(8,128)S(1)} %get-tuple-element.28), channel_id=1, source_target_pairs={{16,0},{32,16},{48,32},{64,48},{80,64},{96,80},{112,96},{128,112},... | collective-permute-start | bytes 282632 | tf_op jit(solution)/shard_map/ppermute | solution.py:482

commit v8 on v7

--- a/solution.py
+++ b/solution.py
@@ -38,11 +38,12 @@
                     out_hbm, table_ref, head_ref, class_ref, ids_ref,
                     count_ref, class_cond_ref, partials_ref, out_ref, count_sem, in_sems, out_sems, field_sems):
     ncols = partials_ref.shape[0]
-    part = ncols // 4
+    part = max(ncols // 8, 1)
+    pieces = ncols // part
     counts = pltpu.make_async_copy(count_hbm, count_ref, count_sem)
     counts.start()
     arriving = []
-    for c in range(4):
+    for c in range(pieces):
         piece = pl.ds(c * part, part)
         arriving.append(pltpu.make_async_copy(partials_hbm.at[piece], partials_ref.at[piece], in_sems.at[c]))
         arriving[c].start()
@@ -458,8 +459,8 @@
         pltpu.VMEM((ncols, SLOTS, CX), F32),
         pltpu.VMEM((ncols, SLOTS + 8, CX), F32),
         pltpu.SemaphoreType.DMA,
-        pltpu.SemaphoreType.DMA((4,)),
-        pltpu.SemaphoreType.DMA((4,)),
+        pltpu.SemaphoreType.DMA((8,)),
+        pltpu.SemaphoreType.DMA((8,)),
         pltpu.SemaphoreType.DMA((4,)),
     ]
     ids = (ncols, SLOTS)

time: 50.8 us -> 51.1 us (level)
  the two profiles are of different devices: /device:TPU:63 before, /device:TPU:65 now
where the time goes in v8:
time: 51.1 us; the launch traced here: 50.8 us
  starting transfers between devices  36 us (70%)
  Pallas kernels  10.5 us (21%)
  waiting for transfers between devices  3.42 us (7%)
  between operations  0.73 us (1%)
    all_to_all x1, starting transfers between devices, body(): lax.all_to_all(payload, 'cols', split_axis=0, concat_axis=0, tiled=True)  17.4 us
    ppermute x1, starting transfers between devices, body(): bottom = lax.ppermute(up, 'rows', backward(ngroups))  5.48 us
    ppermute x1, starting transfers between devices, body(): edge = lax.ppermute(edge, 'rows', backward(ngroups))  4.3 us
    ppermute x1, starting transfers between devices, body(): left = lax.ppermute(to_right, 'cols', forward(ncols))  3.45 us
    ppermute x1, starting transfers between devices, body(): top = lax.ppermute(down, 'rows', forward(ngroups))  3.12 us
    pallas_call x1, Pallas kernels, late_call(): call(kernel, ins, [(NZ, CY, CX)] * 2, scratch, HBM)  2.8 us
    pallas_call x1, Pallas kernels, early_call(): call(early_kernel, [SMEM] + [VMEM] * 6, [(len(EARLY), NZ, LANES)])  2.56 us
    pallas_call x1, Pallas kernels, body(): call(outgoing_kernel, [HBM] * 6, sizes, scratch, (HBM,) + (VMEM,) * 4)  2.27 us
  transfers between devices with their start and end apart: 6, of which 3 were waited for; matrix products, arithmetic and copies ran while one was open for 0% of the time, Pallas kernels for 10%

profile of v8, /device:TPU:65, one launch (start us, length us, event | category | flops | bytes accessed | tf_op | source)
XLA Modules:
  0.0 50.8 jit_solution(999446935906166553)
XLA Ops:
  0.6 2.3 %shard_map.77 = (f32[16,40,128]{2,1,0:T(8,128)}, f32[8,8,128]{2,1,0:T(8,128)S(1)}, f32[256,128]{1,0:T(8,128)S(1)}, s32[256,128]{1,0:T(8,128)S(1)}, s32[16,32]{1,0:T(8,128)S(1)}) custom-call(s32[16]{0:T(128)} %bitcast.11, f32[16,32,128]{2,1,0:T(8,128)} %bitcast.7, f32[8]{0:T(128)} %class_cond_hbm.1, f32[256,128]{1,0:T(8,128)} %bitcast.8, s32[256,128]{1,0:T(8,128)} %bitcast.9, ...), custom_call_target="tpu_custom_call" | custom-call | flops 1048576 | bytes 1048576 | tf_op jit(solution)/shard_map/pallas_call | solution.py:472
  2.9 17.4 %all-to-all-start = ((f32[16,40,128]{2,1,0:T(8,128)}), f32[16,40,128]{2,1,0:T(8,128)S(1)}, u32[]{:S(2)}, u32[]{:S(2)}) async-start(f32[16,40,128]{2,1,0:T(8,128)} %get-tuple-element.18), calls=%async_computation | async-start | bytes 655360 | tf_op jit(solution)/shard_map/all_to_all | solution.py:473
  20.3 0.3 shard_map.78
  20.6 4.3 %collective-permute-start.2 = (f32[26,8,128]{2,1,0:T(8,128)S(1)}, f32[26,8,128]{2,1,0:T(8,128)S(1)}, u32[]{:S(2)}, u32[]{:S(2)}) collective-permute-start(f32[26,8,128]{2,1,0:T(8,128)S(1)} %get-tuple-element.27), channel_id=1, source_target_pairs={{16,0},{32,16},{48,32},{64,48},{80,64},{96,80},{112,96},{128,112},... | collective-permute-start | bytes 319496 | tf_op jit(solution)/shard_map/ppermute | solution.py:478
  24.9 2.3 %collective-permute-start.1 = (f32[9,8,128]{2,1,0:T(8,128)S(1)}, f32[9,8,128]{2,1,0:T(8,128)S(1)}, u32[]{:S(2)}, u32[]{:S(2)}) collective-permute-start(f32[9,8,128]{2,1,0:T(8,128)S(1)} %get-tuple-element.24), channel_id=1, source_target_pairs={{1,0},{2,1},{3,2},{4,3},{5,4},{6,5},{7,6},{8,7},{9,8},{10,9},{11,1... | collective-permute-start | bytes 110600 | tf_op jit(solution)/shard_map/ppermute | solution.py:477
  27.2 3.4 %collective-permute-start = (f32[9,8,128]{2,1,0:T(8,128)S(1)}, f32[9,8,128]{2,1,0:T(8,128)S(1)}, u32[]{:S(2)}, u32[]{:S(2)}) collective-permute-start(f32[9,8,128]{2,1,0:T(8,128)S(1)} %get-tuple-element.23.own_ref), channel_id=1, source_target_pairs={{0,1},{1,2},{2,3},{3,4},{4,5},{5,6},{6,7},{7,8},{8,9},{9,10},{10,1... | collective-permute-start | bytes 110600 | tf_op jit(solution)/shard_map/ppermute | solution.py:476
  30.7 0.0 collective-permute-done.1.right_ref
  30.7 1.0 %collective-permute-done.left_ref = f32[9,8,128]{2,1,0:T(8,128)S(1)} collective-permute-done((f32[9,8,128]{2,1,0:T(8,128)S(1)}, f32[9,8,128]{2,1,0:T(8,128)S(1)}, u32[]{:S(2)}, u32[]{:S(2)}) %collective-permute-start) | collective-permute-done | bytes 36896 | tf_op jit(solution)/shard_map/ppermute | solution.py:476
  31.7 0.0 collective-permute-done.2._.refs_0_
  31.7 1.7 %all-to-all-done.incoming_ref = f32[16,40,128]{2,1,0:T(8,128)S(1)} async-done(((f32[16,40,128]{2,1,0:T(8,128)}), f32[16,40,128]{2,1,0:T(8,128)S(1)}, u32[]{:S(2)}, u32[]{:S(2)}) %all-to-all-start) | async-done | bytes 327712 | tf_op jit(solution)/shard_map/all_to_all | solution.py:473
  33.4 0.4 shard_map.79
  33.8 3.1 %collective-permute-start.4 = (f32[49,8,128]{2,1,0:T(8,128)S(1)}, f32[49,8,128]{2,1,0:T(8,128)S(1)}, u32[]{:S(2)}, u32[]{:S(2)}) collective-permute-start(f32[49,8,128]{2,1,0:T(8,128)S(1)} %get-tuple-element.31), channel_id=1, source_target_pairs={{0,16},{16,32},{32,48},{48,64},{64,80},{80,96},{96,112},{112,128},... | collective-permute-start | bytes 602120 | tf_op jit(solution)/shard_map/ppermute | solution.py:482
  36.9 5.5 %collective-permute-start.3 = (f32[23,8,128]{2,1,0:T(8,128)S(1)}, f32[23,8,128]{2,1,0:T(8,128)S(1)}, u32[]{:S(2)}, u32[]{:S(2)}) collective-permute-start(f32[23,8,128]{2,1,0:T(8,128)S(1)} %get-tuple-element.28), channel_id=1, source_target_pairs={{16,0},{32,16},{48,32},{64,48},{80,64},{96,80},{112,96},{128,112},... | collective-permute-start | bytes 282632 | tf_op jit(solution)/shard_map/ppermute | solution.py:483
  42.4 0.1 pad_add_fusion.place_ref
  42.5 2.6 %shard_map.80.early = f32[440,8,256]{2,1,0:T(8,128)S(1)} custom-call(s32[4]{0:T(128)S(1)} %pad_add_fusion.place_ref, f32[32,8,128]{2,1,0:T(8,128)S(1)} %get-tuple-element.25.head_ref, f32[32,8,128]{2,1,0:T(8,128)S(1)} %get-tuple-element.26.cond_ref, f32[32,8,128]{2,1,0:T(8,128)S(1)} %get-tuple-element.29.main_ref, ...), custom_call_target="tpu_custom_call" | custom-call | flops 1048576 | bytes 1048576 | tf_op jit(solution)/shard_map/pallas_call | solution.py:437
  45.1 0.7 %collective-permute-done.4.sent_ref = f32[49,8,128]{2,1,0:T(8,128)S(1)} collective-permute-done((f32[49,8,128]{2,1,0:T(8,128)S(1)}, f32[49,8,128]{2,1,0:T(8,128)S(1)}, u32[]{:S(2)}, u32[]{:S(2)}) %collective-permute-start.4) | collective-permute-done | bytes 200736 | tf_op jit(solution)/shard_map/ppermute | solution.py:482
  45.8 2.1 %shard_map.81 = (f32[8,16,128]{2,1,0:T(8,128)S(1)}, f32[8,16,128]{2,1,0:T(8,128)S(1)}) custom-call(s32[4]{0:T(128)S(1)} %pad_add_fusion.place_ref, f32[49,8,128]{2,1,0:T(8,128)S(1)} %collective-permute-done.4.sent_ref, f32[440,8,256]{2,1,0:T(8,128)S(1)} %shard_map.80.early), custom_call_target="tpu_custom_call" | custom-call | flops 1048576 | bytes 1048576 | tf_op jit(solution)/shard_map/pallas_call | solution.py:447
  48.0 0.0 collective-permute-done.3.sent_ref
  48.0 2.8 %shard_map.82 = (f32[8,32,128]{2,1,0:T(8,128)}, f32[8,32,128]{2,1,0:T(8,128)}) custom-call(s32[4]{0:T(128)S(1)} %pad_add_fusion.place_ref, f32[23,8,128]{2,1,0:T(8,128)S(1)} %collective-permute-done.3.sent_ref, f32[440,8,256]{2,1,0:T(8,128)S(1)} %shard_map.80.early, f32[26,8,128]{2,1,0:T(8,128)S(1)} %collective-permute-done.2._.refs_0_, ...), custom_call_target="tpu_custom_call" | custom-call | flops 1048576 | bytes 1048576 | tf_op jit(solution)/shard_map/pallas_call | solution.py:449
Async XLA Ops:
  2.9 30.4 %all-to-all-start = ((f32[16,40,128]{2,1,0:T(8,128)}), f32[16,40,128]{2,1,0:T(8,128)S(1)}, u32[]{:S(2)}, u32[]{:S(2)}) async-start(f32[16,40,128]{2,1,0:T(8,128)} %get-tuple-element.18), calls=%async_computation | async-start | bytes 655360 | tf_op jit(solution)/shard_map/all_to_all | solution.py:473
  20.6 11.1 %collective-permute-start.2 = (f32[26,8,128]{2,1,0:T(8,128)S(1)}, f32[26,8,128]{2,1,0:T(8,128)S(1)}, u32[]{:S(2)}, u32[]{:S(2)}) collective-permute-start(f32[26,8,128]{2,1,0:T(8,128)S(1)} %get-tuple-element.27), channel_id=1, source_target_pairs={{16,0},{32,16},{48,32},{64,48},{80,64},{96,80},{112,96},{128,112},... | collective-permute-start | bytes 319496 | tf_op jit(solution)/shard_map/ppermute | solution.py:478
  24.9 5.7 %collective-permute-start.1 = (f32[9,8,128]{2,1,0:T(8,128)S(1)}, f32[9,8,128]{2,1,0:T(8,128)S(1)}, u32[]{:S(2)}, u32[]{:S(2)}) collective-permute-start(f32[9,8,128]{2,1,0:T(8,128)S(1)} %get-tuple-element.24), channel_id=1, source_target_pairs={{1,0},{2,1},{3,2},{4,3},{5,4},{6,5},{7,6},{8,7},{9,8},{10,9},{11,1... | collective-permute-start | bytes 110600 | tf_op jit(solution)/shard_map/ppermute | solution.py:477
  27.2 4.5 %collective-permute-start = (f32[9,8,128]{2,1,0:T(8,128)S(1)}, f32[9,8,128]{2,1,0:T(8,128)S(1)}, u32[]{:S(2)}, u32[]{:S(2)}) collective-permute-start(f32[9,8,128]{2,1,0:T(8,128)S(1)} %get-tuple-element.23.own_ref), channel_id=1, source_target_pairs={{0,1},{1,2},{2,3},{3,4},{4,5},{5,6},{6,7},{7,8},{8,9},{9,10},{10,1... | collective-permute-start | bytes 110600 | tf_op jit(solution)/shard_map/ppermute | solution.py:476
  33.8 12.0 %collective-permute-start.4 = (f32[49,8,128]{2,1,0:T(8,128)S(1)}, f32[49,8,128]{2,1,0:T(8,128)S(1)}, u32[]{:S(2)}, u32[]{:S(2)}) collective-permute-start(f32[49,8,128]{2,1,0:T(8,128)S(1)} %get-tuple-element.31), channel_id=1, source_target_pairs={{0,16},{16,32},{32,48},{48,64},{64,80},{80,96},{96,112},{112,128},... | collective-permute-start | bytes 602120 | tf_op jit(solution)/shard_map/ppermute | solution.py:482
  36.9 11.0 %collective-permute-start.3 = (f32[23,8,128]{2,1,0:T(8,128)S(1)}, f32[23,8,128]{2,1,0:T(8,128)S(1)}, u32[]{:S(2)}, u32[]{:S(2)}) collective-permute-start(f32[23,8,128]{2,1,0:T(8,128)S(1)} %get-tuple-element.28), channel_id=1, source_target_pairs={{16,0},{32,16},{48,32},{64,48},{80,64},{96,80},{112,96},{128,112},... | collective-permute-start | bytes 282632 | tf_op jit(solution)/shard_map/ppermute | solution.py:483
